TPU v7x, 32 devices: a whole 2x2x4 slice. The times are simulated.
32 devices in a mesh: req: 16 (over z, y, x), head: 2 (over core).
Axes of the slice: x: 2, y: 2, z: 4, core: 2. Of those that a mesh axis runs over, the one named last changes fastest.
Arguments:
- hidden_in: bfloat16 [1024, 2048], P('req'), may hold values from -14 to 14
- attn_gain: float32 [2048], replicated, may hold values from 0.1 to 1.9
- w_query: bfloat16 [2048, 2048], P(None, 'head'), may hold values from -0.125 to 0.125
- w_key: bfloat16 [2048, 1024], P(None, 'head'), may hold values from -0.125 to 0.125
- w_value: bfloat16 [2048, 1024], P(None, 'head'), may hold values from -0.125 to 0.125
- query_gain: float32 [128], replicated, may hold values from 0.5 to 2
- key_gain: float32 [128], replicated, may hold values from 0.5 to 2
- w_out: bfloat16 [2048, 2048], P('head'), may hold values from -0.125 to 0.125
- cache_keys: bfloat16 [16, 2048, 1024], P('req', None, 'head'), may hold values from -3.5 to 3.5
- cache_values: bfloat16 [16, 2048, 1024], P('req', None, 'head'), may hold values from -6 to 6
- cache_lengths: int32 [16], replicated, may hold values from 1 to 2048, 16384 in all
- slot_request: int32 [16], replicated, may hold values from 0 to 15, each once
- mlp_gain: float32 [2048], P('head'), may hold values from 0.1 to 1.9
- w_gate: bfloat16 [2048, 6144], P('head', 'req'), may hold values from -0.125 to 0.125
- w_up: bfloat16 [2048, 6144], P('head', 'req'), may hold values from -0.125 to 0.125
- w_down: bfloat16 [6144, 2048], P('req', 'head'), may hold values from -0.078125 to 0.078125
- final_gain: float32 [2048], replicated, may hold values from 0.1 to 1.9
- w_vocab: bfloat16 [2048, 151936], P(None, ('req', 'head')), may hold values from -8 to 8
Outputs:
- hidden_out: bfloat16 [1024, 2048], P('req', 'head')
- log_probs: float32 [16, 151936], P(None, ('req', 'head'))
Inputs may be any that keep to these rules, and one draw needn't show every extreme that they name: `cache_lengths`: the largest length is exactly 2048. `slot_request`: each request appears once.
All inputs are finite; a program needn't handle non-finite values.
Results may differ from a plain program's by a relative error of at most 0.008.
Values may be sent and summed in bfloat16 or wider, within the bound.
No kernel may reach another device: no remote copies, remote signals or barrier semaphores. Data moves between devices by JAX's collectives and lax.ppermute only.
A program may use at most 128 MiB of HBM per device.

v0:
```python
import jax
import jax.numpy as jnp
from jax import lax
from jax.sharding import PartitionSpec as P

D = 2048
HEAD_DIM = 128


EPS = 1e-06
ROPE_BASE = 1000000.0
NEG = -1e30


def norm_rows(field, gain_vec):
    return field * lax.rsqrt(jnp.mean(field * field, axis=-1, keepdims=True) + EPS) * gain_vec


def rotate(field, positions):
    half_dim = field.shape[-1] // 2
    frequency = ROPE_BASE ** (-2.0 * jnp.arange(half_dim, dtype=jnp.float32) / field.shape[-1])
    angles = positions[..., None, None] * frequency
    cosine = jnp.cos(angles)
    sines = jnp.sin(angles)
    lower_half = field[..., :half_dim]
    upper_half = field[..., half_dim:]
    return jnp.concatenate(
        [lower_half * cosine - upper_half * sines, upper_half * cosine + lower_half * sines],
        axis=-1,
    )


def inverse_order(slot_request):
    indices = jnp.arange(slot_request.shape[0], dtype=jnp.int32)
    return jnp.sum(
        jnp.where(slot_request[None, :] == indices[:, None], indices[None, :], 0), axis=1
    )


def attend_slot(queries, keys_new, values_new, keys_cache, values_cache, cache_len):
    row_count, value_heads, head_size = keys_new.shape
    group_size = queries.shape[1] // value_heads
    grouped = queries.reshape(row_count, value_heads, group_size, head_size)
    score_scale = head_size ** (-0.5)
    recent = (
        jnp.einsum("skgd,tkd->kgst", grouped, keys_new, preferred_element_type=jnp.float32)
        * score_scale
    )
    causal = jnp.arange(row_count)[:, None] >= jnp.arange(row_count)[None, :]
    recent = jnp.where(causal, recent, NEG)
    cache_span = keys_cache.shape[0]
    stored = (
        jnp.einsum("skgd,lkd->kgsl", grouped, keys_cache, preferred_element_type=jnp.float32)
        * score_scale
    )
    stored = jnp.where(jnp.arange(cache_span, dtype=jnp.int32) < cache_len, stored, NEG)
    old_weights = jnp.exp(stored)
    new_weights = jnp.exp(recent)
    row_total = jnp.sum(old_weights, axis=-1) + jnp.sum(new_weights, axis=-1)
    old_weights = (old_weights / row_total[..., None]).astype(jnp.bfloat16)
    new_weights = (new_weights / row_total[..., None]).astype(jnp.bfloat16)
    blended = jnp.einsum(
        "kgsl,lkd->skgd", old_weights, values_cache, preferred_element_type=jnp.float32
    )
    blended = blended + jnp.einsum(
        "kgst,tkd->skgd", new_weights, values_new, preferred_element_type=jnp.float32
    )
    return blended.reshape(row_count, value_heads * group_size * head_size).astype(jnp.bfloat16)


def on_device(
    hidden_in,
    attn_gain,
    w_query,
    w_key,
    w_value,
    query_gain,
    key_gain,
    w_out,
    cache_keys,
    cache_values,
    cache_lengths,
    slot_request,
    mlp_gain,
    w_gate,
    w_up,
    w_down,
    final_gain,
    w_vocab,
):
    row_count = hidden_in.shape[0]
    half_width = mlp_gain.shape[0]
    slot_index = lax.axis_index("req")
    request_id = lax.dynamic_index_in_dim(slot_request, slot_index, 0, keepdims=False)
    cache_len = lax.dynamic_index_in_dim(cache_lengths, request_id, 0, keepdims=False)
    tokens = hidden_in.astype(jnp.float32)
    normed = norm_rows(tokens, attn_gain).astype(jnp.bfloat16)
    query_heads = w_query.shape[1] // HEAD_DIM
    value_heads = w_key.shape[1] // HEAD_DIM
    positions = (cache_len + jnp.arange(row_count, dtype=jnp.int32)).astype(jnp.float32)
    queries = jnp.dot(normed, w_query, preferred_element_type=jnp.float32).reshape(
        row_count, query_heads, HEAD_DIM
    )
    queries = rotate(norm_rows(queries, query_gain), positions).astype(jnp.bfloat16)
    keys_new = jnp.dot(normed, w_key, preferred_element_type=jnp.float32).reshape(
        row_count, value_heads, HEAD_DIM
    )
    keys_new = rotate(norm_rows(keys_new, key_gain), positions).astype(jnp.bfloat16)
    values_new = (
        jnp.dot(normed, w_value, preferred_element_type=jnp.float32)
        .astype(jnp.bfloat16)
        .reshape(row_count, value_heads, HEAD_DIM)
    )
    keys_cache = cache_keys.reshape(cache_keys.shape[1], value_heads, HEAD_DIM)
    values_cache = cache_values.reshape(cache_values.shape[1], value_heads, HEAD_DIM)
    attended = attend_slot(queries, keys_new, values_new, keys_cache, values_cache, cache_len)
    projected = jnp.dot(attended, w_out, preferred_element_type=jnp.float32)
    own_sum = lax.psum_scatter(
        projected.astype(jnp.bfloat16), "head", scatter_dimension=1, tiled=True
    ).astype(jnp.float32)
    head_part = lax.axis_index("head")
    residual = lax.dynamic_slice_in_dim(tokens, head_part * half_width, half_width, 1) + own_sum
    squares = lax.psum(jnp.sum(residual * residual, axis=1), "head")
    mixed_rows = (residual * lax.rsqrt(squares[:, None] / D + EPS) * mlp_gain).astype(jnp.bfloat16)
    paired = jnp.concatenate([w_gate, w_up], axis=1)
    partial_rows = jnp.dot(
        lax.all_gather(mixed_rows, "req", axis=0, tiled=True),
        paired,
        preferred_element_type=jnp.float32,
    )
    summed_rows = lax.psum(partial_rows.astype(jnp.bfloat16), "head").astype(jnp.float32)
    unit_count = w_gate.shape[1]
    active = (jax.nn.silu(summed_rows[:, :unit_count]) * summed_rows[:, unit_count:]).astype(
        jnp.bfloat16
    )
    down_part = lax.psum_scatter(
        jnp.dot(active, w_down, preferred_element_type=jnp.float32),
        "req",
        scatter_dimension=0,
        tiled=True,
    )
    output = residual + down_part
    hidden_out = output.astype(jnp.bfloat16)
    last_row = output[row_count - 1 :, :]
    collected = lax.all_gather(last_row, ("req", "head"), axis=1, tiled=True).reshape(-1, D)
    final_rows = norm_rows(collected, final_gain).astype(jnp.bfloat16)
    logits = jnp.dot(final_rows, w_vocab, preferred_element_type=jnp.float32)
    row_max = lax.pmax(jnp.max(logits, axis=1), ("req", "head"))
    row_total = lax.psum(jnp.sum(jnp.exp(logits - row_max[:, None]), axis=1), ("req", "head"))
    log_probs = logits - row_max[:, None] - jnp.log(row_total)[:, None]
    log_probs = jnp.take(log_probs, inverse_order(slot_request), axis=0)
    return (hidden_out, log_probs)


def solution(mesh):
    in_specs = (
        P("req", None),
        P(),
        P(None, "head"),
        P(None, "head"),
        P(None, "head"),
        P(),
        P(),
        P("head", None),
        P("req", None, "head"),
        P("req", None, "head"),
        P(),
        P(),
        P("head"),
        P("head", "req"),
        P("head", "req"),
        P("req", "head"),
        P(),
        P(None, ("req", "head")),
    )
    out_specs = (P("req", "head"), P(None, ("req", "head")))
    return jax.shard_map(
        on_device, mesh=mesh, in_specs=in_specs, out_specs=out_specs, check_vma=False
    )
```

profile of v0, /device:TPU:0, one launch (start us, length us, event | category | flops | bytes accessed | tf_op | source)
XLA Modules:
  0.0 381.6 jit_solution(16592259865770772343)
XLA Ops:
  7.2 1.4 dynamic_slice.11
  10.6 1.2 dynamic_slice.12
  13.2 1.1 multiply_reduce_fusion
  14.3 3.2 convolution_bitcast_fusion
  18.5 4.0 %reshape.165 = bf16[2048,4,128]{2,1,0:T(4,128)(2,1)} reshape(bf16[1,2048,512]{2,1,0:T(8,128)(2,1)} %param.26) | data formatting | bytes 4194304 | tf_op jit(solution)/shard_map/reshape | solution.py:114
  23.5 4.0 %reshape.167 = bf16[2048,4,128]{2,1,0:T(4,128)(2,1)} reshape(bf16[1,2048,512]{2,1,0:T(8,128)(2,1)} %param.27) | data formatting | bytes 4194304 | tf_op jit(solution)/shard_map/reshape | solution.py:115
  27.5 2.1 convolution_convert_fusion.2
  29.7 3.2 bitcast_reduce_fusion
  33.3 1.3 fusion.15
  35.1 3.7 convolution_convert_fusion
  39.0 10.4 %reduce-scatter.3.cloned.1.call-done = bf16[64,1024]{1,0:T(8,128)(2,1)} async-done(((bf16[64,2048]{1,0:T(8,128)(2,1)}), bf16[64,1024]{1,0:T(8,128)(2,1)}) %reduce-scatter.3.cloned.1.call-update) | async-done | bytes 131088 | tf_op jit(solution)/shard_map/reduce_scatter | solution.py:118
  50.5 2.5 psum.21
  52.9 1.7 multiply_convert_fusion.1
  54.7 62.0 %all-gather.2.cloned.1.call-done = bf16[1024,1024]{1,0:T(8,128)(2,1)} async-done(((bf16[64,1024]{1,0:T(8,128)(2,1)}), bf16[1024,1024]{1,0:T(8,128)(2,1)}) %all-gather.2.cloned.1.call-update) | async-done | bytes 2097168 | tf_op jit(solution)/shard_map/all_gather | solution.py:127
  116.6 4.9 %convolution_convert_fusion.1 = bf16[1024,768]{1,0:T(8,128)(2,1)} fusion(bf16[1024,1024]{1,0:T(8,128)(2,1)} %all-gather.2.cloned.1.call-done, bf16[1024,384]{1,0:T(8,128)(2,1)} %param.32, bf16[1024,384]{1,0:T(8,128)(2,1)} %param.31), kind=kOutput, calls=%fused_computation.11 | convolution fusion | flops 1614544896 | bytes 5242880 | tf_op jit(solution)/shard_map/dot_general | solution.py:126
  121.7 19.1 %all-reduce.2.cloned.1.call-done = bf16[1024,768]{1,0:T(8,128)(2,1)} async-done(((bf16[1024,768]{1,0:T(8,128)(2,1)}), bf16[1024,768]{1,0:T(8,128)(2,1)}) %all-reduce.2.cloned.1.call-update) | async-done | bytes 1572880 | tf_op jit(solution)/shard_map/psum | solution.py:131
  140.8 1.6 convert_element_type.67
  142.5 3.2 fusion.21
  146.5 95.7 %reduce-scatter.5.cloned.1.call-done = f32[64,1024]{1,0:T(8,128)} async-done(((f32[1024,1024]{1,0:T(8,128)}), f32[64,1024]{1,0:T(8,128)}) %reduce-scatter.5.cloned.1.call-update) | async-done | bytes 262160 | tf_op jit(solution)/shard_map/reduce_scatter | solution.py:136
  242.2 1.6 fusion.41
  243.9 40.2 %all_gather.7 = f32[1,32768]{1,0:T(1,128)S(1)} all-gather(f32[1,1024]{1,0:T(1,128)S(1)} %slice.36), channel_id=1, replica_groups=mesh['req'=16,'head'=2] {'req','head'}, dimensions={1}, use_global_device_ids=true | all-gather | bytes 135168 | tf_op jit(solution)/shard_map/all_gather | solution.py:145
  285.7 9.4 %fusion.44 = (f32[16]{0:T(128)S(1)}, f32[16,4748]{1,0:T(8,128)S(1)}) fusion(bf16[2048,4748]{0,1:T(8,128)(2,1)} %param.35, f32[16,2048]{1,0:T(8,128)S(1)} %reshape.169, f32[2048]{0:T(1024)S(1)} %copy-done.5, f32[16]{0:T(128)S(1)} %add_rsqrt_fusion.2), kind=kOutput, calls=%fused_computation.86 | convolution fusion | flops 311339200 | bytes 19891072 | tf_op jit(solution)/shard_map/dot_general | solution.py:147
  295.1 36.9 %pmax.7 = f32[16]{0:T(128)S(1)} all-reduce(f32[16]{0:T(128)S(1)} %get-tuple-element.14), channel_id=1, replica_groups=mesh['req'=16,'head'=2] {'req','head'}, use_global_device_ids=true, to_apply=%region_13.14 | all-reduce | flops 16 | bytes 128 | tf_op jit(solution)/shard_map/pmax | solution.py:148
  332.2 41.2 %psum.23 = f32[16]{0:T(128)S(1)} all-reduce(f32[16]{0:T(128)S(1)} %exponential_reduce_fusion), channel_id=1, replica_groups=mesh['req'=16,'head'=2] {'req','head'}, use_global_device_ids=true, to_apply=%region_15.16 | all-reduce | flops 16 | bytes 128 | tf_op jit(solution)/shard_map/psum | solution.py:149
  (76 shorter events, 9.6 us)
Async XLA Ops:
  7.2 15.3 %copy-start = (bf16[2048,512]{1,0:T(8,128)(2,1)S(1)}, bf16[2048,512]{1,0:T(8,128)(2,1)}, u32[]{:S(2)}) copy-start(bf16[2048,512]{1,0:T(8,128)(2,1)} %param.21) | copy-start | bytes 6291460
  7.2 42.2 %reduce-scatter.3.cloned.1.call-start = ((), (), s32[]{:S(2)}) async-start(), calls=%async_computation.2 | async-start | bytes 393216 | tf_op jit(solution)/shard_map/reduce_scatter | solution.py:118
  14.3 3.8 copy-start.7
  18.4 4.0 %copy-start.1 = (bf16[64,2048]{1,0:T(8,128)(2,1)S(1)}, bf16[64,2048]{1,0:T(8,128)(2,1)}, u32[]{:S(2)}) copy-start(bf16[64,2048]{1,0:T(8,128)(2,1)} %param.18) | copy-start | bytes 786436
  18.4 4.0 %copy-start.4 = (f32[2048]{0:T(1024)S(1)}, f32[2048]{0:T(1024)}, u32[]{:S(2)}) copy-start(f32[2048]{0:T(1024)} %param.19) | copy-start | bytes 24580
  22.5 0.8 copy-start.8
  29.7 3.6 copy-start.2
  35.1 17.8 %copy-start.6 = (f32[1024]{0:T(1024)S(1)}, f32[1024]{0:T(1024)}, u32[]{:S(2)}) copy-start(f32[1024]{0:T(1024)} %param.30) | copy-start | bytes 12292
  38.9 77.7 %all-gather.2.cloned.1.call-start = ((), (), s32[]{:S(2)}) async-start(), calls=%async_computation.3 | async-start | bytes 2228224 | tf_op jit(solution)/shard_map/all_gather | solution.py:127
  54.6 86.2 %all-reduce.2.cloned.1.call-start = ((), (), s32[]{:S(2)}) async-start(), calls=%async_computation.4 | async-start | bytes 3145728 | tf_op jit(solution)/shard_map/psum | solution.py:131
  121.6 20.8 %copy-start.9 = (bf16[384,1024]{1,0:T(8,128)(2,1)S(1)}, bf16[384,1024]{1,0:T(8,128)(2,1)}, u32[]{:S(2)}) copy-start(bf16[384,1024]{1,0:T(8,128)(2,1)} %param.33) | copy-start | bytes 2359300
  121.6 120.6 %reduce-scatter.5.cloned.1.call-start = ((), (), s32[]{:S(2)}) async-start(), calls=%async_computation.5 | async-start | bytes 4456448 | tf_op jit(solution)/shard_map/reduce_scatter | solution.py:136
  145.7 0.7 copy-start.10
  145.7 96.5 %copy-start.3 = (bf16[64,1024]{1,0:T(8,128)(2,1)S(1)}, bf16[64,1024]{1,0:T(8,128)(2,1)}, u32[]{:S(2)}) copy-start(bf16[64,1024]{1,0:T(8,128)(2,1)} %reduce-scatter.3.cloned.1.call-done) | copy-start | bytes 393220
  145.7 140.1 %copy-start.5 = (f32[2048]{0:T(1024)S(1)}, f32[2048]{0:T(1024)}, u32[]{:S(2)}) copy-start(f32[2048]{0:T(1024)} %param.34) | copy-start | bytes 24580
Sparse Core Ops, SparseCore 0:
  39.0 10.3 reduce-scatter.2
  54.7 61.8 all-gather.1
  121.7 19.0 all-reduce.1
  145.8 96.3 reduce-scatter.4
where the time goes:
time: 382 us
  waiting for transfers between devices  187 us (49%)
  blocking collectives  121 us (32%)
  matrix products  32.2 us (8%)
  between operations  16.1 us (4%)
  local copies, waits for them, and re-layouts  13.1 us (3%)
  other arithmetic  11.8 us (3%)
    reduce_scatter x1, waiting for transfers between devices, on_device(): lax.psum_scatter(jnp.dot(active, w_down, preferred_element_type=jnp.float...  95.7 us
    all_gather x1, waiting for transfers between devices, on_device(): lax.all_gather(mixed_rows, 'req', axis=0, tiled=True)  62 us
    psum x1, blocking collectives, on_device(): lax.psum(jnp.sum(jnp.exp(logits - row_max[:, None]), axis=1), ('req', 'he...  41.2 us
    all_gather x1, blocking collectives, on_device(): lax.all_gather(last_row, ('req', 'head'), axis=1, tiled=True).reshape(-1, D)  40.2 us
    pmax x1, blocking collectives, on_device(): row_max = lax.pmax(jnp.max(logits, axis=1), ('req', 'head'))  36.9 us
    psum x1, waiting for transfers between devices, on_device(): lax.psum(partial_rows.astype(jnp.bfloat16), 'head').astype(jnp.float32)  19.1 us
    reduce_scatter x1, waiting for transfers between devices, on_device(): lax.psum_scatter(projected.astype(jnp.bfloat16), 'head', scatter_dimensio...  10.4 us
    dot_general x1, matrix products, on_device(): logits = jnp.dot(final_rows, w_vocab, preferred_element_type=jnp.float32)  9.35 us
  transfers between devices with their start and end apart: 4, of which 4 were waited for; matrix products, arithmetic and copies ran while one was open for 0% of the time, Pallas kernels for 0%

commit v1 on v0

--- a/solution.py
+++ b/solution.py
@@ -37,6 +37,42 @@
     )
 
 
+def radices(count):
+    if count == 16:
+        return (4, 2, 2)
+    side = round(count ** (1 / 3))
+    if side**3 == count:
+        return (side, side, side)
+    return (count, 1, 1)
+
+
+def shifted(count, digit, step):
+    sizes = radices(count)
+    stride = 1
+    for size in sizes[digit + 1 :]:
+        stride *= size
+    pairs = []
+    for i in range(count):
+        place = i // stride % sizes[digit]
+        pairs.append((i, i + ((place + step) % sizes[digit] - place) * stride))
+    return pairs
+
+
+def send(rows, count, digit, step):
+    return lax.ppermute(rows, "req", shifted(count, digit, step))
+
+
+def other_core(rows):
+    return lax.ppermute(rows, "head", [(0, 1), (1, 0)])
+
+
+def to_all(block):
+    count = lax.axis_size("req") * lax.axis_size("head")
+    return lax.all_to_all(
+        jnp.broadcast_to(block[None], (count,) + block.shape), ("req", "head"), 0, 0, tiled=True
+    )
+
+
 def attend_slot(queries, keys_new, values_new, keys_cache, values_cache, cache_len):
     row_count, value_heads, head_size = keys_new.shape
     group_size = queries.shape[1] // value_heads
@@ -66,6 +102,46 @@
         "kgst,tkd->skgd", new_weights, values_new, preferred_element_type=jnp.float32
     )
     return blended.reshape(row_count, value_heads * group_size * head_size).astype(jnp.bfloat16)
+
+
+def feed_forward(rows, paired, w_down):
+    partial_rows = jnp.dot(rows, paired, preferred_element_type=jnp.float32)
+    summed = partial_rows + other_core(partial_rows.astype(jnp.bfloat16)).astype(jnp.float32)
+    unit_count = w_down.shape[0]
+    active = (jax.nn.silu(summed[:, :unit_count]) * summed[:, unit_count:]).astype(jnp.bfloat16)
+    return jnp.dot(active, w_down, preferred_element_type=jnp.float32)
+
+
+def spread_feed_forward(mixed_rows, paired, w_down):
+    count = lax.axis_size("req")
+    sizes = radices(count)
+    row_count = mixed_rows.shape[0]
+    levels = [mixed_rows] + [send(mixed_rows, count, 0, step) for step in range(1, sizes[0])]
+    half = max(1, sizes[0] // 2)
+    groups = [(levels[:half], 2, 1), (levels[half:], 1, 2)]
+    back = []
+    for blocks, first, second in groups:
+        if not blocks:
+            continue
+        held = jnp.concatenate(blocks, axis=0)
+        held = jnp.concatenate(
+            [held] + [send(held, count, first, step) for step in range(1, sizes[first])], axis=0
+        )
+        farther = [send(held, count, second, step) for step in range(1, sizes[second])]
+        near = feed_forward(held, paired, w_down)
+        for step, rows in enumerate(farther, 1):
+            part = feed_forward(rows, paired, w_down).astype(jnp.bfloat16)
+            near = near + send(part, count, second, -step).astype(jnp.float32)
+        width = len(blocks) * row_count
+        total = near[:width]
+        for step in range(1, sizes[first]):
+            part = near[step * width : (step + 1) * width].astype(jnp.bfloat16)
+            total = total + send(part, count, first, -step).astype(jnp.float32)
+        back += [total[i * row_count : (i + 1) * row_count] for i in range(len(blocks))]
+    result = back[0]
+    for step in range(1, sizes[0]):
+        result = result + send(back[step].astype(jnp.bfloat16), count, 0, -step).astype(jnp.float32)
+    return result
 
 
 def on_device(
@@ -115,40 +191,29 @@
     values_cache = cache_values.reshape(cache_values.shape[1], value_heads, HEAD_DIM)
     attended = attend_slot(queries, keys_new, values_new, keys_cache, values_cache, cache_len)
     projected = jnp.dot(attended, w_out, preferred_element_type=jnp.float32)
-    own_sum = lax.psum_scatter(
-        projected.astype(jnp.bfloat16), "head", scatter_dimension=1, tiled=True
-    ).astype(jnp.float32)
+    both = tokens + projected + other_core(projected.astype(jnp.bfloat16)).astype(jnp.float32)
+    inverse = lax.rsqrt(jnp.mean(both * both, axis=1, keepdims=True) + EPS)
     head_part = lax.axis_index("head")
-    residual = lax.dynamic_slice_in_dim(tokens, head_part * half_width, half_width, 1) + own_sum
-    squares = lax.psum(jnp.sum(residual * residual, axis=1), "head")
-    mixed_rows = (residual * lax.rsqrt(squares[:, None] / D + EPS) * mlp_gain).astype(jnp.bfloat16)
+    residual = lax.dynamic_slice_in_dim(both, head_part * half_width, half_width, 1)
+    mixed_rows = (residual * inverse * mlp_gain).astype(jnp.bfloat16)
     paired = jnp.concatenate([w_gate, w_up], axis=1)
-    partial_rows = jnp.dot(
-        lax.all_gather(mixed_rows, "req", axis=0, tiled=True),
-        paired,
-        preferred_element_type=jnp.float32,
-    )
-    summed_rows = lax.psum(partial_rows.astype(jnp.bfloat16), "head").astype(jnp.float32)
-    unit_count = w_gate.shape[1]
-    active = (jax.nn.silu(summed_rows[:, :unit_count]) * summed_rows[:, unit_count:]).astype(
-        jnp.bfloat16
-    )
-    down_part = lax.psum_scatter(
-        jnp.dot(active, w_down, preferred_element_type=jnp.float32),
-        "req",
-        scatter_dimension=0,
-        tiled=True,
-    )
-    output = residual + down_part
+    output = residual + spread_feed_forward(mixed_rows, paired, w_down)
     hidden_out = output.astype(jnp.bfloat16)
-    last_row = output[row_count - 1 :, :]
-    collected = lax.all_gather(last_row, ("req", "head"), axis=1, tiled=True).reshape(-1, D)
+    last_row = output[row_count - 1 :, :].reshape(8, half_width // 8)
+    collected = to_all(last_row).reshape(-1, D)
+    collected = jnp.take(collected, inverse_order(slot_request), axis=0)
     final_rows = norm_rows(collected, final_gain).astype(jnp.bfloat16)
     logits = jnp.dot(final_rows, w_vocab, preferred_element_type=jnp.float32)
-    row_max = lax.pmax(jnp.max(logits, axis=1), ("req", "head"))
-    row_total = lax.psum(jnp.sum(jnp.exp(logits - row_max[:, None]), axis=1), ("req", "head"))
-    log_probs = logits - row_max[:, None] - jnp.log(row_total)[:, None]
-    log_probs = jnp.take(log_probs, inverse_order(slot_request), axis=0)
+    own_max = jnp.max(logits, axis=1)
+    own_total = jnp.sum(jnp.exp(logits - own_max[:, None]), axis=1)
+    requests = own_max.shape[0]
+    stats = jnp.zeros((8, 128), jnp.float32).at[0, :requests].set(own_max).at[1, :requests].set(own_total)
+    everyone = to_all(stats)
+    row_max = jnp.max(everyone[:, 0, :requests], axis=0)
+    row_total = jnp.sum(
+        everyone[:, 1, :requests] * jnp.exp(everyone[:, 0, :requests] - row_max[None, :]), axis=0
+    )
+    log_probs = logits - (row_max + jnp.log(row_total))[:, None]
     return (hidden_out, log_probs)
 
 

time: 382 us -> 144 us (0.38)
  waiting for transfers between devices: 187 us -> 56.8 us
  blocking collectives: 121 us -> 10 us
  starting transfers between devices: 0.16 us -> 25.6 us
  between operations: 16.1 us -> 3.24 us
  other arithmetic: 11.8 us -> 6.41 us
  matrix products: 32.2 us -> 27.7 us
    reduce_scatter x2 -> x0, waiting for transfers between devices: 106 us -> none  [the longest x1 95.7 us: on_device(): lax.psum_scatter(jnp.dot(active, w_down, preferred_element_type=jnp.float...]
    all_gather x1 -> x0, waiting for transfers between devices: 62 us -> none  [on_device(): lax.all_gather(mixed_rows, 'req', axis=0, tiled=True)]
    ppermute x0 -> x19, waiting for transfers between devices: none -> 48.6 us  [the longest x14 48.6 us: send(): return lax.ppermute(rows, 'req', shifted(count, digit, step))]
    psum x2 -> x0, blocking collectives: 43.7 us -> none  [the longest x1 41.2 us: on_device(): lax.psum(jnp.sum(jnp.exp(logits - row_max[:, None]), axis=1), ('req', 'he...]
    all_gather x1 -> x0, blocking collectives: 40.2 us -> none  [on_device(): lax.all_gather(last_row, ('req', 'head'), axis=1, tiled=True).reshape(-1, D)]
    pmax x1 -> x0, blocking collectives: 36.9 us -> none  [on_device(): row_max = lax.pmax(jnp.max(logits, axis=1), ('req', 'head'))]
    ppermute x0 -> x19, starting transfers between devices: none -> 21.2 us  [the longest x14 20.4 us: send(): return lax.ppermute(rows, 'req', shifted(count, digit, step))]
    psum x1 -> x0, waiting for transfers between devices: 19.1 us -> none  [on_device(): lax.psum(partial_rows.astype(jnp.bfloat16), 'head').astype(jnp.float32)]
  transfers between devices with their start and end apart: 4 -> 20, of which waited for: 4 -> 11; matrix products, arithmetic and copies ran while one was open for 0% -> 5% of each run, Pallas kernels for 0% -> 0%
where the time goes in v1:
time: 144 us; the launch traced here: 143 us
  waiting for transfers between devices  56.8 us (39%)
  matrix products  27.7 us (19%)
  starting transfers between devices  25.6 us (18%)
  local copies, waits for them, and re-layouts  13.6 us (9%)
  blocking collectives  10 us (7%)
  other arithmetic  6.41 us (4%)
  between operations  3.24 us (2%)
    ppermute x14, waiting for transfers between devices, send(): return lax.ppermute(rows, 'req', shifted(count, digit, step))  48.6 us
    ppermute x14, starting transfers between devices, send(): return lax.ppermute(rows, 'req', shifted(count, digit, step))  20.4 us
    all_to_all x1, blocking collectives, to_all(): lax.all_to_all(jnp.broadcast_to(block[None], (count,) + block.shape), ('r...  10 us
    dot_general x1, matrix products, on_device(): logits = jnp.dot(final_rows, w_vocab, preferred_element_type=jnp.float32)  9.5 us
    all_to_all x1, waiting for transfers between devices, to_all(): lax.all_to_all(jnp.broadcast_to(block[None], (count,) + block.shape), ('r...  8.2 us
    all_to_all x1, starting transfers between devices, to_all(): lax.all_to_all(jnp.broadcast_to(block[None], (count,) + block.shape), ('r...  4.4 us
    reshape x1, local copies, waits for them, and re-layouts, on_device(): keys_cache = cache_keys.reshape(cache_keys.shape[1], value_heads, HEAD_DIM)  4.12 us
    dot_general x1, matrix products, attend_slot(): jnp.einsum('skgd,lkd->kgsl', grouped, keys_cache, preferred_element_type=...  3.25 us
  transfers between devices with their start and end apart: 20, of which 11 were waited for; matrix products, arithmetic and copies ran while one was open for 5% of the time, Pallas kernels for 0%

profile of v1, /device:TPU:0, one launch (start us, length us, event | category | flops | bytes accessed | tf_op | source)
XLA Modules:
  0.0 143.3 jit_solution(7935078646604055856)
XLA Ops:
  7.7 3.2 %convolution_bitcast_fusion = f32[8,8,8,128]{3,1,2,0:T(8,128)S(1)} fusion(bf16[2048,1024]{1,0:T(8,128)(2,1)} %param.24, bf16[64,2048]{1,0:T(8,128)(2,1)} %param.22, f32[2048]{0:T(1024)} %param.23, f32[64]{0:T(128)S(1)} %add_rsqrt_fusion.4), kind=kOutput, calls=%fused_computation.16 | convolution fusion | flops 268959744 | bytes 4727040 | tf_op jit(solution)/shard_map/dot_general | solution.py:177
  13.0 4.1 %reshape.239 = bf16[2048,4,128]{2,1,0:T(4,128)(2,1)} reshape(bf16[1,2048,512]{2,1,0:T(8,128)(2,1)} %param.30) | data formatting | bytes 4194304 | tf_op jit(solution)/shard_map/reshape | solution.py:190
  17.1 2.1 %reshape.241 = bf16[2048,4,128]{2,1,0:T(4,128)(2,1)} reshape(bf16[1,2048,512]{2,1,0:T(8,128)(2,1)S(1)} %copy-done.3) | data formatting | bytes 4194304 | tf_op jit(solution)/shard_map/reshape | solution.py:191
  19.2 2.1 %convolution_convert_fusion.2 = bf16[64,512]{1,0:T(8,128)(2,1)S(1)} fusion(bf16[2048,512]{1,0:T(8,128)(2,1)} %param.26, bf16[64,2048]{1,0:T(8,128)(2,1)S(1)} %copy-done.2, f32[2048]{0:T(1024)S(1)} %copy-done.5, f32[64]{0:T(128)S(1)} %add_rsqrt_fusion.4), kind=kOutput, calls=%fused_computation.21 | convolution fusion | flops 134774784 | bytes 2433280 | tf_op jit(solution)/shard_map/dot_general | solution.py:186
  21.3 3.3 %bitcast_reduce_fusion = (f32[4,2,64]{2,1,0:T(2,128)S(1)}, f32[4,64,2,2048]{3,1,2,0:T(8,128)S(1)}) fusion(pred[2048]{0:T(1024)(128)(4,1)S(1)} %iota_compare_fusion.2, bf16[2048,4,128,1]{2,1,0,3:T(4,128)(2,1)} %bitcast.77, bf16[64,4,2,64]{3,0,2,1:T(8,128)(2,1)S(1)} %bitcast.80, bf16[64,4,2,64]{3,0,2,1:T(8,128)(2,1)S(1)} %bitcast.78), kind=kOutput, calls=%fused_computation.2 | convolution fusion | flops 271842816 | bytes 6426624 | tf_op jit(solution)/shard_map/skgd,lkd->kgsl/dot_general | solution.py:89
  26.8 3.0 %fusion.74 = (bf16[64,2048]{1,0:T(8,128)(2,1)S(1)}, f32[64,2048]{1,0:T(8,128)S(1)}) fusion(bf16[64,1024]{1,0:T(8,128)(2,1)S(1)} %convert_element_type.121, bf16[1024,2048]{1,0:T(8,128)(2,1)} %param.29), kind=kOutput, calls=%fused_computation.129 | convolution fusion | flops 268566528 | bytes 5111808 | tf_op jit(solution)/shard_map/dot_general | solution.py:193
  31.9 2.9 %collective-permute-start.1 = (bf16[64,1024]{1,0:T(8,128)(2,1)S(1)}, bf16[64,1024]{1,0:T(8,128)(2,1)S(1)}, u32[]{:S(2)}, u32[]{:S(2)}) collective-permute-start(bf16[64,1024]{1,0:T(8,128)(2,1)S(1)} %multiply_convert_fusion), channel_id=1, source_target_pairs={{0,8},{2,10},{4,12},{6,14},{8,16},{10,18},{12,20},{14,22},{16,24},... | collective-permute-start | bytes 393224 | tf_op jit(solution)/shard_map/ppermute | solution.py:62
  34.8 2.3 %collective-permute-start.10 = (bf16[64,1024]{1,0:T(8,128)(2,1)S(1)}, bf16[64,1024]{1,0:T(8,128)(2,1)S(1)}, u32[]{:S(2)}, u32[]{:S(2)}) collective-permute-start(bf16[64,1024]{1,0:T(8,128)(2,1)S(1)} %multiply_convert_fusion), channel_id=1, source_target_pairs={{0,24},{2,26},{4,28},{6,30},{8,0},{10,2},{12,4},{14,6},{16,8},{18,... | collective-permute-start | bytes 393224 | tf_op jit(solution)/shard_map/ppermute | solution.py:62
  39.2 2.0 %collective-permute-done.1 = bf16[64,1024]{1,0:T(8,128)(2,1)S(1)} collective-permute-done((bf16[64,1024]{1,0:T(8,128)(2,1)S(1)}, bf16[64,1024]{1,0:T(8,128)(2,1)S(1)}, u32[]{:S(2)}, u32[]{:S(2)}) %collective-permute-start.1) | collective-permute-done | bytes 131104 | tf_op jit(solution)/shard_map/ppermute | solution.py:62
  41.2 1.8 %collective-permute-start.2 = (bf16[128,1024]{1,0:T(8,128)(2,1)S(1)}, bf16[128,1024]{1,0:T(8,128)(2,1)S(1)}, u32[]{:S(2)}, u32[]{:S(2)}) collective-permute-start(bf16[128,1024]{1,0:T(8,128)(2,1)S(1)} %pad_maximum_fusion.1), channel_id=1, source_target_pairs={{0,2},{2,0},{4,6},{6,4},{8,10},{10,8},{12,14},{14,12},{16,18},{18,... | collective-permute-start | bytes 786440 | tf_op jit(solution)/shard_map/ppermute | solution.py:62
  43.0 6.2 %collective-permute-done.9 = bf16[64,1024]{1,0:T(8,128)(2,1)S(1)} collective-permute-done((bf16[64,1024]{1,0:T(8,128)(2,1)S(1)}, bf16[64,1024]{1,0:T(8,128)(2,1)S(1)}, u32[]{:S(2)}, u32[]{:S(2)}) %collective-permute-start.9) | collective-permute-done | bytes 131104 | tf_op jit(solution)/shard_map/ppermute | solution.py:62
  49.2 1.6 %collective-permute-start.11 = (bf16[128,1024]{1,0:T(8,128)(2,1)S(1)}, bf16[128,1024]{1,0:T(8,128)(2,1)S(1)}, u32[]{:S(2)}, u32[]{:S(2)}) collective-permute-start(bf16[128,1024]{1,0:T(8,128)(2,1)S(1)} %pad_maximum_fusion.2), channel_id=1, source_target_pairs={{0,4},{2,6},{4,0},{6,2},{8,12},{10,14},{12,8},{14,10},{16,20},{18,... | collective-permute-start | bytes 786440 | tf_op jit(solution)/shard_map/ppermute | solution.py:62
  52.1 6.3 %collective-permute-done.11 = bf16[128,1024]{1,0:T(8,128)(2,1)S(1)} collective-permute-done((bf16[128,1024]{1,0:T(8,128)(2,1)S(1)}, bf16[128,1024]{1,0:T(8,128)(2,1)S(1)}, u32[]{:S(2)}, u32[]{:S(2)}) %collective-permute-start.11) | collective-permute-done | bytes 262176 | tf_op jit(solution)/shard_map/ppermute | solution.py:62
  60.6 8.1 %collective-permute-done.4 = bf16[256,1024]{1,0:T(8,128)(2,1)S(1)} collective-permute-done((bf16[256,1024]{1,0:T(8,128)(2,1)S(1)}, bf16[256,1024]{1,0:T(8,128)(2,1)S(1)}, u32[]{:S(2)}, u32[]{:S(2)}) %collective-permute-start.4) | collective-permute-done | bytes 524320 | tf_op jit(solution)/shard_map/ppermute | solution.py:62
  69.5 1.7 %collective-permute-done.13 = bf16[256,1024]{1,0:T(8,128)(2,1)S(1)} collective-permute-done((bf16[256,1024]{1,0:T(8,128)(2,1)S(1)}, bf16[256,1024]{1,0:T(8,128)(2,1)S(1)}, u32[]{:S(2)}, u32[]{:S(2)}) %collective-permute-start.13) | collective-permute-done | bytes 524320 | tf_op jit(solution)/shard_map/ppermute | solution.py:62
  74.5 1.6 %collective-permute-start.15 = (bf16[256,1024]{1,0:T(8,128)(2,1)S(1)}, bf16[256,1024]{1,0:T(8,128)(2,1)S(1)}, u32[]{:S(2)}, u32[]{:S(2)}) collective-permute-start(bf16[256,1024]{1,0:T(8,128)(2,1)S(1)} %convolution_convert_fusion), channel_id=1, source_target_pairs={{0,2},{2,0},{4,6},{6,4},{8,10},{10,8},{12,14},{14,12},{16,18},{18,... | collective-permute-start | bytes 1572872 | tf_op jit(solution)/shard_map/ppermute | solution.py:62
  76.1 10.6 %collective-permute-done.6 = bf16[256,1024]{1,0:T(8,128)(2,1)S(1)} collective-permute-done((bf16[256,1024]{1,0:T(8,128)(2,1)S(1)}, bf16[256,1024]{1,0:T(8,128)(2,1)S(1)}, u32[]{:S(2)}, u32[]{:S(2)}) %collective-permute-start.6) | collective-permute-done | bytes 524320 | tf_op jit(solution)/shard_map/ppermute | solution.py:62
  91.0 4.2 %collective-permute-done.7 = bf16[128,1024]{1,0:T(8,128)(2,1)S(1)} collective-permute-done((bf16[128,1024]{1,0:T(8,128)(2,1)S(1)}, bf16[128,1024]{1,0:T(8,128)(2,1)S(1)}, u32[]{:S(2)}, u32[]{:S(2)}) %collective-permute-start.7) | collective-permute-done | bytes 262176 | tf_op jit(solution)/shard_map/ppermute | solution.py:62
  98.7 2.4 %collective-permute-done.8 = bf16[64,1024]{1,0:T(8,128)(2,1)S(1)} collective-permute-done((bf16[64,1024]{1,0:T(8,128)(2,1)S(1)}, bf16[64,1024]{1,0:T(8,128)(2,1)S(1)}, u32[]{:S(2)}, u32[]{:S(2)}) %collective-permute-start.8) | collective-permute-done | bytes 131104 | tf_op jit(solution)/shard_map/ppermute | solution.py:62
  101.2 6.3 %collective-permute-done.17 = bf16[64,1024]{1,0:T(8,128)(2,1)S(1)} collective-permute-done((bf16[64,1024]{1,0:T(8,128)(2,1)S(1)}, bf16[64,1024]{1,0:T(8,128)(2,1)S(1)}, u32[]{:S(2)}, u32[]{:S(2)}) %collective-permute-start.17) | collective-permute-done | bytes 131104 | tf_op jit(solution)/shard_map/ppermute | solution.py:62
  108.9 4.4 %all-to-all-start = ((f32[32,8,128]{2,1,0:T(8,128)}), f32[32,8,128]{2,1,0:T(8,128)S(1)}, u32[]{:S(2)}, u32[]{:S(2)}) async-start(f32[32,8,128]{2,1,0:T(8,128)} %broadcast_in_dim.86), calls=%async_computation | async-start | bytes 262144 | tf_op jit(solution)/shard_map/all_to_all | solution.py:71
  113.3 8.2 %all-to-all-done = f32[32,8,128]{2,1,0:T(8,128)S(1)} async-done(((f32[32,8,128]{2,1,0:T(8,128)}), f32[32,8,128]{2,1,0:T(8,128)S(1)}, u32[]{:S(2)}, u32[]{:S(2)}) %all-to-all-start) | async-done | bytes 131104 | tf_op jit(solution)/shard_map/all_to_all | solution.py:71
  122.4 9.5 %fusion.79 = (f32[16]{0:T(128)S(1)}, f32[16,4748]{1,0:T(8,128)S(1)}) fusion(bf16[2048,4748]{0,1:T(8,128)(2,1)} %param.39, f32[16,2048]{1,0:T(8,128)S(1)} %gather_fusion, f32[2048]{0:T(1024)S(1)} %copy-done.6, f32[16]{0:T(128)S(1)} %add_rsqrt_fusion.2, pred[16]{0:T(512)(128)(4,1)S(1)} %compare_and_fusion), kind=kOutput, calls=%fused_computation.134 | convolution fusion | flops 311371968 | bytes 19891088 | tf_op jit(solution)/shard_map/dot_general | solution.py:206
  132.4 10.0 %all_to_all.10 = f32[32,8,128]{2,1,0:T(8,128)S(1)} all-to-all(f32[32,8,128]{2,1,0:T(8,128)S(1)} %broadcast_in_dim.89), channel_id=1, replica_groups=mesh['req'=16,'head'=2] {'req','head'}, dimensions={0} | all-to-all | bytes 262144 | tf_op jit(solution)/shard_map/all_to_all | solution.py:71
  (129 shorter events, 32.1 us)
Async XLA Ops:
  0.6 11.3 %copy-start = (bf16[2048,512]{1,0:T(8,128)(2,1)S(1)}, bf16[2048,512]{1,0:T(8,128)(2,1)}, u32[]{:S(2)}) copy-start(bf16[2048,512]{1,0:T(8,128)(2,1)} %param.25) | copy-start | bytes 6291460
  13.0 4.1 %copy-start.3 = (bf16[1,2048,512]{2,1,0:T(8,128)(2,1)S(1)}, bf16[1,2048,512]{2,1,0:T(8,128)(2,1)}, u32[]{:S(2)}) copy-start(bf16[1,2048,512]{2,1,0:T(8,128)(2,1)} %param.31) | copy-start | bytes 6291460
  29.9 1.7 %collective-permute-start = (bf16[64,2048]{1,0:T(8,128)(2,1)S(1)}, bf16[64,2048]{1,0:T(8,128)(2,1)S(1)}, u32[]{:S(2)}, u32[]{:S(2)}) collective-permute-start(bf16[64,2048]{1,0:T(8,128)(2,1)S(1)} %get-tuple-element.44), channel_id=1, source_target_pairs={{0,1},{1,0},{2,3},{3,2},{4,5},{5,4},{6,7},{7,6},{8,9},{9,8},{10,11... | collective-permute-start | bytes 786440 | tf_op jit(solution)/shard_map/ppermute | solution.py:66
  31.9 9.3 %collective-permute-start.1 = (bf16[64,1024]{1,0:T(8,128)(2,1)S(1)}, bf16[64,1024]{1,0:T(8,128)(2,1)S(1)}, u32[]{:S(2)}, u32[]{:S(2)}) collective-permute-start(bf16[64,1024]{1,0:T(8,128)(2,1)S(1)} %multiply_convert_fusion), channel_id=1, source_target_pairs={{0,8},{2,10},{4,12},{6,14},{8,16},{10,18},{12,20},{14,22},{16,24},... | collective-permute-start | bytes 393224 | tf_op jit(solution)/shard_map/ppermute | solution.py:62
  34.8 8.2 %collective-permute-start.10 = (bf16[64,1024]{1,0:T(8,128)(2,1)S(1)}, bf16[64,1024]{1,0:T(8,128)(2,1)S(1)}, u32[]{:S(2)}, u32[]{:S(2)}) collective-permute-start(bf16[64,1024]{1,0:T(8,128)(2,1)S(1)} %multiply_convert_fusion), channel_id=1, source_target_pairs={{0,24},{2,26},{4,28},{6,30},{8,0},{10,2},{12,4},{14,6},{16,8},{18,... | collective-permute-start | bytes 393224 | tf_op jit(solution)/shard_map/ppermute | solution.py:62
  37.1 12.0 %collective-permute-start.9 = (bf16[64,1024]{1,0:T(8,128)(2,1)S(1)}, bf16[64,1024]{1,0:T(8,128)(2,1)S(1)}, u32[]{:S(2)}, u32[]{:S(2)}) collective-permute-start(bf16[64,1024]{1,0:T(8,128)(2,1)S(1)} %multiply_convert_fusion), channel_id=1, source_target_pairs={{0,16},{2,18},{4,20},{6,22},{8,24},{10,26},{12,28},{14,30},{16,0},... | collective-permute-start | bytes 393224 | tf_op jit(solution)/shard_map/ppermute | solution.py:62
  41.2 9.6 %collective-permute-start.2 = (bf16[128,1024]{1,0:T(8,128)(2,1)S(1)}, bf16[128,1024]{1,0:T(8,128)(2,1)S(1)}, u32[]{:S(2)}, u32[]{:S(2)}) collective-permute-start(bf16[128,1024]{1,0:T(8,128)(2,1)S(1)} %pad_maximum_fusion.1), channel_id=1, source_target_pairs={{0,2},{2,0},{4,6},{6,4},{8,10},{10,8},{12,14},{14,12},{16,18},{18,... | collective-permute-start | bytes 786440 | tf_op jit(solution)/shard_map/ppermute | solution.py:62
  49.2 9.2 %collective-permute-start.11 = (bf16[128,1024]{1,0:T(8,128)(2,1)S(1)}, bf16[128,1024]{1,0:T(8,128)(2,1)S(1)}, u32[]{:S(2)}, u32[]{:S(2)}) collective-permute-start(bf16[128,1024]{1,0:T(8,128)(2,1)S(1)} %pad_maximum_fusion.2), channel_id=1, source_target_pairs={{0,4},{2,6},{4,0},{6,2},{8,12},{10,14},{12,8},{14,10},{16,20},{18,... | collective-permute-start | bytes 786440 | tf_op jit(solution)/shard_map/ppermute | solution.py:62
  50.9 17.8 %collective-permute-start.4 = (bf16[256,1024]{1,0:T(8,128)(2,1)S(1)}, bf16[256,1024]{1,0:T(8,128)(2,1)S(1)}, u32[]{:S(2)}, u32[]{:S(2)}) collective-permute-start(bf16[256,1024]{1,0:T(8,128)(2,1)S(1)} %pad_maximum_fusion), channel_id=1, source_target_pairs={{0,4},{2,6},{4,0},{6,2},{8,12},{10,14},{12,8},{14,10},{16,20},{18,... | collective-permute-start | bytes 1572872 | tf_op jit(solution)/shard_map/ppermute | solution.py:62
  52.0 17.4 %collective-permute-start.3 = (bf16[256,768]{1,0:T(8,128)(2,1)S(1)}, bf16[256,768]{1,0:T(8,128)(2,1)S(1)}, u32[]{:S(2)}, u32[]{:S(2)}) collective-permute-start(bf16[256,768]{1,0:T(8,128)(2,1)S(1)} %get-tuple-element.52), channel_id=1, source_target_pairs={{0,1},{1,0},{2,3},{3,2},{4,5},{5,4},{6,7},{7,6},{8,9},{9,8},{10,11... | collective-permute-start | bytes 1179656 | tf_op jit(solution)/shard_map/ppermute | solution.py:66
  59.0 12.1 %collective-permute-start.13 = (bf16[256,1024]{1,0:T(8,128)(2,1)S(1)}, bf16[256,1024]{1,0:T(8,128)(2,1)S(1)}, u32[]{:S(2)}, u32[]{:S(2)}) collective-permute-start(bf16[256,1024]{1,0:T(8,128)(2,1)S(1)} %constant_dynamic-update-slice_fusion.2), channel_id=1, source_target_pairs={{0,2},{2,0},{4,6},{6,4},{8,10},{10,8},{12,14},{14,12},{16,18},{18,... | collective-permute-start | bytes 1572872 | tf_op jit(solution)/shard_map/ppermute | solution.py:62
  60.6 15.5 %collective-permute-start.12 = (bf16[256,768]{1,0:T(8,128)(2,1)S(1)}, bf16[256,768]{1,0:T(8,128)(2,1)S(1)}, u32[]{:S(2)}, u32[]{:S(2)}) collective-permute-start(bf16[256,768]{1,0:T(8,128)(2,1)S(1)} %get-tuple-element.48), channel_id=1, source_target_pairs={{0,1},{1,0},{2,3},{3,2},{4,5},{5,4},{6,7},{7,6},{8,9},{9,8},{10,11... | collective-permute-start | bytes 1179656 | tf_op jit(solution)/shard_map/ppermute | solution.py:66
  69.3 2.5 %collective-permute-start.5 = (bf16[256,768]{1,0:T(8,128)(2,1)S(1)}, bf16[256,768]{1,0:T(8,128)(2,1)S(1)}, u32[]{:S(2)}, u32[]{:S(2)}) collective-permute-start(bf16[256,768]{1,0:T(8,128)(2,1)S(1)} %get-tuple-element.50), channel_id=1, source_target_pairs={{0,1},{1,0},{2,3},{3,2},{4,5},{5,4},{6,7},{7,6},{8,9},{9,8},{10,11... | collective-permute-start | bytes 1179656 | tf_op jit(solution)/shard_map/ppermute | solution.py:66
  71.7 2.2 %collective-permute-start.14 = (bf16[256,768]{1,0:T(8,128)(2,1)S(1)}, bf16[256,768]{1,0:T(8,128)(2,1)S(1)}, u32[]{:S(2)}, u32[]{:S(2)}) collective-permute-start(bf16[256,768]{1,0:T(8,128)(2,1)S(1)} %get-tuple-element.46), channel_id=1, source_target_pairs={{0,1},{1,0},{2,3},{3,2},{4,5},{5,4},{6,7},{7,6},{8,9},{9,8},{10,11... | collective-permute-start | bytes 1179656 | tf_op jit(solution)/shard_map/ppermute | solution.py:66
  72.4 14.4 %collective-permute-start.6 = (bf16[256,1024]{1,0:T(8,128)(2,1)S(1)}, bf16[256,1024]{1,0:T(8,128)(2,1)S(1)}, u32[]{:S(2)}, u32[]{:S(2)}) collective-permute-start(bf16[256,1024]{1,0:T(8,128)(2,1)S(1)} %convolution_convert_fusion.1), channel_id=1, source_target_pairs={{0,4},{2,6},{4,0},{6,2},{8,12},{10,14},{12,8},{14,10},{16,20},{18,... | collective-permute-start | bytes 1572872 | tf_op jit(solution)/shard_map/ppermute | solution.py:62
  74.5 14.4 %collective-permute-start.15 = (bf16[256,1024]{1,0:T(8,128)(2,1)S(1)}, bf16[256,1024]{1,0:T(8,128)(2,1)S(1)}, u32[]{:S(2)}, u32[]{:S(2)}) collective-permute-start(bf16[256,1024]{1,0:T(8,128)(2,1)S(1)} %convolution_convert_fusion), channel_id=1, source_target_pairs={{0,2},{2,0},{4,6},{6,4},{8,10},{10,8},{12,14},{14,12},{16,18},{18,... | collective-permute-start | bytes 1572872 | tf_op jit(solution)/shard_map/ppermute | solution.py:62
  87.2 8.0 %collective-permute-start.7 = (bf16[128,1024]{1,0:T(8,128)(2,1)S(1)}, bf16[128,1024]{1,0:T(8,128)(2,1)S(1)}, u32[]{:S(2)}, u32[]{:S(2)}) collective-permute-start(bf16[128,1024]{1,0:T(8,128)(2,1)S(1)} %slice.213), channel_id=1, source_target_pairs={{0,2},{2,0},{4,6},{6,4},{8,10},{10,8},{12,14},{14,12},{16,18},{18,... | collective-permute-start | bytes 786440 | tf_op jit(solution)/shard_map/ppermute | solution.py:62
  89.3 7.7 %collective-permute-start.16 = (bf16[128,1024]{1,0:T(8,128)(2,1)S(1)}, bf16[128,1024]{1,0:T(8,128)(2,1)S(1)}, u32[]{:S(2)}, u32[]{:S(2)}) collective-permute-start(bf16[128,1024]{1,0:T(8,128)(2,1)S(1)} %slice.212), channel_id=1, source_target_pairs={{0,4},{2,6},{4,0},{6,2},{8,12},{10,14},{12,8},{14,10},{16,20},{18,... | collective-permute-start | bytes 786440 | tf_op jit(solution)/shard_map/ppermute | solution.py:62
  95.3 5.9 %collective-permute-start.8 = (bf16[64,1024]{1,0:T(8,128)(2,1)S(1)}, bf16[64,1024]{1,0:T(8,128)(2,1)S(1)}, u32[]{:S(2)}, u32[]{:S(2)}) collective-permute-start(bf16[64,1024]{1,0:T(8,128)(2,1)S(1)} %slice.214), channel_id=1, source_target_pairs={{0,24},{2,26},{4,28},{6,30},{8,0},{10,2},{12,4},{14,6},{16,8},{18,... | collective-permute-start | bytes 393224 | tf_op jit(solution)/shard_map/ppermute | solution.py:62
  97.1 25.3 %copy-start.6 = (f32[2048]{0:T(1024)S(1)}, f32[2048]{0:T(1024)}, u32[]{:S(2)}) copy-start(f32[2048]{0:T(1024)} %param.38) | copy-start | bytes 24580
  97.1 10.4 %collective-permute-start.17 = (bf16[64,1024]{1,0:T(8,128)(2,1)S(1)}, bf16[64,1024]{1,0:T(8,128)(2,1)S(1)}, u32[]{:S(2)}, u32[]{:S(2)}) collective-permute-start(bf16[64,1024]{1,0:T(8,128)(2,1)S(1)} %get-tuple-element.32), channel_id=1, source_target_pairs={{0,16},{2,18},{4,20},{6,22},{8,24},{10,26},{12,28},{14,30},{16,0},... | collective-permute-start | bytes 393224 | tf_op jit(solution)/shard_map/ppermute | solution.py:62
  97.2 10.3 %collective-permute-start.18 = (bf16[64,1024]{1,0:T(8,128)(2,1)S(1)}, bf16[64,1024]{1,0:T(8,128)(2,1)S(1)}, u32[]{:S(2)}, u32[]{:S(2)}) collective-permute-start(bf16[64,1024]{1,0:T(8,128)(2,1)S(1)} %get-tuple-element.33), channel_id=1, source_target_pairs={{0,8},{2,10},{4,12},{6,14},{8,16},{10,18},{12,20},{14,22},{16,24},... | collective-permute-start | bytes 393224 | tf_op jit(solution)/shard_map/ppermute | solution.py:62
  108.9 12.6 %all-to-all-start = ((f32[32,8,128]{2,1,0:T(8,128)}), f32[32,8,128]{2,1,0:T(8,128)S(1)}, u32[]{:S(2)}, u32[]{:S(2)}) async-start(f32[32,8,128]{2,1,0:T(8,128)} %broadcast_in_dim.86), calls=%async_computation | async-start | bytes 262144 | tf_op jit(solution)/shard_map/all_to_all | solution.py:71
  122.4 20.9 %copy-start.1 = (bf16[2048,512]{1,0:T(8,128)(2,1)S(1)}, bf16[2048,512]{1,0:T(8,128)(2,1)}, u32[]{:S(2)}) copy-start(bf16[2048,512]{1,0:T(8,128)(2,1)} %param.25) | copy-start | bytes 6291460
  (8 other events, 18.6 us)

commit v2 on v0

v2 whole, which is shorter than its diff:
```python
import jax
import jax.numpy as jnp
import numpy as np
from jax import lax
from jax.experimental import pallas as pl
from jax.experimental.pallas import tpu as pltpu
from jax.sharding import PartitionSpec as P


HEAD_DIM = 128


EPS = 1e-06
ROPE_BASE = 1000000.0
NEG = -1e30
WEIGHT = 20000000000
VMEM_SPEC = pl.BlockSpec(memory_space=pltpu.VMEM)
LOG2E = 1.4426950408889634
SHIFT = 4.0
QUERY_PARTS, CACHE_PARTS, OUT_PARTS = 4, 4, 4


def sizes_of(count):
    if count == 16:
        return (4, 2, 2)
    side = round(count ** (1 / 3))
    if side**3 == count:
        return (side, side, side)
    return (count, 1, 1)


def send(rows, count, steps):
    sizes = sizes_of(count)
    pairs = []
    for i in range(count):
        target, left = 0, i
        places = []
        for size in reversed(sizes):
            places.append(left % size)
            left //= size
        for place, size, step in zip(reversed(places), sizes, steps):
            target = target * size + (place + step) % size
        pairs.append((i, target))
    return lax.ppermute(rows, "req", pairs)


def along(count, digit):
    steps = []
    for step in range(1, sizes_of(count)[digit]):
        one = [0, 0, 0]
        one[digit] = step
        steps.append(tuple(one))
    return steps


def across(count):
    return [(0, b[1], c[2]) for b in along(count, 1) for c in along(count, 2)]


def add_steps(one, two):
    return tuple(a + b for a, b in zip(one, two))


def slot_behind(slot, count, steps):
    result, stride = 0, 1
    for size, step in zip(reversed(sizes_of(count)), reversed(steps)):
        result = result + lax.rem(lax.div(slot, stride) + size - step % size, size) * stride
        stride *= size
    return result


def back(steps):
    return tuple(-step for step in steps)


def other_core(rows):
    return lax.ppermute(rows, "head", [(0, 1), (1, 0)])


def to_all(block, names):
    count = lax.axis_size(names)
    return lax.all_to_all(jnp.broadcast_to(block[None], (count,) + block.shape), names, 0, 0, tiled=True)


def kernel_call(body, outs, flops, name, *operands, gates=()):
    def run(*refs):
        body(*refs[: len(operands)], *refs[len(operands) + len(gates) :])

    result = pl.pallas_call(
        run,
        out_shape=tuple(pltpu.VMEM(shape, dtype) for shape, dtype in outs),
        in_specs=[VMEM_SPEC] * len(operands) + [pl.BlockSpec(memory_space=pl.ANY)] * len(gates),
        out_specs=(VMEM_SPEC,) * len(outs),
        compiler_params=pltpu.CompilerParams(vmem_limit_bytes=20 * 1024 * 1024),
        cost_estimate=pl.CostEstimate(flops=flops, bytes_accessed=1000000, transcendentals=0),
        name=name,
    )(*operands, *gates)
    return result


def attention_kernel(
    lengths_any,
    requests_any,
    hidden_any,
    attn_gain_any,
    query_gain_any,
    key_gain_any,
    frequency_any,
    w_query_any,
    w_key_any,
    w_value_any,
    cache_keys_any,
    cache_values_any,
    w_out_any,
    own_out,
    send_out,
    lengths,
    requests,
    hidden,
    attn_gain,
    query_gain,
    key_gain,
    frequency,
    w_query,
    w_key,
    w_value,
    cache_keys,
    cache_values,
    w_out,
    sems,
):
    copies = []

    def fetch(source, target, parts):
        rows = target.shape[0] // parts
        group = []
        for i in range(parts):
            copy = pltpu.make_async_copy(
                source.at[pl.ds(i * rows, rows)], target.at[pl.ds(i * rows, rows)], sems.at[len(copies)]
            )
            copy.start()
            copies.append(copy)
            group.append(copy)
        return group

    small_copies = fetch(hidden_any, hidden, 1) + fetch(requests_any, requests, 1)
    small_copies += fetch(lengths_any, lengths, 1) + fetch(frequency_any, frequency, 1)
    small_copies += fetch(attn_gain_any, attn_gain, 1) + fetch(query_gain_any, query_gain, 1)
    small_copies += fetch(key_gain_any, key_gain, 1)
    query_copies = fetch(w_query_any, w_query, QUERY_PARTS)
    key_copies = fetch(w_key_any, w_key, 2)
    value_copies = fetch(w_value_any, w_value, 2)
    cached_key_copies = fetch(cache_keys_any.at[0], cache_keys, CACHE_PARTS)
    cached_value_copies = fetch(cache_values_any.at[0], cache_values, CACHE_PARTS)
    out_copies = fetch(w_out_any, w_out, OUT_PARTS)

    row_count, width = hidden.shape
    query_heads = w_query.shape[1] // HEAD_DIM
    value_heads = w_key.shape[1] // HEAD_DIM
    group = query_heads // value_heads
    span = cache_keys.shape[0]
    for copy in small_copies:
        copy.wait()
    cache_len = lengths[requests[lax.axis_index("req")]]

    row = lax.broadcasted_iota(jnp.int32, (row_count, HEAD_DIM), 0)
    lane = lax.broadcasted_iota(jnp.int32, (row_count, HEAD_DIM), 1)
    angles = (row + cache_len).astype(jnp.float32) * frequency[...]
    cosine = jnp.cos(angles)
    sine = jnp.where(lane < HEAD_DIM // 2, -jnp.sin(angles), jnp.sin(angles))

    def turned(heads, gain):
        scale = lax.rsqrt(jnp.mean(heads * heads, axis=-1, keepdims=True) + EPS)
        heads = heads * scale * gain
        return (heads * cosine + pltpu.roll(heads, HEAD_DIM // 2, 1) * sine).astype(jnp.bfloat16)

    tokens = hidden[...].astype(jnp.float32)
    scale = lax.rsqrt(jnp.mean(tokens * tokens, axis=-1, keepdims=True) + EPS)
    normed = (tokens * scale * attn_gain[...]).astype(jnp.bfloat16)

    def project(weight, group_copies):
        rows = width // len(group_copies)
        total = None
        for i, copy in enumerate(group_copies):
            copy.wait()
            part = jnp.dot(
                normed[:, i * rows : (i + 1) * rows],
                weight[i * rows : (i + 1) * rows, :],
                preferred_element_type=jnp.float32,
            )
            total = part if total is None else total + part
        return total

    def head(field, h):
        return field[:, h * HEAD_DIM : (h + 1) * HEAD_DIM]

    projected = project(w_query, query_copies)
    queries = [turned(head(projected, h), query_gain[...]) for h in range(query_heads)]
    queries = [jnp.concatenate(queries[k * group : (k + 1) * group], axis=0) for k in range(value_heads)]
    projected = project(w_key, key_copies)
    keys_new = [turned(head(projected, k), key_gain[...]) for k in range(value_heads)]
    values_new = project(w_value, value_copies).astype(jnp.bfloat16)

    factor = HEAD_DIM**-0.5 * LOG2E
    contract = (((1,), (1,)), ((), ()))
    totals, blended = [], []
    query_row = lax.broadcasted_iota(jnp.int32, (group * row_count, row_count), 0) % row_count
    column = lax.broadcasted_iota(jnp.int32, (group * row_count, row_count), 1)
    causal = jnp.where(query_row >= column, -SHIFT, NEG)
    for k in range(value_heads):
        scores = lax.dot_general(queries[k], keys_new[k], contract, preferred_element_type=jnp.float32)
        weights = jnp.exp2(scores * factor + causal)
        totals.append(jnp.sum(weights, axis=-1, keepdims=True))
        blended.append(
            jnp.dot(weights.astype(jnp.bfloat16), head(values_new, k), preferred_element_type=jnp.float32)
        )
    rows = span // CACHE_PARTS
    place_in_cache = lax.broadcasted_iota(jnp.int32, (1, rows), 1)
    for i in range(CACHE_PARTS):
        cached_key_copies[i].wait()
        stored = jnp.where(place_in_cache + i * rows < cache_len, -SHIFT, NEG)
        part = []
        for k in range(value_heads):
            keys = cache_keys[i * rows : (i + 1) * rows, k * HEAD_DIM : (k + 1) * HEAD_DIM]
            scores = lax.dot_general(queries[k], keys, contract, preferred_element_type=jnp.float32)
            weights = jnp.exp2(scores * factor + stored)
            totals[k] = totals[k] + jnp.sum(weights, axis=-1, keepdims=True)
            part.append(weights.astype(jnp.bfloat16))
        cached_value_copies[i].wait()
        for k in range(value_heads):
            values = cache_values[i * rows : (i + 1) * rows, k * HEAD_DIM : (k + 1) * HEAD_DIM]
            blended[k] = blended[k] + jnp.dot(part[k], values, preferred_element_type=jnp.float32)
    attended = []
    for k in range(value_heads):
        result = (blended[k] / totals[k]).astype(jnp.bfloat16)
        attended += [result[g * row_count : (g + 1) * row_count] for g in range(group)]
    attended = jnp.concatenate(attended, axis=1)
    for copy in out_copies:
        copy.wait()
    projected = jnp.dot(attended, w_out[...], preferred_element_type=jnp.float32)
    own_out[...] = tokens + projected
    send_out[...] = projected.astype(jnp.bfloat16)


def attention_rows(
    hidden_in, attn_gain, w_query, w_key, w_value, query_gain, key_gain, w_out,
    cache_keys, cache_values, cache_lengths, slot_request,
):
    half = HEAD_DIM // 2
    frequency = ROPE_BASE ** (-2.0 * np.arange(half, dtype=np.float64) / HEAD_DIM)
    frequency = jnp.asarray(np.tile(frequency, 2)[None, :], jnp.float32)
    vmem = pl.BlockSpec(memory_space=pltpu.VMEM)
    anywhere = pl.BlockSpec(memory_space=pltpu.HBM)
    rows, width = hidden_in.shape
    return pl.pallas_call(
        attention_kernel,
        out_shape=(pltpu.VMEM((rows, width), jnp.float32), pltpu.VMEM((rows, width), jnp.bfloat16)),
        in_specs=[anywhere] * 13,
        out_specs=(vmem, vmem),
        scratch_shapes=[
            pltpu.SMEM(cache_lengths.shape, jnp.int32),
            pltpu.SMEM(slot_request.shape, jnp.int32),
            pltpu.VMEM(hidden_in.shape, jnp.bfloat16),
            pltpu.VMEM((1, width), jnp.float32),
            pltpu.VMEM((1, HEAD_DIM), jnp.float32),
            pltpu.VMEM((1, HEAD_DIM), jnp.float32),
            pltpu.VMEM((1, HEAD_DIM), jnp.float32),
            pltpu.VMEM(w_query.shape, jnp.bfloat16),
            pltpu.VMEM(w_key.shape, jnp.bfloat16),
            pltpu.VMEM(w_value.shape, jnp.bfloat16),
            pltpu.VMEM(cache_keys.shape[1:], jnp.bfloat16),
            pltpu.VMEM(cache_values.shape[1:], jnp.bfloat16),
            pltpu.VMEM(w_out.shape, jnp.bfloat16),
            pltpu.SemaphoreType.DMA((QUERY_PARTS + 11 + 2 * CACHE_PARTS + OUT_PARTS,)),
        ],
        compiler_params=pltpu.CompilerParams(vmem_limit_bytes=40 * 1024 * 1024),
        cost_estimate=pl.CostEstimate(flops=1400000000, bytes_accessed=17500000, transcendentals=1100000),
        name="attention_rows",
    )(*[
        pltpu.with_memory_space_constraint(operand, pltpu.HBM)
        for operand in (
            cache_lengths, slot_request, hidden_in, attn_gain[None, :], query_gain[None, :],
            key_gain[None, :], frequency, w_query, w_key, w_value, cache_keys, cache_values, w_out,
        )
    ])


def mix_rows(own, other, mlp_gain):
    rows, half = own.shape[0], mlp_gain.shape[1]

    def body(own, other, gain, mixed_out, residual_out):
        total = own[...] + other[...].astype(jnp.float32)
        scale = lax.rsqrt(jnp.mean(total * total, axis=1, keepdims=True) + EPS)
        for part in range(2):

            @pl.when(lax.axis_index("head") == part)
            def _():
                kept = total[:, part * half : (part + 1) * half]
                residual_out[...] = kept
                mixed_out[...] = (kept * scale * gain[...]).astype(jnp.bfloat16)

    outs = [((rows, half), jnp.bfloat16), ((rows, half), jnp.float32)]
    return kernel_call(body, outs, 1000000, "mix_rows", own, other, mlp_gain)


def stacked(blocks, name, gates=(), flops=1000000):
    rows, width = sum(block.shape[0] for block in blocks), blocks[0].shape[1]

    def body(*refs):
        start = 0
        for ref in refs[:-1]:
            refs[-1][start : start + ref.shape[0]] = ref[...]
            start += ref.shape[0]

    return kernel_call(body, [((rows, width), jnp.bfloat16)], flops, name, *blocks, gates=gates)[0]


def gate_up(blocks, w_gate, w_up, name, gates=()):
    rows, units = sum(block.shape[0] for block in blocks), w_gate.shape[1]

    def body(*refs):
        start = 0
        w_gate, w_up, own_out, send_out = refs[-4:]
        for ref in refs[:-4]:
            for i, weight in enumerate((w_gate, w_up)):
                part = jnp.dot(ref[...], weight[...], preferred_element_type=jnp.float32)
                own_out[i, start : start + ref.shape[0]] = part
                send_out[i, start : start + ref.shape[0]] = part.astype(jnp.bfloat16)
            start += ref.shape[0]

    outs = [((2, rows, units), jnp.float32), ((2, rows, units), jnp.bfloat16)]
    flops = 4 * rows * w_gate.size
    return kernel_call(body, outs, flops, name, *blocks, w_gate, w_up, gates=gates)


def down_parts(own, other, w_down, outs, name, gates=()):
    rows = own.shape[1]

    def body(own, other, w_down, *out_refs):
        gate = own[0] + other[0].astype(jnp.float32)
        up = own[1] + other[1].astype(jnp.float32)
        active = (gate / (1.0 + jnp.exp(-gate)) * up).astype(jnp.bfloat16)
        start = 0
        for ref in out_refs:
            stop = start + ref.shape[0]
            part = jnp.dot(active[start:stop], w_down[...], preferred_element_type=jnp.float32)
            ref[...] = part.astype(ref.dtype)
            start = stop

    return kernel_call(body, outs, 2 * rows * w_down.size, name, own, other, w_down, gates=gates)


def summed(terms, outs, name, gates=(), flops=1000000):
    def body(*refs):
        total = None
        for ref in refs[: len(terms)]:
            part = ref[...].astype(jnp.float32)
            total = part if total is None else total + part
        for ref, (start, shape, dtype) in zip(refs[len(terms) :], outs):
            ref[...] = total[start : start + shape[0]].astype(dtype)

    plain = [(shape, dtype) for _, shape, dtype in outs]
    return kernel_call(body, plain, flops, name, *terms, gates=gates)


def on_device(
    hidden_in,
    attn_gain,
    w_query,
    w_key,
    w_value,
    query_gain,
    key_gain,
    w_out,
    cache_keys,
    cache_values,
    cache_lengths,
    slot_request,
    mlp_gain,
    w_gate,
    w_up,
    w_down,
    final_gain,
    w_vocab,
):
    row_count = hidden_in.shape[0]
    half_width = mlp_gain.shape[0]
    count = lax.axis_size("req")
    own, sent = attention_rows(
        hidden_in, attn_gain, w_query, w_key, w_value, query_gain, key_gain, w_out,
        cache_keys, cache_values, cache_lengths, slot_request,
    )
    mixed, residual = mix_rows(own, other_core(sent), mlp_gain[None, :])
    shape = mixed.shape
    outer, middle, inner, diagonal = along(count, 0), along(count, 1), along(count, 2), across(count)

    columns = [send(mixed, count, steps) for steps in outer]
    corners = [send(mixed, count, steps) for steps in diagonal]
    column = stacked([mixed] + columns, "column", gates=corners)
    corner = stacked(corners, "corner") if len(corners) > 1 else corners[0] if corners else None
    far = [send(column, count, steps) for steps in inner + middle]
    far_corners = [send(corner, count, steps) for steps in outer] if corners else []

    near_own, near_sent = gate_up([column] + ([corner] if corners else []), w_gate, w_up, "near_gate_up")
    near_rows = near_own.shape[1]
    near_outs = [(column.shape, jnp.float32)] + ([(corner.shape, jnp.float32)] if corners else [])
    near = down_parts(near_own, other_core(near_sent), w_down, near_outs, "near_down")

    far_corner = []
    if corners:
        far_corner = [stacked(far_corners, "far_corner", gates=(near_own,), flops=WEIGHT)]
        far = lax.optimization_barrier((far, far_corner))[0]

    at_home = (0, 0, 0)
    places = [at_home] + outer + diagonal
    for steps in inner + middle:
        places += [add_steps(steps, line) for line in [at_home] + outer]
    for steps in outer if corners else []:
        places += [add_steps(steps, turn) for turn in diagonal]
    last_shape = (count, half_width)
    blocks = [column] + ([corner] if corners else []) + far + far_corner

    def request_of(steps, requests):
        slots = lax.broadcasted_iota(jnp.int32, (1, count), 1)
        slot = slot_behind(lax.axis_index("req"), count, steps)
        return jnp.sum(jnp.where(slots == slot, requests[...], 0), axis=1, keepdims=True)

    def last_gate_up(*refs):
        requests, w_gate, w_up, own_out, send_out = refs[-5:]
        order = lax.broadcasted_iota(jnp.int32, (count, 1), 0)
        rows, place = jnp.zeros(last_shape, jnp.float32), 0
        for ref in refs[:-5]:
            for stop in range(row_count, ref.shape[0] + 1, row_count):
                last = ref[stop - 16 : stop].astype(jnp.float32)[15:]
                rows = rows + jnp.where(order == request_of(places[place], requests), last, 0.0)
                place += 1
        rows = rows.astype(jnp.bfloat16)
        for i, weight in enumerate((w_gate, w_up)):
            part = jnp.dot(rows, weight[...], preferred_element_type=jnp.float32)
            own_out[i] = part
            send_out[i] = part.astype(jnp.bfloat16)

    units = w_gate.shape[1]
    last_own, last_sent = kernel_call(
        last_gate_up, [((2, count, units), jnp.float32), ((2, count, units), jnp.bfloat16)], 100000000,
        "last_gate_up", *blocks, slot_request[None, :], w_gate, w_up,
    )
    def last_down(own, other, w_down, residual, requests, kept_out, sent_out):
        gate = own[0] + other[0].astype(jnp.float32)
        up = own[1] + other[1].astype(jnp.float32)
        active = (gate / (1.0 + jnp.exp(-gate)) * up).astype(jnp.bfloat16)
        order = lax.broadcasted_iota(jnp.int32, (count, 1), 0)
        total = jnp.dot(active, w_down[...], preferred_element_type=jnp.float32)
        total = total + jnp.where(order == request_of(at_home, requests), residual[row_count - 1 :, :], 0.0)
        kept_out[...] = total
        sent_out[...] = total.astype(jnp.bfloat16)

    last_outs = [(last_shape, jnp.float32), (last_shape, jnp.bfloat16)]
    last_kept, last_sent = kernel_call(
        last_down, last_outs, 100000000, "last_down",
        last_own, other_core(last_sent), w_down, residual, slot_request[None, :],
    )
    far_own, far_sent = gate_up(far + far_corner, w_gate, w_up, "far_gate_up", gates=(near[0], last_kept))
    last_plane = [send(last_sent, count, steps) for steps in inner + middle + diagonal]
    last_outs = [(0, last_shape, jnp.float32), (0, last_shape, jnp.bfloat16)]
    far_outs = [(column.shape, jnp.bfloat16) for _ in far] + [(corner.shape, jnp.bfloat16) for _ in far_corners]
    parts = down_parts(far_own, other_core(far_sent), w_down, far_outs, "far_down")
    last_kept, last_sent = summed([last_kept] + last_plane, last_outs, "last_plane", gates=(parts[0],))
    last_lines = [send(last_sent, count, steps) for steps in outer]
    half_rows = summed([last_kept] + last_lines, [(0, last_shape, jnp.float32)], "last_line")[0]
    near_parts, far_parts = parts[: len(far)], parts[len(far) :]
    near_parts = lax.optimization_barrier((near_parts, last_kept))[0]
    half_rows, far_parts = lax.optimization_barrier((half_rows, far_parts))

    returned = [send(part, count, back(steps)) for part, steps in zip(near_parts, inner + middle)]
    returned_corners = [send(part, count, back(steps)) for part, steps in zip(far_parts, outer)]

    other_rows = other_core(half_rows)
    final_rows = jnp.where(
        lax.axis_index("head") == 0,
        jnp.concatenate([half_rows, other_rows], axis=1),
        jnp.concatenate([other_rows, half_rows], axis=1),
    )
    scale = lax.rsqrt(jnp.mean(final_rows * final_rows, axis=-1, keepdims=True) + EPS)
    final_rows = (final_rows * scale * final_gain).astype(jnp.bfloat16)
    logits = jnp.dot(final_rows, w_vocab, preferred_element_type=jnp.float32)
    own_max = jnp.max(logits, axis=1)
    own_total = jnp.sum(jnp.exp(logits - own_max[:, None]), axis=1)
    stats = jnp.zeros((8, 128), jnp.float32).at[0, :count].set(own_max).at[1, :count].set(own_total)
    corner_sent = []
    if corners:
        corner_outs = [(row_count * i, shape, jnp.bfloat16) for i in range(len(corners))]
        corner_pieces = summed([near[1]] + returned_corners, corner_outs, "corner_sum", flops=WEIGHT)
        corner_sent = [send(part, count, back(steps)) for part, steps in zip(corner_pieces, diagonal)]
        returned = lax.optimization_barrier((returned, corner_pieces))[0]

    column_outs = [(0, shape, jnp.float32)]
    column_outs += [(row_count * (i + 1), shape, jnp.bfloat16) for i in range(len(outer))]
    pieces = summed([near[0]] + returned, column_outs, "column_sum", gates=(stats,))
    final = [residual, pieces[0]] + corner_sent + [
        send(part, count, back(steps)) for part, steps in zip(pieces[1:], outer)
    ]
    hidden_out = final[0]
    for part in final[1:]:
        hidden_out = hidden_out + part.astype(jnp.float32)
    hidden_out = hidden_out.astype(jnp.bfloat16)
    everyone = to_all(lax.optimization_barrier((stats, pieces))[0], ("req", "head"))
    row_max = jnp.max(everyone[:, 0, :count], axis=0)
    row_total = jnp.sum(everyone[:, 1, :count] * jnp.exp(everyone[:, 0, :count] - row_max[None, :]), axis=0)
    log_probs = logits - (row_max + jnp.log(row_total))[:, None]

    return (hidden_out, log_probs)


def solution(mesh):
    in_specs = (
        P("req", None),
        P(),
        P(None, "head"),
        P(None, "head"),
        P(None, "head"),
        P(),
        P(),
        P("head", None),
        P("req", None, "head"),
        P("req", None, "head"),
        P(),
        P(),
        P("head"),
        P("head", "req"),
        P("head", "req"),
        P("req", "head"),
        P(),
        P(None, ("req", "head")),
    )
    out_specs = (P("req", "head"), P(None, ("req", "head")))
    return jax.shard_map(
        on_device, mesh=mesh, in_specs=in_specs, out_specs=out_specs, check_vma=False
    )
```

time: 382 us -> 105 us (0.27)
  waiting for transfers between devices: 187 us -> 22.1 us
  blocking collectives: 121 us -> 0 us
  starting transfers between devices: 0.16 us -> 49 us
  matrix products: 32.2 us -> 10.1 us
  between operations: 16.1 us -> 0.95 us
  Pallas kernels: 0 us -> 14.7 us
  local copies, waits for them, and re-layouts: 13.1 us -> 2.78 us
  other arithmetic: 11.8 us -> 4.84 us
    reduce_scatter x2 -> x0, waiting for transfers between devices: 106 us -> none  [the longest x1 95.7 us: on_device(): lax.psum_scatter(jnp.dot(active, w_down, preferred_element_type=jnp.float...]
    all_gather x1 -> x0, waiting for transfers between devices: 62 us -> none  [on_device(): lax.all_gather(mixed_rows, 'req', axis=0, tiled=True)]
    ppermute x0 -> x29, starting transfers between devices: none -> 43.9 us  [the longest x24 42.6 us: send(): return lax.ppermute(rows, 'req', pairs)]
    psum x2 -> x0, blocking collectives: 43.7 us -> none  [the longest x1 41.2 us: on_device(): lax.psum(jnp.sum(jnp.exp(logits - row_max[:, None]), axis=1), ('req', 'he...]
    all_gather x1 -> x0, blocking collectives: 40.2 us -> none  [on_device(): lax.all_gather(last_row, ('req', 'head'), axis=1, tiled=True).reshape(-1, D)]
    pmax x1 -> x0, blocking collectives: 36.9 us -> none  [on_device(): row_max = lax.pmax(jnp.max(logits, axis=1), ('req', 'head'))]
    dot_general x10 -> x0, matrix products: 22.9 us -> none  [the longest x1 4.94 us: on_device(): jnp.dot(lax.all_gather(mixed_rows, 'req', axis=0, tiled=True), paired, pr...]
    ppermute x0 -> x29, waiting for transfers between devices: none -> 22.1 us  [the longest x24 20.9 us: send(): return lax.ppermute(rows, 'req', pairs)]
  transfers between devices with their start and end apart: 4 -> 30, of which waited for: 4 -> 10; matrix products, arithmetic and copies ran while one was open for 0% -> 13% of each run, Pallas kernels for 0% -> 4%
where the time goes in v2:
time: 105 us; the launch traced here: 104 us
  starting transfers between devices  49 us (47%)
  waiting for transfers between devices  22.1 us (21%)
  Pallas kernels  14.7 us (14%)
  matrix products  10.1 us (10%)
  other arithmetic  4.84 us (5%)
  local copies, waits for them, and re-layouts  2.78 us (3%)
    ppermute x24, starting transfers between devices, send(): return lax.ppermute(rows, 'req', pairs)  42.6 us
    ppermute x24, waiting for transfers between devices, send(): return lax.ppermute(rows, 'req', pairs)  20.9 us
    dot_general x1, matrix products, on_device(): logits = jnp.dot(final_rows, w_vocab, preferred_element_type=jnp.float32)  10.1 us
    pallas_call x1, Pallas kernels, attention_rows(): pl.pallas_call(attention_kernel, out_shape=(pltpu.VMEM((rows, width), jnp...  8.25 us
    pallas_call x13, Pallas kernels, kernel_call(): pl.pallas_call(run, out_shape=tuple((pltpu.VMEM(shape, dtype) for shape,...  6.46 us
    all_to_all x1, starting transfers between devices, to_all(): lax.all_to_all(jnp.broadcast_to(block[None], (count,) + block.shape), nam...  5.14 us
  transfers between devices with their start and end apart: 30, of which 10 were waited for; matrix products, arithmetic and copies ran while one was open for 13% of the time, Pallas kernels for 4%

profile of v2, /device:TPU:0, one launch (start us, length us, event | category | flops | bytes accessed | tf_op | source)
XLA Modules:
  0.0 104.5 jit_solution(14893647808954699315)
XLA Ops:
  0.6 8.3 %attention_rows.1 = (f32[64,2048]{1,0:T(8,128)S(1)}, bf16[64,2048]{1,0:T(8,128)(2,1)S(1)}) custom-call(s32[16]{0:T(128)} %lengths_any.1, s32[16]{0:T(128)} %requests_any.1, bf16[64,2048]{1,0:T(8,128)(2,1)} %hidden_any.1, f32[1,2048]{1,0:T(1,128)} %bitcast.18, f32[1,128]{1,0:T(1,128)} %bitcast.21, f32[1,128]{1,0:T(1,128)} %bitcast.22, ...), custom_call_target="tpu_custom_call" | custom-call | flops 1400000000 | bytes 17500000 | tf_op jit(solution)/shard_map/attention_rows/pallas_call | solution.py:255
  10.8 3.9 %collective-permute-start.4 = (bf16[64,1024]{1,0:T(8,128)(2,1)S(1)}, bf16[64,1024]{1,0:T(8,128)(2,1)S(1)}, u32[]{:S(2)}, u32[]{:S(2)}) collective-permute-start(bf16[64,1024]{1,0:T(8,128)(2,1)S(1)} %get-tuple-element.65.refs_0_), channel_id=1, source_target_pairs={{0,6},{2,4},{4,2},{6,0},{8,14},{10,12},{12,10},{14,8},{16,22},{18,... | collective-permute-start | bytes 393224 | tf_op jit(solution)/shard_map/ppermute | solution.py:44
  14.7 1.6 %collective-permute-start.1 = (bf16[64,1024]{1,0:T(8,128)(2,1)S(1)}, bf16[64,1024]{1,0:T(8,128)(2,1)S(1)}, u32[]{:S(2)}, u32[]{:S(2)}) collective-permute-start(bf16[64,1024]{1,0:T(8,128)(2,1)S(1)} %get-tuple-element.65.refs_0_), channel_id=1, source_target_pairs={{0,8},{2,10},{4,12},{6,14},{8,16},{10,18},{12,20},{14,22},{16,24},... | collective-permute-start | bytes 393224 | tf_op jit(solution)/shard_map/ppermute | solution.py:44
  16.3 2.6 %collective-permute-start.2 = (bf16[64,1024]{1,0:T(8,128)(2,1)S(1)}, bf16[64,1024]{1,0:T(8,128)(2,1)S(1)}, u32[]{:S(2)}, u32[]{:S(2)}) collective-permute-start(bf16[64,1024]{1,0:T(8,128)(2,1)S(1)} %get-tuple-element.65.refs_0_), channel_id=1, source_target_pairs={{0,16},{2,18},{4,20},{6,22},{8,24},{10,26},{12,28},{14,30},{16,0},... | collective-permute-start | bytes 393224 | tf_op jit(solution)/shard_map/ppermute | solution.py:44
  18.9 1.3 %collective-permute-start.3 = (bf16[64,1024]{1,0:T(8,128)(2,1)S(1)}, bf16[64,1024]{1,0:T(8,128)(2,1)S(1)}, u32[]{:S(2)}, u32[]{:S(2)}) collective-permute-start(bf16[64,1024]{1,0:T(8,128)(2,1)S(1)} %get-tuple-element.65.refs_0_), channel_id=1, source_target_pairs={{0,24},{2,26},{4,28},{6,30},{8,0},{10,2},{12,4},{14,6},{16,8},{18,... | collective-permute-start | bytes 393224 | tf_op jit(solution)/shard_map/ppermute | solution.py:44
  20.2 2.1 %collective-permute-start.10 = (bf16[64,1024]{1,0:T(8,128)(2,1)S(1)}, bf16[64,1024]{1,0:T(8,128)(2,1)S(1)}, u32[]{:S(2)}, u32[]{:S(2)}) collective-permute-start(bf16[64,1024]{1,0:T(8,128)(2,1)S(1)} %collective-permute-done.4.refs_4_.refs_1_), channel_id=1, source_target_pairs={{0,24},{2,26},{4,28},{6,30},{8,0},{10,2},{12,4},{14,6},{16,8},{18,... | collective-permute-start | bytes 393224 | tf_op jit(solution)/shard_map/ppermute | solution.py:44
  23.0 9.2 %collective-permute-start.9 = (bf16[64,1024]{1,0:T(8,128)(2,1)S(1)}, bf16[64,1024]{1,0:T(8,128)(2,1)S(1)}, u32[]{:S(2)}, u32[]{:S(2)}) collective-permute-start(bf16[64,1024]{1,0:T(8,128)(2,1)S(1)} %collective-permute-done.4.refs_4_.refs_1_), channel_id=1, source_target_pairs={{0,16},{2,18},{4,20},{6,22},{8,24},{10,26},{12,28},{14,30},{16,0},... | collective-permute-start | bytes 393224 | tf_op jit(solution)/shard_map/ppermute | solution.py:44
  34.3 7.2 %collective-permute-done.9.refs_1_ = bf16[64,1024]{1,0:T(8,128)(2,1)S(1)} collective-permute-done((bf16[64,1024]{1,0:T(8,128)(2,1)S(1)}, bf16[64,1024]{1,0:T(8,128)(2,1)S(1)}, u32[]{:S(2)}, u32[]{:S(2)}) %collective-permute-start.9) | collective-permute-done | bytes 131104 | tf_op jit(solution)/shard_map/ppermute | solution.py:44
  44.2 1.7 %far_gate_up.1 = (f32[2,704,384]{2,1,0:T(8,128)S(1)}, bf16[2,704,384]{2,1,0:T(8,128)(2,1)S(1)}) custom-call(bf16[256,1024]{1,0:T(8,128)(2,1)S(1)} %collective-permute-done.6.refs_2_.refs_0_, bf16[256,1024]{1,0:T(8,128)(2,1)S(1)} %collective-permute-done.7.refs_3_.refs_1_, bf16[192,1024]{1,0:T(8,128)(2,1)S(1)} %far_corner.1.refs_4_.refs_2_, ...), custom_call_target="tpu_custom_call" | custom-call | flops 1107296256 | bytes 1000000 | tf_op jit(solution)/shard_map/far_gate_up/pallas_call | solution.py:89
  46.4 1.3 %collective-permute-start.13 = (bf16[16,1024]{1,0:T(8,128)(2,1)S(1)}, bf16[16,1024]{1,0:T(8,128)(2,1)S(1)}, u32[]{:S(2)}, u32[]{:S(2)}) collective-permute-start(bf16[16,1024]{1,0:T(8,128)(2,1)S(1)} %get-tuple-element.78), channel_id=1, source_target_pairs={{0,2},{2,0},{4,6},{6,4},{8,10},{10,8},{12,14},{14,12},{16,18},{18,... | collective-permute-start | bytes 98312 | tf_op jit(solution)/shard_map/ppermute | solution.py:44
  48.2 1.7 %collective-permute-start.15 = (bf16[16,1024]{1,0:T(8,128)(2,1)S(1)}, bf16[16,1024]{1,0:T(8,128)(2,1)S(1)}, u32[]{:S(2)}, u32[]{:S(2)}) collective-permute-start(bf16[16,1024]{1,0:T(8,128)(2,1)S(1)} %get-tuple-element.78), channel_id=1, source_target_pairs={{0,6},{2,4},{4,2},{6,0},{8,14},{10,12},{12,10},{14,8},{16,22},{18,... | collective-permute-start | bytes 98312 | tf_op jit(solution)/shard_map/ppermute | solution.py:44
  53.0 4.1 %collective-permute-start.18 = (bf16[16,1024]{1,0:T(8,128)(2,1)S(1)}, bf16[16,1024]{1,0:T(8,128)(2,1)S(1)}, u32[]{:S(2)}, u32[]{:S(2)}) collective-permute-start(bf16[16,1024]{1,0:T(8,128)(2,1)S(1)} %get-tuple-element.83), channel_id=1, source_target_pairs={{0,8},{2,10},{4,12},{6,14},{8,16},{10,18},{12,20},{14,22},{16,24},... | collective-permute-start | bytes 98312 | tf_op jit(solution)/shard_map/ppermute | solution.py:44
  57.1 2.5 %collective-permute-start.19 = (bf16[16,1024]{1,0:T(8,128)(2,1)S(1)}, bf16[16,1024]{1,0:T(8,128)(2,1)S(1)}, u32[]{:S(2)}, u32[]{:S(2)}) collective-permute-start(bf16[16,1024]{1,0:T(8,128)(2,1)S(1)} %get-tuple-element.83), channel_id=1, source_target_pairs={{0,16},{2,18},{4,20},{6,22},{8,24},{10,26},{12,28},{14,30},{16,0},... | collective-permute-start | bytes 98312 | tf_op jit(solution)/shard_map/ppermute | solution.py:44
  59.6 1.3 %collective-permute-done.18.refs_1_ = bf16[16,1024]{1,0:T(8,128)(2,1)S(1)} collective-permute-done((bf16[16,1024]{1,0:T(8,128)(2,1)S(1)}, bf16[16,1024]{1,0:T(8,128)(2,1)S(1)}, u32[]{:S(2)}, u32[]{:S(2)}) %collective-permute-start.18) | collective-permute-done | bytes 32800 | tf_op jit(solution)/shard_map/ppermute | solution.py:44
  62.0 1.6 %collective-permute-done.20.refs_3_ = bf16[16,1024]{1,0:T(8,128)(2,1)S(1)} collective-permute-done((bf16[16,1024]{1,0:T(8,128)(2,1)S(1)}, bf16[16,1024]{1,0:T(8,128)(2,1)S(1)}, u32[]{:S(2)}, u32[]{:S(2)}) %collective-permute-start.20) | collective-permute-done | bytes 32800 | tf_op jit(solution)/shard_map/ppermute | solution.py:44
  64.3 1.5 %collective-permute-start.17 = (bf16[256,1024]{1,0:T(8,128)(2,1)S(1)}, bf16[256,1024]{1,0:T(8,128)(2,1)S(1)}, u32[]{:S(2)}, u32[]{:S(2)}) collective-permute-start(bf16[256,1024]{1,0:T(8,128)(2,1)S(1)} %get-tuple-element.81), channel_id=1, source_target_pairs={{0,4},{2,6},{4,0},{6,2},{8,12},{10,14},{12,8},{14,10},{16,20},{18,... | collective-permute-start | bytes 1572872 | tf_op jit(solution)/shard_map/ppermute | solution.py:44
  65.8 2.1 %collective-permute-start.21 = (bf16[64,1024]{1,0:T(8,128)(2,1)}, bf16[64,1024]{1,0:T(8,128)(2,1)}, u32[]{:S(2)}, u32[]{:S(2)}) collective-permute-start(bf16[64,1024]{1,0:T(8,128)(2,1)} %copy-done.9), channel_id=1, source_target_pairs={{0,24},{2,26},{4,28},{6,30},{8,0},{10,2},{12,4},{14,6},{16,8},{18,... | collective-permute-start | bytes 393224 | tf_op jit(solution)/shard_map/ppermute | solution.py:44
  68.9 10.1 %fusion.6 = (f32[16]{0:T(128)S(1)}, f32[16,4748]{1,0:T(8,128)}) fusion(bf16[2048,4748]{0,1:T(8,128)(2,1)} %param.40, f32[16,1024]{1,0:T(8,128)S(1)} %last_line.1, f32[16,1024]{1,0:T(8,128)S(1)} %collective-permute-done.24, f32[2048]{0:T(1024)S(1)} %copy-done.10, f32[16]{0:T(128)S(1)} %add_rsqrt_fusion, pred[]{:T(512)S(6)} %eq.3), kind=kOutput, calls=%fused_computation.15 | convolution fusion | flops 311437504 | bytes 19891072 | tf_op jit(solution)/shard_map/dot_general | solution.py:486
  82.4 1.5 %collective-permute-start.25 = (bf16[64,1024]{1,0:T(8,128)(2,1)S(1)}, bf16[64,1024]{1,0:T(8,128)(2,1)}, u32[]{:S(2)}, u32[]{:S(2)}) collective-permute-start(bf16[64,1024]{1,0:T(8,128)(2,1)S(1)} %corner_sum.1), channel_id=1, source_target_pairs={{0,6},{2,4},{4,2},{6,0},{8,14},{10,12},{12,10},{14,8},{16,22},{18,... | collective-permute-start | bytes 393224 | tf_op jit(solution)/shard_map/ppermute | solution.py:44
  84.1 3.1 %collective-permute-start.26 = (bf16[64,1024]{1,0:T(8,128)(2,1)S(1)}, bf16[64,1024]{1,0:T(8,128)(2,1)S(1)}, u32[]{:S(2)}, u32[]{:S(2)}) collective-permute-start(bf16[64,1024]{1,0:T(8,128)(2,1)S(1)} %get-tuple-element.94), channel_id=1, source_target_pairs={{0,24},{2,26},{4,28},{6,30},{8,0},{10,2},{12,4},{14,6},{16,8},{18,... | collective-permute-start | bytes 393224 | tf_op jit(solution)/shard_map/ppermute | solution.py:44
  89.0 5.1 %all-to-all-start = ((f32[32,8,128]{2,1,0:T(8,128)}), f32[32,8,128]{2,1,0:T(8,128)S(1)}, u32[]{:S(2)}, u32[]{:S(2)}) async-start(f32[32,8,128]{2,1,0:T(8,128)} %broadcast_in_dim.33), calls=%async_computation | async-start | bytes 262144 | tf_op jit(solution)/shard_map/all_to_all | solution.py:82
  94.1 6.8 %collective-permute-done.27 = bf16[64,1024]{1,0:T(8,128)(2,1)S(1)} collective-permute-done((bf16[64,1024]{1,0:T(8,128)(2,1)S(1)}, bf16[64,1024]{1,0:T(8,128)(2,1)S(1)}, u32[]{:S(2)}, u32[]{:S(2)}) %collective-permute-start.27) | collective-permute-done | bytes 131104 | tf_op jit(solution)/shard_map/ppermute | solution.py:44
  101.0 1.7 %add_convert_fusion = bf16[64,1024]{1,0:T(8,128)(2,1)} fusion(bf16[64,1024]{1,0:T(8,128)(2,1)S(1)} %collective-permute-done.28, bf16[64,1024]{1,0:T(8,128)(2,1)S(1)} %collective-permute-done.27, bf16[64,1024]{1,0:T(8,128)(2,1)S(1)} %collective-permute-done.26, bf16[64,1024]{1,0:T(8,128)(2,1)} %collective-permute-done.25, ...), kind=kLoop, calls=%fused_computation.1 | loop fusion | flops 655360 | bytes 1179648 | tf_op jit(solution)/shard_map/convert_element_type | solution.py:506
  102.7 1.8 %broadcast_subtract_fusion = f32[16,4748]{1,0:T(8,128)} fusion(f32[16,4748]{1,0:T(8,128)} %get-tuple-element.101, f32[16]{0:T(128)S(1)} %log_add_fusion), kind=kLoop, calls=%fused_computation.2 | loop fusion | flops 75968 | bytes 607808 | tf_op jit(solution)/shard_map/sub | solution.py:510
  (85 shorter events, 19.5 us)
Async XLA Ops:
  10.8 9.4 %collective-permute-start.4 = (bf16[64,1024]{1,0:T(8,128)(2,1)S(1)}, bf16[64,1024]{1,0:T(8,128)(2,1)S(1)}, u32[]{:S(2)}, u32[]{:S(2)}) collective-permute-start(bf16[64,1024]{1,0:T(8,128)(2,1)S(1)} %get-tuple-element.65.refs_0_), channel_id=1, source_target_pairs={{0,6},{2,4},{4,2},{6,0},{8,14},{10,12},{12,10},{14,8},{16,22},{18,... | collective-permute-start | bytes 393224 | tf_op jit(solution)/shard_map/ppermute | solution.py:44
  14.7 8.3 %collective-permute-start.1 = (bf16[64,1024]{1,0:T(8,128)(2,1)S(1)}, bf16[64,1024]{1,0:T(8,128)(2,1)S(1)}, u32[]{:S(2)}, u32[]{:S(2)}) collective-permute-start(bf16[64,1024]{1,0:T(8,128)(2,1)S(1)} %get-tuple-element.65.refs_0_), channel_id=1, source_target_pairs={{0,8},{2,10},{4,12},{6,14},{8,16},{10,18},{12,20},{14,22},{16,24},... | collective-permute-start | bytes 393224 | tf_op jit(solution)/shard_map/ppermute | solution.py:44
  16.3 15.9 %collective-permute-start.2 = (bf16[64,1024]{1,0:T(8,128)(2,1)S(1)}, bf16[64,1024]{1,0:T(8,128)(2,1)S(1)}, u32[]{:S(2)}, u32[]{:S(2)}) collective-permute-start(bf16[64,1024]{1,0:T(8,128)(2,1)S(1)} %get-tuple-element.65.refs_0_), channel_id=1, source_target_pairs={{0,16},{2,18},{4,20},{6,22},{8,24},{10,26},{12,28},{14,30},{16,0},... | collective-permute-start | bytes 393224 | tf_op jit(solution)/shard_map/ppermute | solution.py:44
  18.9 13.3 %collective-permute-start.3 = (bf16[64,1024]{1,0:T(8,128)(2,1)S(1)}, bf16[64,1024]{1,0:T(8,128)(2,1)S(1)}, u32[]{:S(2)}, u32[]{:S(2)}) collective-permute-start(bf16[64,1024]{1,0:T(8,128)(2,1)S(1)} %get-tuple-element.65.refs_0_), channel_id=1, source_target_pairs={{0,24},{2,26},{4,28},{6,30},{8,0},{10,2},{12,4},{14,6},{16,8},{18,... | collective-permute-start | bytes 393224 | tf_op jit(solution)/shard_map/ppermute | solution.py:44
  20.2 14.0 %collective-permute-start.10 = (bf16[64,1024]{1,0:T(8,128)(2,1)S(1)}, bf16[64,1024]{1,0:T(8,128)(2,1)S(1)}, u32[]{:S(2)}, u32[]{:S(2)}) collective-permute-start(bf16[64,1024]{1,0:T(8,128)(2,1)S(1)} %collective-permute-done.4.refs_4_.refs_1_), channel_id=1, source_target_pairs={{0,24},{2,26},{4,28},{6,30},{8,0},{10,2},{12,4},{14,6},{16,8},{18,... | collective-permute-start | bytes 393224 | tf_op jit(solution)/shard_map/ppermute | solution.py:44
  22.3 12.0 %collective-permute-start.8 = (bf16[64,1024]{1,0:T(8,128)(2,1)S(1)}, bf16[64,1024]{1,0:T(8,128)(2,1)S(1)}, u32[]{:S(2)}, u32[]{:S(2)}) collective-permute-start(bf16[64,1024]{1,0:T(8,128)(2,1)S(1)} %collective-permute-done.4.refs_4_.refs_1_), channel_id=1, source_target_pairs={{0,8},{2,10},{4,12},{6,14},{8,16},{10,18},{12,20},{14,22},{16,24},... | collective-permute-start | bytes 393224 | tf_op jit(solution)/shard_map/ppermute | solution.py:44
  23.0 18.6 %collective-permute-start.9 = (bf16[64,1024]{1,0:T(8,128)(2,1)S(1)}, bf16[64,1024]{1,0:T(8,128)(2,1)S(1)}, u32[]{:S(2)}, u32[]{:S(2)}) collective-permute-start(bf16[64,1024]{1,0:T(8,128)(2,1)S(1)} %collective-permute-done.4.refs_4_.refs_1_), channel_id=1, source_target_pairs={{0,16},{2,18},{4,20},{6,22},{8,24},{10,26},{12,28},{14,30},{16,0},... | collective-permute-start | bytes 393224 | tf_op jit(solution)/shard_map/ppermute | solution.py:44
  32.2 9.4 %collective-permute-start.6 = (bf16[256,1024]{1,0:T(8,128)(2,1)S(1)}, bf16[256,1024]{1,0:T(8,128)(2,1)S(1)}, u32[]{:S(2)}, u32[]{:S(2)}) collective-permute-start(bf16[256,1024]{1,0:T(8,128)(2,1)S(1)} %column.1.refs_0_), channel_id=1, source_target_pairs={{0,2},{2,0},{4,6},{6,4},{8,10},{10,8},{12,14},{14,12},{16,18},{18,... | collective-permute-start | bytes 1572872 | tf_op jit(solution)/shard_map/ppermute | solution.py:44
  32.8 9.2 %collective-permute-start.7 = (bf16[256,1024]{1,0:T(8,128)(2,1)S(1)}, bf16[256,1024]{1,0:T(8,128)(2,1)S(1)}, u32[]{:S(2)}, u32[]{:S(2)}) collective-permute-start(bf16[256,1024]{1,0:T(8,128)(2,1)S(1)} %column.1.refs_0_), channel_id=1, source_target_pairs={{0,4},{2,6},{4,0},{6,2},{8,12},{10,14},{12,8},{14,10},{16,20},{18,... | collective-permute-start | bytes 1572872 | tf_op jit(solution)/shard_map/ppermute | solution.py:44
  34.2 8.5 %collective-permute-start.5 = (bf16[2,320,384]{2,1,0:T(8,128)(2,1)S(1)}, bf16[2,320,384]{2,1,0:T(8,128)(2,1)S(1)}, u32[]{:S(2)}, u32[]{:S(2)}) collective-permute-start(bf16[2,320,384]{2,1,0:T(8,128)(2,1)S(1)} %get-tuple-element.67), channel_id=1, source_target_pairs={{0,1},{1,0},{2,3},{3,2},{4,5},{5,4},{6,7},{7,6},{8,9},{9,8},{10,11... | collective-permute-start | bytes 1474568 | tf_op jit(solution)/shard_map/ppermute | solution.py:77
  46.4 4.7 %collective-permute-start.13 = (bf16[16,1024]{1,0:T(8,128)(2,1)S(1)}, bf16[16,1024]{1,0:T(8,128)(2,1)S(1)}, u32[]{:S(2)}, u32[]{:S(2)}) collective-permute-start(bf16[16,1024]{1,0:T(8,128)(2,1)S(1)} %get-tuple-element.78), channel_id=1, source_target_pairs={{0,2},{2,0},{4,6},{6,4},{8,10},{10,8},{12,14},{14,12},{16,18},{18,... | collective-permute-start | bytes 98312 | tf_op jit(solution)/shard_map/ppermute | solution.py:44
  48.2 4.8 %collective-permute-start.15 = (bf16[16,1024]{1,0:T(8,128)(2,1)S(1)}, bf16[16,1024]{1,0:T(8,128)(2,1)S(1)}, u32[]{:S(2)}, u32[]{:S(2)}) collective-permute-start(bf16[16,1024]{1,0:T(8,128)(2,1)S(1)} %get-tuple-element.78), channel_id=1, source_target_pairs={{0,6},{2,4},{4,2},{6,0},{8,14},{10,12},{12,10},{14,8},{16,22},{18,... | collective-permute-start | bytes 98312 | tf_op jit(solution)/shard_map/ppermute | solution.py:44
  53.0 7.9 %collective-permute-start.18 = (bf16[16,1024]{1,0:T(8,128)(2,1)S(1)}, bf16[16,1024]{1,0:T(8,128)(2,1)S(1)}, u32[]{:S(2)}, u32[]{:S(2)}) collective-permute-start(bf16[16,1024]{1,0:T(8,128)(2,1)S(1)} %get-tuple-element.83), channel_id=1, source_target_pairs={{0,8},{2,10},{4,12},{6,14},{8,16},{10,18},{12,20},{14,22},{16,24},... | collective-permute-start | bytes 98312 | tf_op jit(solution)/shard_map/ppermute | solution.py:44
  57.1 4.8 %collective-permute-start.19 = (bf16[16,1024]{1,0:T(8,128)(2,1)S(1)}, bf16[16,1024]{1,0:T(8,128)(2,1)S(1)}, u32[]{:S(2)}, u32[]{:S(2)}) collective-permute-start(bf16[16,1024]{1,0:T(8,128)(2,1)S(1)} %get-tuple-element.83), channel_id=1, source_target_pairs={{0,16},{2,18},{4,20},{6,22},{8,24},{10,26},{12,28},{14,30},{16,0},... | collective-permute-start | bytes 98312 | tf_op jit(solution)/shard_map/ppermute | solution.py:44
  63.7 20.2 %collective-permute-start.16 = (bf16[256,1024]{1,0:T(8,128)(2,1)S(1)}, bf16[256,1024]{1,0:T(8,128)(2,1)S(1)}, u32[]{:S(2)}, u32[]{:S(2)}) collective-permute-start(bf16[256,1024]{1,0:T(8,128)(2,1)S(1)} %get-tuple-element.80.refs_4_), channel_id=1, source_target_pairs={{0,2},{2,0},{4,6},{6,4},{8,10},{10,8},{12,14},{14,12},{16,18},{18,... | collective-permute-start | bytes 1572872 | tf_op jit(solution)/shard_map/ppermute | solution.py:44
  64.3 19.6 %collective-permute-start.17 = (bf16[256,1024]{1,0:T(8,128)(2,1)S(1)}, bf16[256,1024]{1,0:T(8,128)(2,1)S(1)}, u32[]{:S(2)}, u32[]{:S(2)}) collective-permute-start(bf16[256,1024]{1,0:T(8,128)(2,1)S(1)} %get-tuple-element.81), channel_id=1, source_target_pairs={{0,4},{2,6},{4,0},{6,2},{8,12},{10,14},{12,8},{14,10},{16,20},{18,... | collective-permute-start | bytes 1572872 | tf_op jit(solution)/shard_map/ppermute | solution.py:44
  65.8 14.5 %collective-permute-start.21 = (bf16[64,1024]{1,0:T(8,128)(2,1)}, bf16[64,1024]{1,0:T(8,128)(2,1)}, u32[]{:S(2)}, u32[]{:S(2)}) collective-permute-start(bf16[64,1024]{1,0:T(8,128)(2,1)} %copy-done.9), channel_id=1, source_target_pairs={{0,24},{2,26},{4,28},{6,30},{8,0},{10,2},{12,4},{14,6},{16,8},{18,... | collective-permute-start | bytes 393224 | tf_op jit(solution)/shard_map/ppermute | solution.py:44
  68.0 12.4 %collective-permute-start.22 = (bf16[64,1024]{1,0:T(8,128)(2,1)}, bf16[64,1024]{1,0:T(8,128)(2,1)}, u32[]{:S(2)}, u32[]{:S(2)}) collective-permute-start(bf16[64,1024]{1,0:T(8,128)(2,1)} %copy-done.8), channel_id=1, source_target_pairs={{0,16},{2,18},{4,20},{6,22},{8,24},{10,26},{12,28},{14,30},{16,0},... | collective-permute-start | bytes 393224 | tf_op jit(solution)/shard_map/ppermute | solution.py:44
  68.0 12.4 %collective-permute-start.23 = (bf16[64,1024]{1,0:T(8,128)(2,1)}, bf16[64,1024]{1,0:T(8,128)(2,1)}, u32[]{:S(2)}, u32[]{:S(2)}) collective-permute-start(bf16[64,1024]{1,0:T(8,128)(2,1)} %copy-done.7), channel_id=1, source_target_pairs={{0,8},{2,10},{4,12},{6,14},{8,16},{10,18},{12,20},{14,22},{16,24},... | collective-permute-start | bytes 393224 | tf_op jit(solution)/shard_map/ppermute | solution.py:44
  82.4 11.7 %collective-permute-start.25 = (bf16[64,1024]{1,0:T(8,128)(2,1)S(1)}, bf16[64,1024]{1,0:T(8,128)(2,1)}, u32[]{:S(2)}, u32[]{:S(2)}) collective-permute-start(bf16[64,1024]{1,0:T(8,128)(2,1)S(1)} %corner_sum.1), channel_id=1, source_target_pairs={{0,6},{2,4},{4,2},{6,0},{8,14},{10,12},{12,10},{14,8},{16,22},{18,... | collective-permute-start | bytes 393224 | tf_op jit(solution)/shard_map/ppermute | solution.py:44
  84.1 10.0 %collective-permute-start.26 = (bf16[64,1024]{1,0:T(8,128)(2,1)S(1)}, bf16[64,1024]{1,0:T(8,128)(2,1)S(1)}, u32[]{:S(2)}, u32[]{:S(2)}) collective-permute-start(bf16[64,1024]{1,0:T(8,128)(2,1)S(1)} %get-tuple-element.94), channel_id=1, source_target_pairs={{0,24},{2,26},{4,28},{6,30},{8,0},{10,2},{12,4},{14,6},{16,8},{18,... | collective-permute-start | bytes 393224 | tf_op jit(solution)/shard_map/ppermute | solution.py:44
  87.2 13.8 %collective-permute-start.27 = (bf16[64,1024]{1,0:T(8,128)(2,1)S(1)}, bf16[64,1024]{1,0:T(8,128)(2,1)S(1)}, u32[]{:S(2)}, u32[]{:S(2)}) collective-permute-start(bf16[64,1024]{1,0:T(8,128)(2,1)S(1)} %get-tuple-element.95), channel_id=1, source_target_pairs={{0,16},{2,18},{4,20},{6,22},{8,24},{10,26},{12,28},{14,30},{16,0},... | collective-permute-start | bytes 393224 | tf_op jit(solution)/shard_map/ppermute | solution.py:44
  88.3 12.7 %collective-permute-start.28 = (bf16[64,1024]{1,0:T(8,128)(2,1)S(1)}, bf16[64,1024]{1,0:T(8,128)(2,1)S(1)}, u32[]{:S(2)}, u32[]{:S(2)}) collective-permute-start(bf16[64,1024]{1,0:T(8,128)(2,1)S(1)} %get-tuple-element.96), channel_id=1, source_target_pairs={{0,8},{2,10},{4,12},{6,14},{8,16},{10,18},{12,20},{14,22},{16,24},... | collective-permute-start | bytes 393224 | tf_op jit(solution)/shard_map/ppermute | solution.py:44
  89.0 13.7 %all-to-all-start = ((f32[32,8,128]{2,1,0:T(8,128)}), f32[32,8,128]{2,1,0:T(8,128)S(1)}, u32[]{:S(2)}, u32[]{:S(2)}) async-start(f32[32,8,128]{2,1,0:T(8,128)} %broadcast_in_dim.33), calls=%async_computation | async-start | bytes 262144 | tf_op jit(solution)/shard_map/all_to_all | solution.py:82
  (17 other events, 138.3 us)

commit v3 on v2

--- a/solution.py
+++ b/solution.py
@@ -82,13 +82,13 @@
     return lax.all_to_all(jnp.broadcast_to(block[None], (count,) + block.shape), names, 0, 0, tiled=True)
 
 
-def kernel_call(body, outs, flops, name, *operands, gates=()):
+def kernel_call(body, outs, flops, name, *operands, gates=(), pinned=True):
     def run(*refs):
         body(*refs[: len(operands)], *refs[len(operands) + len(gates) :])
 
     result = pl.pallas_call(
         run,
-        out_shape=tuple(pltpu.VMEM(shape, dtype) for shape, dtype in outs),
+        out_shape=tuple((pltpu.VMEM if pinned else jax.ShapeDtypeStruct)(shape, dtype) for shape, dtype in outs),
         in_specs=[VMEM_SPEC] * len(operands) + [pl.BlockSpec(memory_space=pl.ANY)] * len(gates),
         out_specs=(VMEM_SPEC,) * len(outs),
         compiler_params=pltpu.CompilerParams(vmem_limit_bytes=20 * 1024 * 1024),
@@ -350,7 +350,7 @@
     return kernel_call(body, outs, 2 * rows * w_down.size, name, own, other, w_down, gates=gates)
 
 
-def summed(terms, outs, name, gates=(), flops=1000000):
+def summed(terms, outs, name, gates=(), flops=1000000, pinned=True):
     def body(*refs):
         total = None
         for ref in refs[: len(terms)]:
@@ -360,7 +360,7 @@
             ref[...] = total[start : start + shape[0]].astype(dtype)
 
     plain = [(shape, dtype) for _, shape, dtype in outs]
-    return kernel_call(body, plain, flops, name, *terms, gates=gates)
+    return kernel_call(body, plain, flops, name, *terms, gates=gates, pinned=pinned)
 
 
 def on_device(
@@ -461,55 +461,114 @@
         last_own, other_core(last_sent), w_down, residual, slot_request[None, :],
     )
     far_own, far_sent = gate_up(far + far_corner, w_gate, w_up, "far_gate_up", gates=(near[0], last_kept))
-    last_plane = [send(last_sent, count, steps) for steps in inner + middle + diagonal]
+    last_lines = [send(last_sent, count, steps) for steps in outer]
     last_outs = [(0, last_shape, jnp.float32), (0, last_shape, jnp.bfloat16)]
     far_outs = [(column.shape, jnp.bfloat16) for _ in far] + [(corner.shape, jnp.bfloat16) for _ in far_corners]
     parts = down_parts(far_own, other_core(far_sent), w_down, far_outs, "far_down")
-    last_kept, last_sent = summed([last_kept] + last_plane, last_outs, "last_plane", gates=(parts[0],))
-    last_lines = [send(last_sent, count, steps) for steps in outer]
-    half_rows = summed([last_kept] + last_lines, [(0, last_shape, jnp.float32)], "last_line")[0]
-    near_parts, far_parts = parts[: len(far)], parts[len(far) :]
-    near_parts = lax.optimization_barrier((near_parts, last_kept))[0]
-    half_rows, far_parts = lax.optimization_barrier((half_rows, far_parts))
-
-    returned = [send(part, count, back(steps)) for part, steps in zip(near_parts, inner + middle)]
+    last_outs = [(0, last_shape, jnp.float32), (0, last_shape, jnp.bfloat16)]
+
+    def join_lines(*refs):
+        lines, sources = refs[1 : 1 + len(outer)], refs[1 + len(outer) : 1 + len(outer) + len(far)]
+        kept_out, sent_out, *packed_outs = refs[1 + len(outer) + len(far) :]
+        total = refs[0][...]
+        for ref in lines:
+            total = total + ref[...].astype(jnp.float32)
+        kept_out[...] = total
+        sent_out[...] = total.astype(jnp.bfloat16)
+        for source, ref in zip(sources, packed_outs):
+            ref[: source.shape[0]] = source[...]
+            ref[source.shape[0] :] = total.astype(jnp.bfloat16)
+
+    column_rows = column.shape[0]
+    packed_out = ((column_rows + count, half_width), jnp.bfloat16)
+    last_kept, last_sent, *packed = kernel_call(
+        join_lines, [(last_shape, jnp.float32), (last_shape, jnp.bfloat16)] + [packed_out] * len(far), 1000000,
+        "join_lines", last_kept, *last_lines, *parts[: len(far)],
+    )
+
+    returned = [send(part, count, back(steps)) for part, steps in zip(packed, inner + middle)]
+    last_corners = [send(last_sent, count, steps) for steps in diagonal]
+    far_parts = lax.optimization_barrier((parts[len(far) :], last_kept))[0]
     returned_corners = [send(part, count, back(steps)) for part, steps in zip(far_parts, outer)]
 
-    other_rows = other_core(half_rows)
-    final_rows = jnp.where(
-        lax.axis_index("head") == 0,
-        jnp.concatenate([half_rows, other_rows], axis=1),
-        jnp.concatenate([other_rows, half_rows], axis=1),
-    )
-    scale = lax.rsqrt(jnp.mean(final_rows * final_rows, axis=-1, keepdims=True) + EPS)
-    final_rows = (final_rows * scale * final_gain).astype(jnp.bfloat16)
-    logits = jnp.dot(final_rows, w_vocab, preferred_element_type=jnp.float32)
-    own_max = jnp.max(logits, axis=1)
-    own_total = jnp.sum(jnp.exp(logits - own_max[:, None]), axis=1)
-    stats = jnp.zeros((8, 128), jnp.float32).at[0, :count].set(own_max).at[1, :count].set(own_total)
+    def join_columns(*refs):
+        own, last, sums = refs[0], refs[1], refs[2 : 2 + len(far)]
+        turns, out_refs = refs[2 + len(far) : 2 + len(far) + len(diagonal)], refs[2 + len(far) + len(diagonal) :]
+        for i, ref in enumerate(out_refs[:-1]):
+            rows = slice(i * row_count, (i + 1) * row_count)
+            total = own[rows]
+            for part in sums:
+                total = total + part[rows].astype(jnp.float32)
+            ref[...] = total.astype(ref.dtype)
+        total = last[...]
+        for part in sums:
+            total = total + part[column_rows:].astype(jnp.float32)
+        for part in turns:
+            total = total + part[...].astype(jnp.float32)
+        out_refs[-1][...] = total
+
+    column_outs = [(shape, jnp.float32)] + [(shape, jnp.bfloat16)] * len(outer) + [(last_shape, jnp.float32)]
+    *pieces, half_rows = kernel_call(
+        join_columns, column_outs, 1000000, "join_columns", near[0], last_kept, *returned, *last_corners,
+    )
+    devices = count * lax.axis_size("head")
+    vocab = w_vocab.shape[1]
+
+    def vocab_logits(own, other, gain, weight, logits_out, stats_out):
+        rows = []
+        for part in range(2):
+            mine = lax.axis_index("head") == part
+            rows.append(jnp.where(mine, own[...], other[...]))
+        rows = jnp.concatenate(rows, axis=1)
+        scale = lax.rsqrt(jnp.mean(rows * rows, axis=1, keepdims=True) + EPS)
+        rows = (rows * scale * gain[...]).astype(jnp.bfloat16)
+        largest = None
+        for start in range(0, vocab, 512):
+            stop = min(start + 512, vocab)
+            part = lax.dot_general(
+                rows, weight[start:stop, :], (((1,), (1,)), ((), ())), preferred_element_type=jnp.float32
+            )
+            logits_out[:, start:stop] = part
+            top = jnp.max(part, axis=1, keepdims=True)
+            largest = top if largest is None else jnp.maximum(largest, top)
+        total = jnp.sum(jnp.exp(logits_out[...] - largest), axis=1, keepdims=True)
+        row = lax.broadcasted_iota(jnp.int32, (count, 128), 0)
+        lane = lax.broadcasted_iota(jnp.int32, (count, 128), 1)
+        stats = jnp.where(lane == row, largest, 0.0) + jnp.where(lane == row + 64, total, 0.0)
+        stats_out[...] = jnp.broadcast_to(jnp.sum(stats, axis=0)[None, None], stats_out.shape)
+
+    logits, stats = kernel_call(
+        vocab_logits, [((count, vocab), jnp.float32), ((devices, 1, 128), jnp.float32)], 2 * count * w_vocab.size,
+        "vocab_logits", half_rows, other_core(half_rows), final_gain[None, :],
+        pltpu.with_memory_space_constraint(w_vocab.T, pltpu.VMEM),
+    )
     corner_sent = []
     if corners:
         corner_outs = [(row_count * i, shape, jnp.bfloat16) for i in range(len(corners))]
-        corner_pieces = summed([near[1]] + returned_corners, corner_outs, "corner_sum", flops=WEIGHT)
+        corner_pieces = summed([near[1]] + returned_corners, corner_outs, "corner_sum", gates=(stats,))
         corner_sent = [send(part, count, back(steps)) for part, steps in zip(corner_pieces, diagonal)]
-        returned = lax.optimization_barrier((returned, corner_pieces))[0]
-
-    column_outs = [(0, shape, jnp.float32)]
-    column_outs += [(row_count * (i + 1), shape, jnp.bfloat16) for i in range(len(outer))]
-    pieces = summed([near[0]] + returned, column_outs, "column_sum", gates=(stats,))
     final = [residual, pieces[0]] + corner_sent + [
         send(part, count, back(steps)) for part, steps in zip(pieces[1:], outer)
     ]
-    hidden_out = final[0]
-    for part in final[1:]:
-        hidden_out = hidden_out + part.astype(jnp.float32)
-    hidden_out = hidden_out.astype(jnp.bfloat16)
-    everyone = to_all(lax.optimization_barrier((stats, pieces))[0], ("req", "head"))
-    row_max = jnp.max(everyone[:, 0, :count], axis=0)
-    row_total = jnp.sum(everyone[:, 1, :count] * jnp.exp(everyone[:, 0, :count] - row_max[None, :]), axis=0)
-    log_probs = logits - (row_max + jnp.log(row_total))[:, None]
-
-    return (hidden_out, log_probs)
+    everyone = lax.all_to_all(stats, ("req", "head"), 0, 0, tiled=True)
+
+    def finish(*refs):
+        logits, everyone, hidden_out, log_out = *refs[:2], *refs[-2:]
+        total = None
+        for ref in refs[2:-2]:
+            part = ref[...].astype(jnp.float32)
+            total = part if total is None else total + part
+        hidden_out[...] = total.astype(jnp.bfloat16)
+        tiles = everyone[...]
+        top = jnp.max(tiles, axis=0, keepdims=True)
+        scaled = jnp.exp(jnp.minimum(tiles - top, 0.0))[:, :64] * tiles[:, 64:]
+        shift = top[:, :64] + jnp.log(jnp.sum(scaled, axis=0, keepdims=True))
+        row = lax.broadcasted_iota(jnp.int32, (count, 64), 0)
+        lane = lax.broadcasted_iota(jnp.int32, (count, 64), 1)
+        log_out[...] = logits[...] - jnp.sum(jnp.where(lane == row, shift, 0.0), axis=1, keepdims=True)
+
+    outs = [(shape, jnp.bfloat16), ((count, vocab), jnp.float32)]
+    return kernel_call(finish, outs, WEIGHT, "finish", logits, everyone[:, 0], *final, pinned=False)
 
 
 def solution(mesh):

time: 105 us -> 95.4 us (0.909)
  matrix products: 10.1 us -> 0 us
  blocking collectives: 0 us -> 9.68 us
  starting transfers between devices: 49 us -> 42.5 us
  Pallas kernels: 14.7 us -> 20.2 us
  other arithmetic: 4.84 us -> 0.01 us
  local copies, waits for them, and re-layouts: 2.78 us -> 0.45 us
    dot_general x1 -> x0, matrix products: 10.1 us -> none  [on_device(): logits = jnp.dot(final_rows, w_vocab, preferred_element_type=jnp.float32)]
    all_to_all x0 -> x1, blocking collectives: none -> 9.68 us  [on_device(): everyone = lax.all_to_all(stats, ('req', 'head'), 0, 0, tiled=True)]
    pallas_call x13 -> x14, Pallas kernels: 6.46 us -> 11.9 us  [kernel_call(): pl.pallas_call(run, out_shape=tuple(((pltpu.VMEM if pinned else jax.Shape...]
    all_to_all x1 -> x0, starting transfers between devices: 5.14 us -> none  [to_all(): lax.all_to_all(jnp.broadcast_to(block[None], (count,) + block.shape), nam...]
    sub x1 -> x0, other arithmetic: 1.78 us -> none  [on_device(): log_probs = logits - (row_max + jnp.log(row_total))[:, None]]
    convert_element_type x1 -> x0, other arithmetic: 1.66 us -> none  [on_device(): hidden_out = hidden_out.astype(jnp.bfloat16)]
    unnamed x22, local copies, waits for them, and re-layouts: 1.91 us -> 0.45 us
    reduce_sum x3 -> x0, other arithmetic: 1.36 us -> none  [the longest x1 1.2 us: on_device(): own_total = jnp.sum(jnp.exp(logits - own_max[:, None]), axis=1)]
  transfers between devices with their start and end apart: 30 -> 27, of which waited for: 10 -> 10; matrix products, arithmetic and copies ran while one was open for 13% -> 0% of each run, Pallas kernels for 4% -> 9%
where the time goes in v3:
time: 95.4 us; the launch traced here: 95.3 us
  starting transfers between devices  42.5 us (45%)
  waiting for transfers between devices  21.6 us (23%)
  Pallas kernels  20.2 us (21%)
  blocking collectives  9.68 us (10%)
    ppermute x22, starting transfers between devices, send(): return lax.ppermute(rows, 'req', pairs)  41.5 us
    ppermute x22, waiting for transfers between devices, send(): return lax.ppermute(rows, 'req', pairs)  20 us
    pallas_call x14, Pallas kernels, kernel_call(): pl.pallas_call(run, out_shape=tuple(((pltpu.VMEM if pinned else jax.Shape...  11.9 us
    all_to_all x1, blocking collectives, on_device(): everyone = lax.all_to_all(stats, ('req', 'head'), 0, 0, tiled=True)  9.68 us
    pallas_call x1, Pallas kernels, attention_rows(): pl.pallas_call(attention_kernel, out_shape=(pltpu.VMEM((rows, width), jnp...  8.25 us
  transfers between devices with their start and end apart: 27, of which 10 were waited for; matrix products, arithmetic and copies ran while one was open for 0% of the time, Pallas kernels for 9%

profile of v3, /device:TPU:0, one launch (start us, length us, event | category | flops | bytes accessed | tf_op | source)
XLA Modules:
  0.0 95.3 jit_solution(16080783132013332777)
XLA Ops:
  0.6 8.3 %attention_rows.1 = (f32[64,2048]{1,0:T(8,128)S(1)}, bf16[64,2048]{1,0:T(8,128)(2,1)S(1)}) custom-call(s32[16]{0:T(128)} %lengths_any.1, s32[16]{0:T(128)} %requests_any.1, bf16[64,2048]{1,0:T(8,128)(2,1)} %hidden_any.1, f32[1,2048]{1,0:T(1,128)} %bitcast.16, f32[1,128]{1,0:T(1,128)} %bitcast.17, f32[1,128]{1,0:T(1,128)} %bitcast.18, ...), custom_call_target="tpu_custom_call" | custom-call | flops 1400000000 | bytes 17500000 | tf_op jit(solution)/shard_map/attention_rows/pallas_call | solution.py:255
  9.4 1.2 %collective-permute-done.refs_1_ = bf16[64,2048]{1,0:T(8,128)(2,1)S(1)} collective-permute-done((bf16[64,2048]{1,0:T(8,128)(2,1)S(1)}, bf16[64,2048]{1,0:T(8,128)(2,1)S(1)}, u32[]{:S(2)}, u32[]{:S(2)}) %collective-permute-start) | collective-permute-done | bytes 262176 | tf_op jit(solution)/shard_map/ppermute | solution.py:77
  10.8 3.9 %collective-permute-start.4 = (bf16[64,1024]{1,0:T(8,128)(2,1)S(1)}, bf16[64,1024]{1,0:T(8,128)(2,1)S(1)}, u32[]{:S(2)}, u32[]{:S(2)}) collective-permute-start(bf16[64,1024]{1,0:T(8,128)(2,1)S(1)} %get-tuple-element.39.refs_0_), channel_id=1, source_target_pairs={{0,6},{2,4},{4,2},{6,0},{8,14},{10,12},{12,10},{14,8},{16,22},{18,... | collective-permute-start | bytes 393224 | tf_op jit(solution)/shard_map/ppermute | solution.py:44
  14.7 1.6 %collective-permute-start.1 = (bf16[64,1024]{1,0:T(8,128)(2,1)S(1)}, bf16[64,1024]{1,0:T(8,128)(2,1)S(1)}, u32[]{:S(2)}, u32[]{:S(2)}) collective-permute-start(bf16[64,1024]{1,0:T(8,128)(2,1)S(1)} %get-tuple-element.39.refs_0_), channel_id=1, source_target_pairs={{0,8},{2,10},{4,12},{6,14},{8,16},{10,18},{12,20},{14,22},{16,24},... | collective-permute-start | bytes 393224 | tf_op jit(solution)/shard_map/ppermute | solution.py:44
  16.3 2.6 %collective-permute-start.2 = (bf16[64,1024]{1,0:T(8,128)(2,1)S(1)}, bf16[64,1024]{1,0:T(8,128)(2,1)S(1)}, u32[]{:S(2)}, u32[]{:S(2)}) collective-permute-start(bf16[64,1024]{1,0:T(8,128)(2,1)S(1)} %get-tuple-element.39.refs_0_), channel_id=1, source_target_pairs={{0,16},{2,18},{4,20},{6,22},{8,24},{10,26},{12,28},{14,30},{16,0},... | collective-permute-start | bytes 393224 | tf_op jit(solution)/shard_map/ppermute | solution.py:44
  18.9 1.3 %collective-permute-start.3 = (bf16[64,1024]{1,0:T(8,128)(2,1)S(1)}, bf16[64,1024]{1,0:T(8,128)(2,1)S(1)}, u32[]{:S(2)}, u32[]{:S(2)}) collective-permute-start(bf16[64,1024]{1,0:T(8,128)(2,1)S(1)} %get-tuple-element.39.refs_0_), channel_id=1, source_target_pairs={{0,24},{2,26},{4,28},{6,30},{8,0},{10,2},{12,4},{14,6},{16,8},{18,... | collective-permute-start | bytes 393224 | tf_op jit(solution)/shard_map/ppermute | solution.py:44
  20.2 2.1 %collective-permute-start.10 = (bf16[64,1024]{1,0:T(8,128)(2,1)S(1)}, bf16[64,1024]{1,0:T(8,128)(2,1)S(1)}, u32[]{:S(2)}, u32[]{:S(2)}) collective-permute-start(bf16[64,1024]{1,0:T(8,128)(2,1)S(1)} %collective-permute-done.4.refs_4_.refs_1_), channel_id=1, source_target_pairs={{0,24},{2,26},{4,28},{6,30},{8,0},{10,2},{12,4},{14,6},{16,8},{18,... | collective-permute-start | bytes 393224 | tf_op jit(solution)/shard_map/ppermute | solution.py:44
  23.0 9.2 %collective-permute-start.9 = (bf16[64,1024]{1,0:T(8,128)(2,1)S(1)}, bf16[64,1024]{1,0:T(8,128)(2,1)S(1)}, u32[]{:S(2)}, u32[]{:S(2)}) collective-permute-start(bf16[64,1024]{1,0:T(8,128)(2,1)S(1)} %collective-permute-done.4.refs_4_.refs_1_), channel_id=1, source_target_pairs={{0,16},{2,18},{4,20},{6,22},{8,24},{10,26},{12,28},{14,30},{16,0},... | collective-permute-start | bytes 393224 | tf_op jit(solution)/shard_map/ppermute | solution.py:44
  34.3 7.2 %collective-permute-done.9.refs_1_ = bf16[64,1024]{1,0:T(8,128)(2,1)S(1)} collective-permute-done((bf16[64,1024]{1,0:T(8,128)(2,1)S(1)}, bf16[64,1024]{1,0:T(8,128)(2,1)S(1)}, u32[]{:S(2)}, u32[]{:S(2)}) %collective-permute-start.9) | collective-permute-done | bytes 131104 | tf_op jit(solution)/shard_map/ppermute | solution.py:44
  44.1 1.7 %far_gate_up.1 = (f32[2,704,384]{2,1,0:T(8,128)S(1)}, bf16[2,704,384]{2,1,0:T(8,128)(2,1)S(1)}) custom-call(bf16[256,1024]{1,0:T(8,128)(2,1)S(1)} %collective-permute-done.6.refs_2_.refs_0_, bf16[256,1024]{1,0:T(8,128)(2,1)S(1)} %collective-permute-done.7.refs_3_.refs_1_, bf16[192,1024]{1,0:T(8,128)(2,1)S(1)} %far_corner.1.refs_4_.refs_2_, ...), custom_call_target="tpu_custom_call" | custom-call | flops 1107296256 | bytes 1000000 | tf_op jit(solution)/shard_map/far_gate_up/pallas_call | solution.py:89
  46.0 3.8 %collective-permute-start.12 = (bf16[16,1024]{1,0:T(8,128)(2,1)S(1)}, bf16[16,1024]{1,0:T(8,128)(2,1)S(1)}, u32[]{:S(2)}, u32[]{:S(2)}) collective-permute-start(bf16[16,1024]{1,0:T(8,128)(2,1)S(1)} %get-tuple-element.49), channel_id=1, source_target_pairs={{0,8},{2,10},{4,12},{6,14},{8,16},{10,18},{12,20},{14,22},{16,24},... | collective-permute-start | bytes 98312 | tf_op jit(solution)/shard_map/ppermute | solution.py:44
  49.8 2.5 %collective-permute-start.13 = (bf16[16,1024]{1,0:T(8,128)(2,1)S(1)}, bf16[16,1024]{1,0:T(8,128)(2,1)S(1)}, u32[]{:S(2)}, u32[]{:S(2)}) collective-permute-start(bf16[16,1024]{1,0:T(8,128)(2,1)S(1)} %get-tuple-element.49), channel_id=1, source_target_pairs={{0,16},{2,18},{4,20},{6,22},{8,24},{10,26},{12,28},{14,30},{16,0},... | collective-permute-start | bytes 98312 | tf_op jit(solution)/shard_map/ppermute | solution.py:44
  52.3 1.1 %far_down.1 = (bf16[256,1024]{1,0:T(8,128)(2,1)S(1)}, bf16[256,1024]{1,0:T(8,128)(2,1)S(1)}, bf16[64,1024]{1,0:T(8,128)(2,1)S(1)}, bf16[64,1024]{1,0:T(8,128)(2,1)S(1)}, bf16[64,1024]{1,0:T(8,128)(2,1)S(1)}) custom-call(f32[2,704,384]{2,1,0:T(8,128)S(1)} %get-tuple-element.50.refs_0_, bf16[2,704,384]{2,1,0:T(8,128)(2,1)S(1)} %collective-permute-done.15.refs_1_, ...), custom_call_target="tpu_custom_call" | custom-call | flops 553648128 | bytes 1000000 | tf_op jit(solution)/shard_map/far_down/pallas_call | solution.py:89
  54.1 1.1 %collective-permute-done.13.refs_2_ = bf16[16,1024]{1,0:T(8,128)(2,1)S(1)} collective-permute-done((bf16[16,1024]{1,0:T(8,128)(2,1)S(1)}, bf16[16,1024]{1,0:T(8,128)(2,1)S(1)}, u32[]{:S(2)}, u32[]{:S(2)}) %collective-permute-start.13) | collective-permute-done | bytes 32800 | tf_op jit(solution)/shard_map/ppermute | solution.py:44
  55.1 1.1 %collective-permute-done.14.refs_3_ = bf16[16,1024]{1,0:T(8,128)(2,1)S(1)} collective-permute-done((bf16[16,1024]{1,0:T(8,128)(2,1)S(1)}, bf16[16,1024]{1,0:T(8,128)(2,1)S(1)}, u32[]{:S(2)}, u32[]{:S(2)}) %collective-permute-start.14) | collective-permute-done | bytes 32800 | tf_op jit(solution)/shard_map/ppermute | solution.py:44
  56.3 1.6 %collective-permute-start.16 = (bf16[272,1024]{1,0:T(8,128)(2,1)S(1)}, bf16[272,1024]{1,0:T(8,128)(2,1)S(1)}, u32[]{:S(2)}, u32[]{:S(2)}) collective-permute-start(bf16[272,1024]{1,0:T(8,128)(2,1)S(1)} %get-tuple-element.55), channel_id=1, source_target_pairs={{0,2},{2,0},{4,6},{6,4},{8,10},{10,8},{12,14},{14,12},{16,18},{18,... | collective-permute-start | bytes 1671176 | tf_op jit(solution)/shard_map/ppermute | solution.py:44
  58.4 1.5 %collective-permute-start.18 = (bf16[16,1024]{1,0:T(8,128)(2,1)S(1)}, bf16[16,1024]{1,0:T(8,128)(2,1)S(1)}, u32[]{:S(2)}, u32[]{:S(2)}) collective-permute-start(bf16[16,1024]{1,0:T(8,128)(2,1)S(1)} %get-tuple-element.57), channel_id=1, source_target_pairs={{0,6},{2,4},{4,2},{6,0},{8,14},{10,12},{12,10},{14,8},{16,22},{18,... | collective-permute-start | bytes 98312 | tf_op jit(solution)/shard_map/ppermute | solution.py:44
  59.9 2.1 %collective-permute-start.20 = (bf16[64,1024]{1,0:T(8,128)(2,1)S(1)}, bf16[64,1024]{1,0:T(8,128)(2,1)S(1)}, u32[]{:S(2)}, u32[]{:S(2)}) collective-permute-start(bf16[64,1024]{1,0:T(8,128)(2,1)S(1)} %get-tuple-element.66), channel_id=1, source_target_pairs={{0,24},{2,26},{4,28},{6,30},{8,0},{10,2},{12,4},{14,6},{16,8},{18,... | collective-permute-start | bytes 393224 | tf_op jit(solution)/shard_map/ppermute | solution.py:44
  62.0 8.7 %collective-permute-done.18.refs_4_ = bf16[16,1024]{1,0:T(8,128)(2,1)S(1)} collective-permute-done((bf16[16,1024]{1,0:T(8,128)(2,1)S(1)}, bf16[16,1024]{1,0:T(8,128)(2,1)S(1)}, u32[]{:S(2)}, u32[]{:S(2)}) %collective-permute-start.18) | collective-permute-done | bytes 32800 | tf_op jit(solution)/shard_map/ppermute | solution.py:44
  72.1 2.9 %collective-permute-start.24 = (bf16[64,1024]{1,0:T(8,128)(2,1)S(1)}, bf16[64,1024]{1,0:T(8,128)(2,1)S(1)}, u32[]{:S(2)}, u32[]{:S(2)}) collective-permute-start(bf16[64,1024]{1,0:T(8,128)(2,1)S(1)} %get-tuple-element.69), channel_id=1, source_target_pairs={{0,24},{2,26},{4,28},{6,30},{8,0},{10,2},{12,4},{14,6},{16,8},{18,... | collective-permute-start | bytes 393224 | tf_op jit(solution)/shard_map/ppermute | solution.py:44
  75.1 5.4 %vocab_logits.1 = (f32[16,4748]{1,0:T(8,128)S(1)}, f32[32,1,128]{2,1,0:T(1,128)S(1)}) custom-call(f32[16,1024]{1,0:T(8,128)S(1)} %get-tuple-element.58.refs_0_, f32[16,1024]{1,0:T(8,128)S(1)} %collective-permute-done.19.refs_1_, f32[1,2048]{1,0:T(1,128)S(1)} %bitcast.12, bf16[4748,2048]{1,0:T(8,128)(2,1)S(1)} %bitcast.10), custom_call_target="tpu_custom_call" | custom-call | flops 311164928 | bytes 1000000 | tf_op jit(solution)/shard_map/vocab_logits/pallas_call | solution.py:89
  80.5 1.6 %collective-permute-start.26 = (bf16[64,1024]{1,0:T(8,128)(2,1)S(1)}, bf16[64,1024]{1,0:T(8,128)(2,1)S(1)}, u32[]{:S(2)}, u32[]{:S(2)}) collective-permute-start(bf16[64,1024]{1,0:T(8,128)(2,1)S(1)} %get-tuple-element.71), channel_id=1, source_target_pairs={{0,8},{2,10},{4,12},{6,14},{8,16},{10,18},{12,20},{14,22},{16,24},... | collective-permute-start | bytes 393224 | tf_op jit(solution)/shard_map/ppermute | solution.py:44
  82.2 2.4 %collective-permute-start.23 = (bf16[64,1024]{1,0:T(8,128)(2,1)S(1)}, bf16[64,1024]{1,0:T(8,128)(2,1)S(1)}, u32[]{:S(2)}, u32[]{:S(2)}) collective-permute-start(bf16[64,1024]{1,0:T(8,128)(2,1)S(1)} %corner_sum.1), channel_id=1, source_target_pairs={{0,6},{2,4},{4,2},{6,0},{8,14},{10,12},{12,10},{14,8},{16,22},{18,... | collective-permute-start | bytes 393224 | tf_op jit(solution)/shard_map/ppermute | solution.py:44
  84.6 9.7 %all_to_all.5 = f32[32,1,128]{2,1,0:T(1,128)S(1)} all-to-all(f32[32,1,128]{2,1,0:T(1,128)S(1)} %get-tuple-element.60.refs_4_), channel_id=1, replica_groups=mesh['req'=16,'head'=2] {'req','head'}, dimensions={0} | all-to-all | bytes 32768 | tf_op jit(solution)/shard_map/all_to_all | solution.py:553
  (69 shorter events, 9.9 us)
Async XLA Ops:
  10.8 9.4 %collective-permute-start.4 = (bf16[64,1024]{1,0:T(8,128)(2,1)S(1)}, bf16[64,1024]{1,0:T(8,128)(2,1)S(1)}, u32[]{:S(2)}, u32[]{:S(2)}) collective-permute-start(bf16[64,1024]{1,0:T(8,128)(2,1)S(1)} %get-tuple-element.39.refs_0_), channel_id=1, source_target_pairs={{0,6},{2,4},{4,2},{6,0},{8,14},{10,12},{12,10},{14,8},{16,22},{18,... | collective-permute-start | bytes 393224 | tf_op jit(solution)/shard_map/ppermute | solution.py:44
  14.7 8.3 %collective-permute-start.1 = (bf16[64,1024]{1,0:T(8,128)(2,1)S(1)}, bf16[64,1024]{1,0:T(8,128)(2,1)S(1)}, u32[]{:S(2)}, u32[]{:S(2)}) collective-permute-start(bf16[64,1024]{1,0:T(8,128)(2,1)S(1)} %get-tuple-element.39.refs_0_), channel_id=1, source_target_pairs={{0,8},{2,10},{4,12},{6,14},{8,16},{10,18},{12,20},{14,22},{16,24},... | collective-permute-start | bytes 393224 | tf_op jit(solution)/shard_map/ppermute | solution.py:44
  16.3 15.9 %collective-permute-start.2 = (bf16[64,1024]{1,0:T(8,128)(2,1)S(1)}, bf16[64,1024]{1,0:T(8,128)(2,1)S(1)}, u32[]{:S(2)}, u32[]{:S(2)}) collective-permute-start(bf16[64,1024]{1,0:T(8,128)(2,1)S(1)} %get-tuple-element.39.refs_0_), channel_id=1, source_target_pairs={{0,16},{2,18},{4,20},{6,22},{8,24},{10,26},{12,28},{14,30},{16,0},... | collective-permute-start | bytes 393224 | tf_op jit(solution)/shard_map/ppermute | solution.py:44
  18.9 13.3 %collective-permute-start.3 = (bf16[64,1024]{1,0:T(8,128)(2,1)S(1)}, bf16[64,1024]{1,0:T(8,128)(2,1)S(1)}, u32[]{:S(2)}, u32[]{:S(2)}) collective-permute-start(bf16[64,1024]{1,0:T(8,128)(2,1)S(1)} %get-tuple-element.39.refs_0_), channel_id=1, source_target_pairs={{0,24},{2,26},{4,28},{6,30},{8,0},{10,2},{12,4},{14,6},{16,8},{18,... | collective-permute-start | bytes 393224 | tf_op jit(solution)/shard_map/ppermute | solution.py:44
  20.2 14.0 %collective-permute-start.10 = (bf16[64,1024]{1,0:T(8,128)(2,1)S(1)}, bf16[64,1024]{1,0:T(8,128)(2,1)S(1)}, u32[]{:S(2)}, u32[]{:S(2)}) collective-permute-start(bf16[64,1024]{1,0:T(8,128)(2,1)S(1)} %collective-permute-done.4.refs_4_.refs_1_), channel_id=1, source_target_pairs={{0,24},{2,26},{4,28},{6,30},{8,0},{10,2},{12,4},{14,6},{16,8},{18,... | collective-permute-start | bytes 393224 | tf_op jit(solution)/shard_map/ppermute | solution.py:44
  22.3 12.0 %collective-permute-start.8 = (bf16[64,1024]{1,0:T(8,128)(2,1)S(1)}, bf16[64,1024]{1,0:T(8,128)(2,1)S(1)}, u32[]{:S(2)}, u32[]{:S(2)}) collective-permute-start(bf16[64,1024]{1,0:T(8,128)(2,1)S(1)} %collective-permute-done.4.refs_4_.refs_1_), channel_id=1, source_target_pairs={{0,8},{2,10},{4,12},{6,14},{8,16},{10,18},{12,20},{14,22},{16,24},... | collective-permute-start | bytes 393224 | tf_op jit(solution)/shard_map/ppermute | solution.py:44
  23.0 18.6 %collective-permute-start.9 = (bf16[64,1024]{1,0:T(8,128)(2,1)S(1)}, bf16[64,1024]{1,0:T(8,128)(2,1)S(1)}, u32[]{:S(2)}, u32[]{:S(2)}) collective-permute-start(bf16[64,1024]{1,0:T(8,128)(2,1)S(1)} %collective-permute-done.4.refs_4_.refs_1_), channel_id=1, source_target_pairs={{0,16},{2,18},{4,20},{6,22},{8,24},{10,26},{12,28},{14,30},{16,0},... | collective-permute-start | bytes 393224 | tf_op jit(solution)/shard_map/ppermute | solution.py:44
  32.2 9.4 %collective-permute-start.6 = (bf16[256,1024]{1,0:T(8,128)(2,1)S(1)}, bf16[256,1024]{1,0:T(8,128)(2,1)S(1)}, u32[]{:S(2)}, u32[]{:S(2)}) collective-permute-start(bf16[256,1024]{1,0:T(8,128)(2,1)S(1)} %column.1.refs_0_), channel_id=1, source_target_pairs={{0,2},{2,0},{4,6},{6,4},{8,10},{10,8},{12,14},{14,12},{16,18},{18,... | collective-permute-start | bytes 1572872 | tf_op jit(solution)/shard_map/ppermute | solution.py:44
  32.8 9.2 %collective-permute-start.7 = (bf16[256,1024]{1,0:T(8,128)(2,1)S(1)}, bf16[256,1024]{1,0:T(8,128)(2,1)S(1)}, u32[]{:S(2)}, u32[]{:S(2)}) collective-permute-start(bf16[256,1024]{1,0:T(8,128)(2,1)S(1)} %column.1.refs_0_), channel_id=1, source_target_pairs={{0,4},{2,6},{4,0},{6,2},{8,12},{10,14},{12,8},{14,10},{16,20},{18,... | collective-permute-start | bytes 1572872 | tf_op jit(solution)/shard_map/ppermute | solution.py:44
  34.2 8.5 %collective-permute-start.5 = (bf16[2,320,384]{2,1,0:T(8,128)(2,1)S(1)}, bf16[2,320,384]{2,1,0:T(8,128)(2,1)S(1)}, u32[]{:S(2)}, u32[]{:S(2)}) collective-permute-start(bf16[2,320,384]{2,1,0:T(8,128)(2,1)S(1)} %get-tuple-element.41), channel_id=1, source_target_pairs={{0,1},{1,0},{2,3},{3,2},{4,5},{5,4},{6,7},{7,6},{8,9},{9,8},{10,11... | collective-permute-start | bytes 1474568 | tf_op jit(solution)/shard_map/ppermute | solution.py:77
  45.8 6.5 %collective-permute-start.15 = (bf16[2,704,384]{2,1,0:T(8,128)(2,1)S(1)}, bf16[2,704,384]{2,1,0:T(8,128)(2,1)S(1)}, u32[]{:S(2)}, u32[]{:S(2)}) collective-permute-start(bf16[2,704,384]{2,1,0:T(8,128)(2,1)S(1)} %get-tuple-element.51), channel_id=1, source_target_pairs={{0,1},{1,0},{2,3},{3,2},{4,5},{5,4},{6,7},{7,6},{8,9},{9,8},{10,11... | collective-permute-start | bytes 3244040 | tf_op jit(solution)/shard_map/ppermute | solution.py:77
  46.0 8.1 %collective-permute-start.12 = (bf16[16,1024]{1,0:T(8,128)(2,1)S(1)}, bf16[16,1024]{1,0:T(8,128)(2,1)S(1)}, u32[]{:S(2)}, u32[]{:S(2)}) collective-permute-start(bf16[16,1024]{1,0:T(8,128)(2,1)S(1)} %get-tuple-element.49), channel_id=1, source_target_pairs={{0,8},{2,10},{4,12},{6,14},{8,16},{10,18},{12,20},{14,22},{16,24},... | collective-permute-start | bytes 98312 | tf_op jit(solution)/shard_map/ppermute | solution.py:44
  49.8 5.3 %collective-permute-start.13 = (bf16[16,1024]{1,0:T(8,128)(2,1)S(1)}, bf16[16,1024]{1,0:T(8,128)(2,1)S(1)}, u32[]{:S(2)}, u32[]{:S(2)}) collective-permute-start(bf16[16,1024]{1,0:T(8,128)(2,1)S(1)} %get-tuple-element.49), channel_id=1, source_target_pairs={{0,16},{2,18},{4,20},{6,22},{8,24},{10,26},{12,28},{14,30},{16,0},... | collective-permute-start | bytes 98312 | tf_op jit(solution)/shard_map/ppermute | solution.py:44
  52.3 3.9 %collective-permute-start.14 = (bf16[16,1024]{1,0:T(8,128)(2,1)S(1)}, bf16[16,1024]{1,0:T(8,128)(2,1)S(1)}, u32[]{:S(2)}, u32[]{:S(2)}) collective-permute-start(bf16[16,1024]{1,0:T(8,128)(2,1)S(1)} %get-tuple-element.49), channel_id=1, source_target_pairs={{0,24},{2,26},{4,28},{6,30},{8,0},{10,2},{12,4},{14,6},{16,8},{18,... | collective-permute-start | bytes 98312 | tf_op jit(solution)/shard_map/ppermute | solution.py:44
  56.3 15.2 %collective-permute-start.16 = (bf16[272,1024]{1,0:T(8,128)(2,1)S(1)}, bf16[272,1024]{1,0:T(8,128)(2,1)S(1)}, u32[]{:S(2)}, u32[]{:S(2)}) collective-permute-start(bf16[272,1024]{1,0:T(8,128)(2,1)S(1)} %get-tuple-element.55), channel_id=1, source_target_pairs={{0,2},{2,0},{4,6},{6,4},{8,10},{10,8},{12,14},{14,12},{16,18},{18,... | collective-permute-start | bytes 1671176 | tf_op jit(solution)/shard_map/ppermute | solution.py:44
  57.9 14.0 %collective-permute-start.17 = (bf16[272,1024]{1,0:T(8,128)(2,1)S(1)}, bf16[272,1024]{1,0:T(8,128)(2,1)S(1)}, u32[]{:S(2)}, u32[]{:S(2)}) collective-permute-start(bf16[272,1024]{1,0:T(8,128)(2,1)S(1)} %get-tuple-element.56), channel_id=1, source_target_pairs={{0,4},{2,6},{4,0},{6,2},{8,12},{10,14},{12,8},{14,10},{16,20},{18,... | collective-permute-start | bytes 1671176 | tf_op jit(solution)/shard_map/ppermute | solution.py:44
  58.4 12.3 %collective-permute-start.18 = (bf16[16,1024]{1,0:T(8,128)(2,1)S(1)}, bf16[16,1024]{1,0:T(8,128)(2,1)S(1)}, u32[]{:S(2)}, u32[]{:S(2)}) collective-permute-start(bf16[16,1024]{1,0:T(8,128)(2,1)S(1)} %get-tuple-element.57), channel_id=1, source_target_pairs={{0,6},{2,4},{4,2},{6,0},{8,14},{10,12},{12,10},{14,8},{16,22},{18,... | collective-permute-start | bytes 98312 | tf_op jit(solution)/shard_map/ppermute | solution.py:44
  59.9 20.6 %collective-permute-start.20 = (bf16[64,1024]{1,0:T(8,128)(2,1)S(1)}, bf16[64,1024]{1,0:T(8,128)(2,1)S(1)}, u32[]{:S(2)}, u32[]{:S(2)}) collective-permute-start(bf16[64,1024]{1,0:T(8,128)(2,1)S(1)} %get-tuple-element.66), channel_id=1, source_target_pairs={{0,24},{2,26},{4,28},{6,30},{8,0},{10,2},{12,4},{14,6},{16,8},{18,... | collective-permute-start | bytes 393224 | tf_op jit(solution)/shard_map/ppermute | solution.py:44
  62.0 20.1 %collective-permute-start.21 = (bf16[64,1024]{1,0:T(8,128)(2,1)S(1)}, bf16[64,1024]{1,0:T(8,128)(2,1)S(1)}, u32[]{:S(2)}, u32[]{:S(2)}) collective-permute-start(bf16[64,1024]{1,0:T(8,128)(2,1)S(1)} %get-tuple-element.67), channel_id=1, source_target_pairs={{0,16},{2,18},{4,20},{6,22},{8,24},{10,26},{12,28},{14,30},{16,0},... | collective-permute-start | bytes 393224 | tf_op jit(solution)/shard_map/ppermute | solution.py:44
  70.7 11.4 %collective-permute-start.22 = (bf16[64,1024]{1,0:T(8,128)(2,1)S(1)}, bf16[64,1024]{1,0:T(8,128)(2,1)S(1)}, u32[]{:S(2)}, u32[]{:S(2)}) collective-permute-start(bf16[64,1024]{1,0:T(8,128)(2,1)S(1)} %get-tuple-element.68), channel_id=1, source_target_pairs={{0,8},{2,10},{4,12},{6,14},{8,16},{10,18},{12,20},{14,22},{16,24},... | collective-permute-start | bytes 393224 | tf_op jit(solution)/shard_map/ppermute | solution.py:44
  72.1 22.2 %collective-permute-start.24 = (bf16[64,1024]{1,0:T(8,128)(2,1)S(1)}, bf16[64,1024]{1,0:T(8,128)(2,1)S(1)}, u32[]{:S(2)}, u32[]{:S(2)}) collective-permute-start(bf16[64,1024]{1,0:T(8,128)(2,1)S(1)} %get-tuple-element.69), channel_id=1, source_target_pairs={{0,24},{2,26},{4,28},{6,30},{8,0},{10,2},{12,4},{14,6},{16,8},{18,... | collective-permute-start | bytes 393224 | tf_op jit(solution)/shard_map/ppermute | solution.py:44
  75.0 19.3 %collective-permute-start.25 = (bf16[64,1024]{1,0:T(8,128)(2,1)S(1)}, bf16[64,1024]{1,0:T(8,128)(2,1)S(1)}, u32[]{:S(2)}, u32[]{:S(2)}) collective-permute-start(bf16[64,1024]{1,0:T(8,128)(2,1)S(1)} %get-tuple-element.70), channel_id=1, source_target_pairs={{0,16},{2,18},{4,20},{6,22},{8,24},{10,26},{12,28},{14,30},{16,0},... | collective-permute-start | bytes 393224 | tf_op jit(solution)/shard_map/ppermute | solution.py:44
  80.5 13.8 %collective-permute-start.26 = (bf16[64,1024]{1,0:T(8,128)(2,1)S(1)}, bf16[64,1024]{1,0:T(8,128)(2,1)S(1)}, u32[]{:S(2)}, u32[]{:S(2)}) collective-permute-start(bf16[64,1024]{1,0:T(8,128)(2,1)S(1)} %get-tuple-element.71), channel_id=1, source_target_pairs={{0,8},{2,10},{4,12},{6,14},{8,16},{10,18},{12,20},{14,22},{16,24},... | collective-permute-start | bytes 393224 | tf_op jit(solution)/shard_map/ppermute | solution.py:44
  82.2 12.1 %collective-permute-start.23 = (bf16[64,1024]{1,0:T(8,128)(2,1)S(1)}, bf16[64,1024]{1,0:T(8,128)(2,1)S(1)}, u32[]{:S(2)}, u32[]{:S(2)}) collective-permute-start(bf16[64,1024]{1,0:T(8,128)(2,1)S(1)} %corner_sum.1), channel_id=1, source_target_pairs={{0,6},{2,4},{4,2},{6,0},{8,14},{10,12},{12,10},{14,8},{16,22},{18,... | collective-permute-start | bytes 393224 | tf_op jit(solution)/shard_map/ppermute | solution.py:44
  (14 other events, 254.9 us)

commit v4 on v3

--- a/solution.py
+++ b/solution.py
@@ -27,6 +27,12 @@
     if side**3 == count:
         return (side, side, side)
     return (count, 1, 1)
+
+
+def moved(place, size, step):
+    if size & (size - 1) == 0:
+        return place ^ abs(step)
+    return (place + step) % size
 
 
 def send(rows, count, steps):
@@ -39,14 +45,14 @@
             places.append(left % size)
             left //= size
         for place, size, step in zip(reversed(places), sizes, steps):
-            target = target * size + (place + step) % size
+            target = target * size + moved(place, size, step)
         pairs.append((i, target))
     return lax.ppermute(rows, "req", pairs)
 
 
 def along(count, digit):
     steps = []
-    for step in range(1, sizes_of(count)[digit]):
+    for step in reversed(range(1, sizes_of(count)[digit])):
         one = [0, 0, 0]
         one[digit] = step
         steps.append(tuple(one))
@@ -64,7 +70,12 @@
 def slot_behind(slot, count, steps):
     result, stride = 0, 1
     for size, step in zip(reversed(sizes_of(count)), reversed(steps)):
-        result = result + lax.rem(lax.div(slot, stride) + size - step % size, size) * stride
+        place = lax.rem(lax.div(slot, stride), size)
+        if size & (size - 1) == 0:
+            place = place ^ abs(step)
+        else:
+            place = lax.rem(place + size - step % size, size)
+        result = result + place * stride
         stride *= size
     return result
 

time: 95.4 us -> 93.8 us (0.983)
  starting transfers between devices: 42.5 us -> 37.7 us
  waiting for transfers between devices: 21.6 us -> 23.9 us
  blocking collectives: 9.68 us -> 10.8 us
    ppermute x22, starting transfers between devices: 41.5 us -> 36.7 us  [send(): return lax.ppermute(rows, 'req', pairs)]
    ppermute x22, waiting for transfers between devices: 20 us -> 22.2 us  [send(): return lax.ppermute(rows, 'req', pairs)]
    all_to_all x1, blocking collectives: 9.68 us -> 10.8 us  [on_device(): everyone = lax.all_to_all(stats, ('req', 'head'), 0, 0, tiled=True)]
  transfers between devices with their start and end apart: 27 -> 27, of which waited for: 10 -> 12; matrix products, arithmetic and copies ran while one was open for 0% -> 0% of each run, Pallas kernels for 9% -> 9%
where the time goes in v4:
time: 93.8 us; the launch traced here: 93.6 us
  starting transfers between devices  37.7 us (40%)
  waiting for transfers between devices  23.9 us (25%)
  Pallas kernels  20.4 us (22%)
  blocking collectives  10.8 us (12%)
    ppermute x22, starting transfers between devices, send(): return lax.ppermute(rows, 'req', pairs)  36.7 us
    ppermute x22, waiting for transfers between devices, send(): return lax.ppermute(rows, 'req', pairs)  22.2 us
    pallas_call x14, Pallas kernels, kernel_call(): pl.pallas_call(run, out_shape=tuple(((pltpu.VMEM if pinned else jax.Shape...  12.1 us
    all_to_all x1, blocking collectives, on_device(): everyone = lax.all_to_all(stats, ('req', 'head'), 0, 0, tiled=True)  10.8 us
    pallas_call x1, Pallas kernels, attention_rows(): pl.pallas_call(attention_kernel, out_shape=(pltpu.VMEM((rows, width), jnp...  8.25 us
  transfers between devices with their start and end apart: 27, of which 12 were waited for; matrix products, arithmetic and copies ran while one was open for 0% of the time, Pallas kernels for 9%

profile of v4, /device:TPU:0, one launch (start us, length us, event | category | flops | bytes accessed | tf_op | source)
XLA Modules:
  0.0 93.6 jit_solution(10515970540380426554)
XLA Ops:
  0.6 8.3 %attention_rows.1 = (f32[64,2048]{1,0:T(8,128)S(1)}, bf16[64,2048]{1,0:T(8,128)(2,1)S(1)}) custom-call(s32[16]{0:T(128)} %lengths_any.1, s32[16]{0:T(128)} %requests_any.1, bf16[64,2048]{1,0:T(8,128)(2,1)} %hidden_any.1, f32[1,2048]{1,0:T(1,128)} %bitcast.16, f32[1,128]{1,0:T(1,128)} %bitcast.17, f32[1,128]{1,0:T(1,128)} %bitcast.18, ...), custom_call_target="tpu_custom_call" | custom-call | flops 1400000000 | bytes 17500000 | tf_op jit(solution)/shard_map/attention_rows/pallas_call | solution.py:266
  9.4 1.2 %collective-permute-done.refs_1_ = bf16[64,2048]{1,0:T(8,128)(2,1)S(1)} collective-permute-done((bf16[64,2048]{1,0:T(8,128)(2,1)S(1)}, bf16[64,2048]{1,0:T(8,128)(2,1)S(1)}, u32[]{:S(2)}, u32[]{:S(2)}) %collective-permute-start) | collective-permute-done | bytes 262176 | tf_op jit(solution)/shard_map/ppermute | solution.py:88
  11.0 3.9 %collective-permute-start.4 = (bf16[64,1024]{1,0:T(8,128)(2,1)S(1)}, bf16[64,1024]{1,0:T(8,128)(2,1)S(1)}, u32[]{:S(2)}, u32[]{:S(2)}) collective-permute-start(bf16[64,1024]{1,0:T(8,128)(2,1)S(1)} %get-tuple-element.39.refs_0_), channel_id=1, source_target_pairs={{0,6},{2,4},{4,2},{6,0},{8,14},{10,12},{12,10},{14,8},{16,22},{18,... | collective-permute-start | bytes 393224 | tf_op jit(solution)/shard_map/ppermute | solution.py:50
  14.9 3.6 %collective-permute-start.1 = (bf16[64,1024]{1,0:T(8,128)(2,1)S(1)}, bf16[64,1024]{1,0:T(8,128)(2,1)S(1)}, u32[]{:S(2)}, u32[]{:S(2)}) collective-permute-start(bf16[64,1024]{1,0:T(8,128)(2,1)S(1)} %get-tuple-element.39.refs_0_), channel_id=1, source_target_pairs={{0,24},{2,26},{4,28},{6,30},{8,16},{10,18},{12,20},{14,22},{16,8},... | collective-permute-start | bytes 393224 | tf_op jit(solution)/shard_map/ppermute | solution.py:50
  19.3 1.2 %collective-permute-start.10 = (bf16[64,1024]{1,0:T(8,128)(2,1)S(1)}, bf16[64,1024]{1,0:T(8,128)(2,1)S(1)}, u32[]{:S(2)}, u32[]{:S(2)}) collective-permute-start(bf16[64,1024]{1,0:T(8,128)(2,1)S(1)} %collective-permute-done.4.refs_4_.refs_1_), channel_id=1, source_target_pairs={{0,8},{2,10},{4,12},{6,14},{8,0},{10,2},{12,4},{14,6},{16,24},{18,... | collective-permute-start | bytes 393224 | tf_op jit(solution)/shard_map/ppermute | solution.py:50
  20.5 2.4 %collective-permute-start.8 = (bf16[64,1024]{1,0:T(8,128)(2,1)S(1)}, bf16[64,1024]{1,0:T(8,128)(2,1)S(1)}, u32[]{:S(2)}, u32[]{:S(2)}) collective-permute-start(bf16[64,1024]{1,0:T(8,128)(2,1)S(1)} %collective-permute-done.4.refs_4_.refs_1_), channel_id=1, source_target_pairs={{0,24},{2,26},{4,28},{6,30},{8,16},{10,18},{12,20},{14,22},{16,8},... | collective-permute-start | bytes 393224 | tf_op jit(solution)/shard_map/ppermute | solution.py:50
  23.1 6.4 %collective-permute-start.9 = (bf16[64,1024]{1,0:T(8,128)(2,1)S(1)}, bf16[64,1024]{1,0:T(8,128)(2,1)S(1)}, u32[]{:S(2)}, u32[]{:S(2)}) collective-permute-start(bf16[64,1024]{1,0:T(8,128)(2,1)S(1)} %collective-permute-done.4.refs_4_.refs_1_), channel_id=1, source_target_pairs={{0,16},{2,18},{4,20},{6,22},{8,24},{10,26},{12,28},{14,30},{16,0},... | collective-permute-start | bytes 393224 | tf_op jit(solution)/shard_map/ppermute | solution.py:50
  29.5 2.1 %collective-permute-done.2.refs_2_ = bf16[64,1024]{1,0:T(8,128)(2,1)S(1)} collective-permute-done((bf16[64,1024]{1,0:T(8,128)(2,1)S(1)}, bf16[64,1024]{1,0:T(8,128)(2,1)S(1)}, u32[]{:S(2)}, u32[]{:S(2)}) %collective-permute-start.2) | collective-permute-done | bytes 131104 | tf_op jit(solution)/shard_map/ppermute | solution.py:50
  34.4 6.5 %collective-permute-done.9.refs_1_ = bf16[64,1024]{1,0:T(8,128)(2,1)S(1)} collective-permute-done((bf16[64,1024]{1,0:T(8,128)(2,1)S(1)}, bf16[64,1024]{1,0:T(8,128)(2,1)S(1)}, u32[]{:S(2)}, u32[]{:S(2)}) %collective-permute-start.9) | collective-permute-done | bytes 131104 | tf_op jit(solution)/shard_map/ppermute | solution.py:50
  40.9 1.8 %collective-permute-done.6.refs_2_.refs_0_ = bf16[256,1024]{1,0:T(8,128)(2,1)S(1)} collective-permute-done((bf16[256,1024]{1,0:T(8,128)(2,1)S(1)}, bf16[256,1024]{1,0:T(8,128)(2,1)S(1)}, u32[]{:S(2)}, u32[]{:S(2)}) %collective-permute-start.6) | collective-permute-done | bytes 524320 | tf_op jit(solution)/shard_map/ppermute | solution.py:50
  44.9 1.7 %far_gate_up.1 = (f32[2,704,384]{2,1,0:T(8,128)S(1)}, bf16[2,704,384]{2,1,0:T(8,128)(2,1)S(1)}) custom-call(bf16[256,1024]{1,0:T(8,128)(2,1)S(1)} %collective-permute-done.6.refs_2_.refs_0_, bf16[256,1024]{1,0:T(8,128)(2,1)S(1)} %collective-permute-done.7.refs_3_.refs_1_, bf16[192,1024]{1,0:T(8,128)(2,1)S(1)} %far_corner.1.refs_4_.refs_2_, ...), custom_call_target="tpu_custom_call" | custom-call | flops 1107296256 | bytes 1000000 | tf_op jit(solution)/shard_map/far_gate_up/pallas_call | solution.py:100
  46.8 2.3 %collective-permute-start.12 = (bf16[16,1024]{1,0:T(8,128)(2,1)S(1)}, bf16[16,1024]{1,0:T(8,128)(2,1)S(1)}, u32[]{:S(2)}, u32[]{:S(2)}) collective-permute-start(bf16[16,1024]{1,0:T(8,128)(2,1)S(1)} %get-tuple-element.49), channel_id=1, source_target_pairs={{0,24},{2,26},{4,28},{6,30},{8,16},{10,18},{12,20},{14,22},{16,8},... | collective-permute-start | bytes 98312 | tf_op jit(solution)/shard_map/ppermute | solution.py:50
  49.1 2.1 %collective-permute-start.14 = (bf16[16,1024]{1,0:T(8,128)(2,1)S(1)}, bf16[16,1024]{1,0:T(8,128)(2,1)S(1)}, u32[]{:S(2)}, u32[]{:S(2)}) collective-permute-start(bf16[16,1024]{1,0:T(8,128)(2,1)S(1)} %get-tuple-element.49), channel_id=1, source_target_pairs={{0,8},{2,10},{4,12},{6,14},{8,0},{10,2},{12,4},{14,6},{16,24},{18,... | collective-permute-start | bytes 98312 | tf_op jit(solution)/shard_map/ppermute | solution.py:50
  51.2 1.1 %far_down.1 = (bf16[256,1024]{1,0:T(8,128)(2,1)S(1)}, bf16[256,1024]{1,0:T(8,128)(2,1)S(1)}, bf16[64,1024]{1,0:T(8,128)(2,1)S(1)}, bf16[64,1024]{1,0:T(8,128)(2,1)S(1)}, bf16[64,1024]{1,0:T(8,128)(2,1)S(1)}) custom-call(f32[2,704,384]{2,1,0:T(8,128)S(1)} %get-tuple-element.50.refs_0_, bf16[2,704,384]{2,1,0:T(8,128)(2,1)S(1)} %collective-permute-done.15.refs_1_, ...), custom_call_target="tpu_custom_call" | custom-call | flops 553648128 | bytes 1000000 | tf_op jit(solution)/shard_map/far_down/pallas_call | solution.py:100
  52.6 1.3 %collective-permute-done.13.refs_2_ = bf16[16,1024]{1,0:T(8,128)(2,1)S(1)} collective-permute-done((bf16[16,1024]{1,0:T(8,128)(2,1)S(1)}, bf16[16,1024]{1,0:T(8,128)(2,1)S(1)}, u32[]{:S(2)}, u32[]{:S(2)}) %collective-permute-start.13) | collective-permute-done | bytes 32800 | tf_op jit(solution)/shard_map/ppermute | solution.py:50
  54.0 1.6 %collective-permute-start.16 = (bf16[272,1024]{1,0:T(8,128)(2,1)S(1)}, bf16[272,1024]{1,0:T(8,128)(2,1)S(1)}, u32[]{:S(2)}, u32[]{:S(2)}) collective-permute-start(bf16[272,1024]{1,0:T(8,128)(2,1)S(1)} %get-tuple-element.55), channel_id=1, source_target_pairs={{0,2},{2,0},{4,6},{6,4},{8,10},{10,8},{12,14},{14,12},{16,18},{18,... | collective-permute-start | bytes 1671176 | tf_op jit(solution)/shard_map/ppermute | solution.py:50
  56.1 1.5 %collective-permute-start.18 = (bf16[16,1024]{1,0:T(8,128)(2,1)S(1)}, bf16[16,1024]{1,0:T(8,128)(2,1)S(1)}, u32[]{:S(2)}, u32[]{:S(2)}) collective-permute-start(bf16[16,1024]{1,0:T(8,128)(2,1)S(1)} %get-tuple-element.57), channel_id=1, source_target_pairs={{0,6},{2,4},{4,2},{6,0},{8,14},{10,12},{12,10},{14,8},{16,22},{18,... | collective-permute-start | bytes 98312 | tf_op jit(solution)/shard_map/ppermute | solution.py:50
  57.6 2.1 %collective-permute-start.20 = (bf16[64,1024]{1,0:T(8,128)(2,1)S(1)}, bf16[64,1024]{1,0:T(8,128)(2,1)S(1)}, u32[]{:S(2)}, u32[]{:S(2)}) collective-permute-start(bf16[64,1024]{1,0:T(8,128)(2,1)S(1)} %get-tuple-element.66), channel_id=1, source_target_pairs={{0,24},{2,26},{4,28},{6,30},{8,16},{10,18},{12,20},{14,22},{16,8},... | collective-permute-start | bytes 393224 | tf_op jit(solution)/shard_map/ppermute | solution.py:50
  60.2 8.4 %collective-permute-done.18.refs_4_ = bf16[16,1024]{1,0:T(8,128)(2,1)S(1)} collective-permute-done((bf16[16,1024]{1,0:T(8,128)(2,1)S(1)}, bf16[16,1024]{1,0:T(8,128)(2,1)S(1)}, u32[]{:S(2)}, u32[]{:S(2)}) %collective-permute-start.18) | collective-permute-done | bytes 32800 | tf_op jit(solution)/shard_map/ppermute | solution.py:50
  70.0 2.9 %collective-permute-start.24 = (bf16[64,1024]{1,0:T(8,128)(2,1)S(1)}, bf16[64,1024]{1,0:T(8,128)(2,1)S(1)}, u32[]{:S(2)}, u32[]{:S(2)}) collective-permute-start(bf16[64,1024]{1,0:T(8,128)(2,1)S(1)} %get-tuple-element.69), channel_id=1, source_target_pairs={{0,24},{2,26},{4,28},{6,30},{8,16},{10,18},{12,20},{14,22},{16,8},... | collective-permute-start | bytes 393224 | tf_op jit(solution)/shard_map/ppermute | solution.py:50
  73.5 5.4 %vocab_logits.1 = (f32[16,4748]{1,0:T(8,128)S(1)}, f32[32,1,128]{2,1,0:T(1,128)S(1)}) custom-call(f32[16,1024]{1,0:T(8,128)S(1)} %get-tuple-element.58.refs_0_, f32[16,1024]{1,0:T(8,128)S(1)} %collective-permute-done.19.refs_1_, f32[1,2048]{1,0:T(1,128)S(1)} %bitcast.12, bf16[4748,2048]{1,0:T(8,128)(2,1)S(1)} %bitcast.10), custom_call_target="tpu_custom_call" | custom-call | flops 311164928 | bytes 1000000 | tf_op jit(solution)/shard_map/vocab_logits/pallas_call | solution.py:100
  79.0 1.2 %collective-permute-start.26 = (bf16[64,1024]{1,0:T(8,128)(2,1)S(1)}, bf16[64,1024]{1,0:T(8,128)(2,1)S(1)}, u32[]{:S(2)}, u32[]{:S(2)}) collective-permute-start(bf16[64,1024]{1,0:T(8,128)(2,1)S(1)} %get-tuple-element.71), channel_id=1, source_target_pairs={{0,8},{2,10},{4,12},{6,14},{8,0},{10,2},{12,4},{14,6},{16,24},{18,... | collective-permute-start | bytes 393224 | tf_op jit(solution)/shard_map/ppermute | solution.py:50
  80.3 1.6 %collective-permute-start.23 = (bf16[64,1024]{1,0:T(8,128)(2,1)S(1)}, bf16[64,1024]{1,0:T(8,128)(2,1)S(1)}, u32[]{:S(2)}, u32[]{:S(2)}) collective-permute-start(bf16[64,1024]{1,0:T(8,128)(2,1)S(1)} %corner_sum.1), channel_id=1, source_target_pairs={{0,6},{2,4},{4,2},{6,0},{8,14},{10,12},{12,10},{14,8},{16,22},{18,... | collective-permute-start | bytes 393224 | tf_op jit(solution)/shard_map/ppermute | solution.py:50
  81.9 10.8 %all_to_all.5 = f32[32,1,128]{2,1,0:T(1,128)S(1)} all-to-all(f32[32,1,128]{2,1,0:T(1,128)S(1)} %get-tuple-element.60.refs_4_), channel_id=1, replica_groups=mesh['req'=16,'head'=2] {'req','head'}, dimensions={0} | all-to-all | bytes 32768 | tf_op jit(solution)/shard_map/all_to_all | solution.py:564
  (69 shorter events, 11.5 us)
Async XLA Ops:
  11.0 8.3 %collective-permute-start.4 = (bf16[64,1024]{1,0:T(8,128)(2,1)S(1)}, bf16[64,1024]{1,0:T(8,128)(2,1)S(1)}, u32[]{:S(2)}, u32[]{:S(2)}) collective-permute-start(bf16[64,1024]{1,0:T(8,128)(2,1)S(1)} %get-tuple-element.39.refs_0_), channel_id=1, source_target_pairs={{0,6},{2,4},{4,2},{6,0},{8,14},{10,12},{12,10},{14,8},{16,22},{18,... | collective-permute-start | bytes 393224 | tf_op jit(solution)/shard_map/ppermute | solution.py:50
  14.9 8.2 %collective-permute-start.1 = (bf16[64,1024]{1,0:T(8,128)(2,1)S(1)}, bf16[64,1024]{1,0:T(8,128)(2,1)S(1)}, u32[]{:S(2)}, u32[]{:S(2)}) collective-permute-start(bf16[64,1024]{1,0:T(8,128)(2,1)S(1)} %get-tuple-element.39.refs_0_), channel_id=1, source_target_pairs={{0,24},{2,26},{4,28},{6,30},{8,16},{10,18},{12,20},{14,22},{16,8},... | collective-permute-start | bytes 393224 | tf_op jit(solution)/shard_map/ppermute | solution.py:50
  18.5 13.1 %collective-permute-start.2 = (bf16[64,1024]{1,0:T(8,128)(2,1)S(1)}, bf16[64,1024]{1,0:T(8,128)(2,1)S(1)}, u32[]{:S(2)}, u32[]{:S(2)}) collective-permute-start(bf16[64,1024]{1,0:T(8,128)(2,1)S(1)} %get-tuple-element.39.refs_0_), channel_id=1, source_target_pairs={{0,16},{2,18},{4,20},{6,22},{8,24},{10,26},{12,28},{14,30},{16,0},... | collective-permute-start | bytes 393224 | tf_op jit(solution)/shard_map/ppermute | solution.py:50
  18.5 13.1 %collective-permute-start.3 = (bf16[64,1024]{1,0:T(8,128)(2,1)S(1)}, bf16[64,1024]{1,0:T(8,128)(2,1)S(1)}, u32[]{:S(2)}, u32[]{:S(2)}) collective-permute-start(bf16[64,1024]{1,0:T(8,128)(2,1)S(1)} %get-tuple-element.39.refs_0_), channel_id=1, source_target_pairs={{0,8},{2,10},{4,12},{6,14},{8,0},{10,2},{12,4},{14,6},{16,24},{18,... | collective-permute-start | bytes 393224 | tf_op jit(solution)/shard_map/ppermute | solution.py:50
  19.3 14.2 %collective-permute-start.10 = (bf16[64,1024]{1,0:T(8,128)(2,1)S(1)}, bf16[64,1024]{1,0:T(8,128)(2,1)S(1)}, u32[]{:S(2)}, u32[]{:S(2)}) collective-permute-start(bf16[64,1024]{1,0:T(8,128)(2,1)S(1)} %collective-permute-done.4.refs_4_.refs_1_), channel_id=1, source_target_pairs={{0,8},{2,10},{4,12},{6,14},{8,0},{10,2},{12,4},{14,6},{16,24},{18,... | collective-permute-start | bytes 393224 | tf_op jit(solution)/shard_map/ppermute | solution.py:50
  20.5 13.9 %collective-permute-start.8 = (bf16[64,1024]{1,0:T(8,128)(2,1)S(1)}, bf16[64,1024]{1,0:T(8,128)(2,1)S(1)}, u32[]{:S(2)}, u32[]{:S(2)}) collective-permute-start(bf16[64,1024]{1,0:T(8,128)(2,1)S(1)} %collective-permute-done.4.refs_4_.refs_1_), channel_id=1, source_target_pairs={{0,24},{2,26},{4,28},{6,30},{8,16},{10,18},{12,20},{14,22},{16,8},... | collective-permute-start | bytes 393224 | tf_op jit(solution)/shard_map/ppermute | solution.py:50
  23.1 17.7 %collective-permute-start.9 = (bf16[64,1024]{1,0:T(8,128)(2,1)S(1)}, bf16[64,1024]{1,0:T(8,128)(2,1)S(1)}, u32[]{:S(2)}, u32[]{:S(2)}) collective-permute-start(bf16[64,1024]{1,0:T(8,128)(2,1)S(1)} %collective-permute-done.4.refs_4_.refs_1_), channel_id=1, source_target_pairs={{0,16},{2,18},{4,20},{6,22},{8,24},{10,26},{12,28},{14,30},{16,0},... | collective-permute-start | bytes 393224 | tf_op jit(solution)/shard_map/ppermute | solution.py:50
  31.6 11.1 %collective-permute-start.6 = (bf16[256,1024]{1,0:T(8,128)(2,1)S(1)}, bf16[256,1024]{1,0:T(8,128)(2,1)S(1)}, u32[]{:S(2)}, u32[]{:S(2)}) collective-permute-start(bf16[256,1024]{1,0:T(8,128)(2,1)S(1)} %column.1.refs_0_), channel_id=1, source_target_pairs={{0,2},{2,0},{4,6},{6,4},{8,10},{10,8},{12,14},{14,12},{16,18},{18,... | collective-permute-start | bytes 1572872 | tf_op jit(solution)/shard_map/ppermute | solution.py:50
  32.2 10.8 %collective-permute-start.7 = (bf16[256,1024]{1,0:T(8,128)(2,1)S(1)}, bf16[256,1024]{1,0:T(8,128)(2,1)S(1)}, u32[]{:S(2)}, u32[]{:S(2)}) collective-permute-start(bf16[256,1024]{1,0:T(8,128)(2,1)S(1)} %column.1.refs_0_), channel_id=1, source_target_pairs={{0,4},{2,6},{4,0},{6,2},{8,12},{10,14},{12,8},{14,10},{16,20},{18,... | collective-permute-start | bytes 1572872 | tf_op jit(solution)/shard_map/ppermute | solution.py:50
  33.4 10.0 %collective-permute-start.5 = (bf16[2,320,384]{2,1,0:T(8,128)(2,1)S(1)}, bf16[2,320,384]{2,1,0:T(8,128)(2,1)S(1)}, u32[]{:S(2)}, u32[]{:S(2)}) collective-permute-start(bf16[2,320,384]{2,1,0:T(8,128)(2,1)S(1)} %get-tuple-element.41), channel_id=1, source_target_pairs={{0,1},{1,0},{2,3},{3,2},{4,5},{5,4},{6,7},{7,6},{8,9},{9,8},{10,11... | collective-permute-start | bytes 1474568 | tf_op jit(solution)/shard_map/ppermute | solution.py:88
  46.5 4.6 %collective-permute-start.15 = (bf16[2,704,384]{2,1,0:T(8,128)(2,1)S(1)}, bf16[2,704,384]{2,1,0:T(8,128)(2,1)S(1)}, u32[]{:S(2)}, u32[]{:S(2)}) collective-permute-start(bf16[2,704,384]{2,1,0:T(8,128)(2,1)S(1)} %get-tuple-element.51), channel_id=1, source_target_pairs={{0,1},{1,0},{2,3},{3,2},{4,5},{5,4},{6,7},{7,6},{8,9},{9,8},{10,11... | collective-permute-start | bytes 3244040 | tf_op jit(solution)/shard_map/ppermute | solution.py:88
  46.8 5.8 %collective-permute-start.12 = (bf16[16,1024]{1,0:T(8,128)(2,1)S(1)}, bf16[16,1024]{1,0:T(8,128)(2,1)S(1)}, u32[]{:S(2)}, u32[]{:S(2)}) collective-permute-start(bf16[16,1024]{1,0:T(8,128)(2,1)S(1)} %get-tuple-element.49), channel_id=1, source_target_pairs={{0,24},{2,26},{4,28},{6,30},{8,16},{10,18},{12,20},{14,22},{16,8},... | collective-permute-start | bytes 98312 | tf_op jit(solution)/shard_map/ppermute | solution.py:50
  49.1 4.8 %collective-permute-start.13 = (bf16[16,1024]{1,0:T(8,128)(2,1)S(1)}, bf16[16,1024]{1,0:T(8,128)(2,1)S(1)}, u32[]{:S(2)}, u32[]{:S(2)}) collective-permute-start(bf16[16,1024]{1,0:T(8,128)(2,1)S(1)} %get-tuple-element.49), channel_id=1, source_target_pairs={{0,16},{2,18},{4,20},{6,22},{8,24},{10,26},{12,28},{14,30},{16,0},... | collective-permute-start | bytes 98312 | tf_op jit(solution)/shard_map/ppermute | solution.py:50
  49.1 4.8 %collective-permute-start.14 = (bf16[16,1024]{1,0:T(8,128)(2,1)S(1)}, bf16[16,1024]{1,0:T(8,128)(2,1)S(1)}, u32[]{:S(2)}, u32[]{:S(2)}) collective-permute-start(bf16[16,1024]{1,0:T(8,128)(2,1)S(1)} %get-tuple-element.49), channel_id=1, source_target_pairs={{0,8},{2,10},{4,12},{6,14},{8,0},{10,2},{12,4},{14,6},{16,24},{18,... | collective-permute-start | bytes 98312 | tf_op jit(solution)/shard_map/ppermute | solution.py:50
  54.0 15.1 %collective-permute-start.16 = (bf16[272,1024]{1,0:T(8,128)(2,1)S(1)}, bf16[272,1024]{1,0:T(8,128)(2,1)S(1)}, u32[]{:S(2)}, u32[]{:S(2)}) collective-permute-start(bf16[272,1024]{1,0:T(8,128)(2,1)S(1)} %get-tuple-element.55), channel_id=1, source_target_pairs={{0,2},{2,0},{4,6},{6,4},{8,10},{10,8},{12,14},{14,12},{16,18},{18,... | collective-permute-start | bytes 1671176 | tf_op jit(solution)/shard_map/ppermute | solution.py:50
  55.6 14.2 %collective-permute-start.17 = (bf16[272,1024]{1,0:T(8,128)(2,1)S(1)}, bf16[272,1024]{1,0:T(8,128)(2,1)S(1)}, u32[]{:S(2)}, u32[]{:S(2)}) collective-permute-start(bf16[272,1024]{1,0:T(8,128)(2,1)S(1)} %get-tuple-element.56), channel_id=1, source_target_pairs={{0,4},{2,6},{4,0},{6,2},{8,12},{10,14},{12,8},{14,10},{16,20},{18,... | collective-permute-start | bytes 1671176 | tf_op jit(solution)/shard_map/ppermute | solution.py:50
  56.1 12.5 %collective-permute-start.18 = (bf16[16,1024]{1,0:T(8,128)(2,1)S(1)}, bf16[16,1024]{1,0:T(8,128)(2,1)S(1)}, u32[]{:S(2)}, u32[]{:S(2)}) collective-permute-start(bf16[16,1024]{1,0:T(8,128)(2,1)S(1)} %get-tuple-element.57), channel_id=1, source_target_pairs={{0,6},{2,4},{4,2},{6,0},{8,14},{10,12},{12,10},{14,8},{16,22},{18,... | collective-permute-start | bytes 98312 | tf_op jit(solution)/shard_map/ppermute | solution.py:50
  57.6 21.4 %collective-permute-start.20 = (bf16[64,1024]{1,0:T(8,128)(2,1)S(1)}, bf16[64,1024]{1,0:T(8,128)(2,1)S(1)}, u32[]{:S(2)}, u32[]{:S(2)}) collective-permute-start(bf16[64,1024]{1,0:T(8,128)(2,1)S(1)} %get-tuple-element.66), channel_id=1, source_target_pairs={{0,24},{2,26},{4,28},{6,30},{8,16},{10,18},{12,20},{14,22},{16,8},... | collective-permute-start | bytes 393224 | tf_op jit(solution)/shard_map/ppermute | solution.py:50
  59.6 20.6 %collective-permute-start.21 = (bf16[64,1024]{1,0:T(8,128)(2,1)S(1)}, bf16[64,1024]{1,0:T(8,128)(2,1)S(1)}, u32[]{:S(2)}, u32[]{:S(2)}) collective-permute-start(bf16[64,1024]{1,0:T(8,128)(2,1)S(1)} %get-tuple-element.67), channel_id=1, source_target_pairs={{0,16},{2,18},{4,20},{6,22},{8,24},{10,26},{12,28},{14,30},{16,0},... | collective-permute-start | bytes 393224 | tf_op jit(solution)/shard_map/ppermute | solution.py:50
  68.5 11.7 %collective-permute-start.22 = (bf16[64,1024]{1,0:T(8,128)(2,1)S(1)}, bf16[64,1024]{1,0:T(8,128)(2,1)S(1)}, u32[]{:S(2)}, u32[]{:S(2)}) collective-permute-start(bf16[64,1024]{1,0:T(8,128)(2,1)S(1)} %get-tuple-element.68), channel_id=1, source_target_pairs={{0,8},{2,10},{4,12},{6,14},{8,0},{10,2},{12,4},{14,6},{16,24},{18,... | collective-permute-start | bytes 393224 | tf_op jit(solution)/shard_map/ppermute | solution.py:50
  70.0 22.7 %collective-permute-start.24 = (bf16[64,1024]{1,0:T(8,128)(2,1)S(1)}, bf16[64,1024]{1,0:T(8,128)(2,1)S(1)}, u32[]{:S(2)}, u32[]{:S(2)}) collective-permute-start(bf16[64,1024]{1,0:T(8,128)(2,1)S(1)} %get-tuple-element.69), channel_id=1, source_target_pairs={{0,24},{2,26},{4,28},{6,30},{8,16},{10,18},{12,20},{14,22},{16,8},... | collective-permute-start | bytes 393224 | tf_op jit(solution)/shard_map/ppermute | solution.py:50
  72.9 19.8 %collective-permute-start.25 = (bf16[64,1024]{1,0:T(8,128)(2,1)S(1)}, bf16[64,1024]{1,0:T(8,128)(2,1)S(1)}, u32[]{:S(2)}, u32[]{:S(2)}) collective-permute-start(bf16[64,1024]{1,0:T(8,128)(2,1)S(1)} %get-tuple-element.70), channel_id=1, source_target_pairs={{0,16},{2,18},{4,20},{6,22},{8,24},{10,26},{12,28},{14,30},{16,0},... | collective-permute-start | bytes 393224 | tf_op jit(solution)/shard_map/ppermute | solution.py:50
  79.0 13.7 %collective-permute-start.26 = (bf16[64,1024]{1,0:T(8,128)(2,1)S(1)}, bf16[64,1024]{1,0:T(8,128)(2,1)S(1)}, u32[]{:S(2)}, u32[]{:S(2)}) collective-permute-start(bf16[64,1024]{1,0:T(8,128)(2,1)S(1)} %get-tuple-element.71), channel_id=1, source_target_pairs={{0,8},{2,10},{4,12},{6,14},{8,0},{10,2},{12,4},{14,6},{16,24},{18,... | collective-permute-start | bytes 393224 | tf_op jit(solution)/shard_map/ppermute | solution.py:50
  80.3 12.4 %collective-permute-start.23 = (bf16[64,1024]{1,0:T(8,128)(2,1)S(1)}, bf16[64,1024]{1,0:T(8,128)(2,1)S(1)}, u32[]{:S(2)}, u32[]{:S(2)}) collective-permute-start(bf16[64,1024]{1,0:T(8,128)(2,1)S(1)} %corner_sum.1), channel_id=1, source_target_pairs={{0,6},{2,4},{4,2},{6,0},{8,14},{10,12},{12,10},{14,8},{16,22},{18,... | collective-permute-start | bytes 393224 | tf_op jit(solution)/shard_map/ppermute | solution.py:50
  (14 other events, 250.1 us)

commit v5 on v4

--- a/solution.py
+++ b/solution.py
@@ -17,7 +17,7 @@
 VMEM_SPEC = pl.BlockSpec(memory_space=pltpu.VMEM)
 LOG2E = 1.4426950408889634
 SHIFT = 4.0
-QUERY_PARTS, CACHE_PARTS, OUT_PARTS = 4, 4, 4
+QUERY_PARTS, CACHE_PARTS, OUT_PARTS = 4, 1, 4
 
 
 def sizes_of(count):

time: 93.8 us -> 92.6 us (0.987)
  Pallas kernels: 20.4 us -> 19.2 us
    pallas_call x1, Pallas kernels: 8.25 us -> 7.03 us  [attention_rows(): pl.pallas_call(attention_kernel, out_shape=(pltpu.VMEM((rows, width), jnp...]
  transfers between devices with their start and end apart: 27 -> 27, of which waited for: 12 -> 12; matrix products, arithmetic and copies ran while one was open for 0% -> 0% of each run, Pallas kernels for 9% -> 10%
where the time goes in v5:
time: 92.6 us; the launch traced here: 92.4 us
  starting transfers between devices  37.7 us (41%)
  waiting for transfers between devices  23.9 us (26%)
  Pallas kernels  19.2 us (21%)
  blocking collectives  10.8 us (12%)
    ppermute x22, starting transfers between devices, send(): return lax.ppermute(rows, 'req', pairs)  36.7 us
    ppermute x22, waiting for transfers between devices, send(): return lax.ppermute(rows, 'req', pairs)  22.2 us
    pallas_call x14, Pallas kernels, kernel_call(): pl.pallas_call(run, out_shape=tuple(((pltpu.VMEM if pinned else jax.Shape...  12.1 us
    all_to_all x1, blocking collectives, on_device(): everyone = lax.all_to_all(stats, ('req', 'head'), 0, 0, tiled=True)  10.8 us
    pallas_call x1, Pallas kernels, attention_rows(): pl.pallas_call(attention_kernel, out_shape=(pltpu.VMEM((rows, width), jnp...  7.03 us
  transfers between devices with their start and end apart: 27, of which 12 were waited for; matrix products, arithmetic and copies ran while one was open for 0% of the time, Pallas kernels for 10%

profile of v5, /device:TPU:0, one launch (start us, length us, event | category | flops | bytes accessed | tf_op | source)
XLA Modules:
  0.0 92.4 jit_solution(5005351151612972594)
XLA Ops:
  0.6 7.0 %attention_rows.1 = (f32[64,2048]{1,0:T(8,128)S(1)}, bf16[64,2048]{1,0:T(8,128)(2,1)S(1)}) custom-call(s32[16]{0:T(128)} %lengths_any.1, s32[16]{0:T(128)} %requests_any.1, bf16[64,2048]{1,0:T(8,128)(2,1)} %hidden_any.1, f32[1,2048]{1,0:T(1,128)} %bitcast.16, f32[1,128]{1,0:T(1,128)} %bitcast.17, f32[1,128]{1,0:T(1,128)} %bitcast.18, ...), custom_call_target="tpu_custom_call" | custom-call | flops 1400000000 | bytes 17500000 | tf_op jit(solution)/shard_map/attention_rows/pallas_call | solution.py:266
  8.2 1.2 %collective-permute-done.refs_1_ = bf16[64,2048]{1,0:T(8,128)(2,1)S(1)} collective-permute-done((bf16[64,2048]{1,0:T(8,128)(2,1)S(1)}, bf16[64,2048]{1,0:T(8,128)(2,1)S(1)}, u32[]{:S(2)}, u32[]{:S(2)}) %collective-permute-start) | collective-permute-done | bytes 262176 | tf_op jit(solution)/shard_map/ppermute | solution.py:88
  9.8 3.9 %collective-permute-start.4 = (bf16[64,1024]{1,0:T(8,128)(2,1)S(1)}, bf16[64,1024]{1,0:T(8,128)(2,1)S(1)}, u32[]{:S(2)}, u32[]{:S(2)}) collective-permute-start(bf16[64,1024]{1,0:T(8,128)(2,1)S(1)} %get-tuple-element.39.refs_0_), channel_id=1, source_target_pairs={{0,6},{2,4},{4,2},{6,0},{8,14},{10,12},{12,10},{14,8},{16,22},{18,... | collective-permute-start | bytes 393224 | tf_op jit(solution)/shard_map/ppermute | solution.py:50
  13.6 3.6 %collective-permute-start.1 = (bf16[64,1024]{1,0:T(8,128)(2,1)S(1)}, bf16[64,1024]{1,0:T(8,128)(2,1)S(1)}, u32[]{:S(2)}, u32[]{:S(2)}) collective-permute-start(bf16[64,1024]{1,0:T(8,128)(2,1)S(1)} %get-tuple-element.39.refs_0_), channel_id=1, source_target_pairs={{0,24},{2,26},{4,28},{6,30},{8,16},{10,18},{12,20},{14,22},{16,8},... | collective-permute-start | bytes 393224 | tf_op jit(solution)/shard_map/ppermute | solution.py:50
  18.0 1.2 %collective-permute-start.10 = (bf16[64,1024]{1,0:T(8,128)(2,1)S(1)}, bf16[64,1024]{1,0:T(8,128)(2,1)S(1)}, u32[]{:S(2)}, u32[]{:S(2)}) collective-permute-start(bf16[64,1024]{1,0:T(8,128)(2,1)S(1)} %collective-permute-done.4.refs_4_.refs_1_), channel_id=1, source_target_pairs={{0,8},{2,10},{4,12},{6,14},{8,0},{10,2},{12,4},{14,6},{16,24},{18,... | collective-permute-start | bytes 393224 | tf_op jit(solution)/shard_map/ppermute | solution.py:50
  19.3 2.4 %collective-permute-start.8 = (bf16[64,1024]{1,0:T(8,128)(2,1)S(1)}, bf16[64,1024]{1,0:T(8,128)(2,1)S(1)}, u32[]{:S(2)}, u32[]{:S(2)}) collective-permute-start(bf16[64,1024]{1,0:T(8,128)(2,1)S(1)} %collective-permute-done.4.refs_4_.refs_1_), channel_id=1, source_target_pairs={{0,24},{2,26},{4,28},{6,30},{8,16},{10,18},{12,20},{14,22},{16,8},... | collective-permute-start | bytes 393224 | tf_op jit(solution)/shard_map/ppermute | solution.py:50
  21.9 6.4 %collective-permute-start.9 = (bf16[64,1024]{1,0:T(8,128)(2,1)S(1)}, bf16[64,1024]{1,0:T(8,128)(2,1)S(1)}, u32[]{:S(2)}, u32[]{:S(2)}) collective-permute-start(bf16[64,1024]{1,0:T(8,128)(2,1)S(1)} %collective-permute-done.4.refs_4_.refs_1_), channel_id=1, source_target_pairs={{0,16},{2,18},{4,20},{6,22},{8,24},{10,26},{12,28},{14,30},{16,0},... | collective-permute-start | bytes 393224 | tf_op jit(solution)/shard_map/ppermute | solution.py:50
  28.2 2.1 %collective-permute-done.2.refs_2_ = bf16[64,1024]{1,0:T(8,128)(2,1)S(1)} collective-permute-done((bf16[64,1024]{1,0:T(8,128)(2,1)S(1)}, bf16[64,1024]{1,0:T(8,128)(2,1)S(1)}, u32[]{:S(2)}, u32[]{:S(2)}) %collective-permute-start.2) | collective-permute-done | bytes 131104 | tf_op jit(solution)/shard_map/ppermute | solution.py:50
  33.2 6.4 %collective-permute-done.9.refs_1_ = bf16[64,1024]{1,0:T(8,128)(2,1)S(1)} collective-permute-done((bf16[64,1024]{1,0:T(8,128)(2,1)S(1)}, bf16[64,1024]{1,0:T(8,128)(2,1)S(1)}, u32[]{:S(2)}, u32[]{:S(2)}) %collective-permute-start.9) | collective-permute-done | bytes 131104 | tf_op jit(solution)/shard_map/ppermute | solution.py:50
  39.7 1.8 %collective-permute-done.6.refs_2_.refs_0_ = bf16[256,1024]{1,0:T(8,128)(2,1)S(1)} collective-permute-done((bf16[256,1024]{1,0:T(8,128)(2,1)S(1)}, bf16[256,1024]{1,0:T(8,128)(2,1)S(1)}, u32[]{:S(2)}, u32[]{:S(2)}) %collective-permute-start.6) | collective-permute-done | bytes 524320 | tf_op jit(solution)/shard_map/ppermute | solution.py:50
  43.6 1.7 %far_gate_up.1 = (f32[2,704,384]{2,1,0:T(8,128)S(1)}, bf16[2,704,384]{2,1,0:T(8,128)(2,1)S(1)}) custom-call(bf16[256,1024]{1,0:T(8,128)(2,1)S(1)} %collective-permute-done.6.refs_2_.refs_0_, bf16[256,1024]{1,0:T(8,128)(2,1)S(1)} %collective-permute-done.7.refs_3_.refs_1_, bf16[192,1024]{1,0:T(8,128)(2,1)S(1)} %far_corner.1.refs_4_.refs_2_, ...), custom_call_target="tpu_custom_call" | custom-call | flops 1107296256 | bytes 1000000 | tf_op jit(solution)/shard_map/far_gate_up/pallas_call | solution.py:100
  45.5 2.3 %collective-permute-start.12 = (bf16[16,1024]{1,0:T(8,128)(2,1)S(1)}, bf16[16,1024]{1,0:T(8,128)(2,1)S(1)}, u32[]{:S(2)}, u32[]{:S(2)}) collective-permute-start(bf16[16,1024]{1,0:T(8,128)(2,1)S(1)} %get-tuple-element.49), channel_id=1, source_target_pairs={{0,24},{2,26},{4,28},{6,30},{8,16},{10,18},{12,20},{14,22},{16,8},... | collective-permute-start | bytes 98312 | tf_op jit(solution)/shard_map/ppermute | solution.py:50
  47.9 2.1 %collective-permute-start.14 = (bf16[16,1024]{1,0:T(8,128)(2,1)S(1)}, bf16[16,1024]{1,0:T(8,128)(2,1)S(1)}, u32[]{:S(2)}, u32[]{:S(2)}) collective-permute-start(bf16[16,1024]{1,0:T(8,128)(2,1)S(1)} %get-tuple-element.49), channel_id=1, source_target_pairs={{0,8},{2,10},{4,12},{6,14},{8,0},{10,2},{12,4},{14,6},{16,24},{18,... | collective-permute-start | bytes 98312 | tf_op jit(solution)/shard_map/ppermute | solution.py:50
  49.9 1.1 %far_down.1 = (bf16[256,1024]{1,0:T(8,128)(2,1)S(1)}, bf16[256,1024]{1,0:T(8,128)(2,1)S(1)}, bf16[64,1024]{1,0:T(8,128)(2,1)S(1)}, bf16[64,1024]{1,0:T(8,128)(2,1)S(1)}, bf16[64,1024]{1,0:T(8,128)(2,1)S(1)}) custom-call(f32[2,704,384]{2,1,0:T(8,128)S(1)} %get-tuple-element.50.refs_0_, bf16[2,704,384]{2,1,0:T(8,128)(2,1)S(1)} %collective-permute-done.15.refs_1_, ...), custom_call_target="tpu_custom_call" | custom-call | flops 553648128 | bytes 1000000 | tf_op jit(solution)/shard_map/far_down/pallas_call | solution.py:100
  51.3 1.3 %collective-permute-done.13.refs_2_ = bf16[16,1024]{1,0:T(8,128)(2,1)S(1)} collective-permute-done((bf16[16,1024]{1,0:T(8,128)(2,1)S(1)}, bf16[16,1024]{1,0:T(8,128)(2,1)S(1)}, u32[]{:S(2)}, u32[]{:S(2)}) %collective-permute-start.13) | collective-permute-done | bytes 32800 | tf_op jit(solution)/shard_map/ppermute | solution.py:50
  52.8 1.6 %collective-permute-start.16 = (bf16[272,1024]{1,0:T(8,128)(2,1)S(1)}, bf16[272,1024]{1,0:T(8,128)(2,1)S(1)}, u32[]{:S(2)}, u32[]{:S(2)}) collective-permute-start(bf16[272,1024]{1,0:T(8,128)(2,1)S(1)} %get-tuple-element.55), channel_id=1, source_target_pairs={{0,2},{2,0},{4,6},{6,4},{8,10},{10,8},{12,14},{14,12},{16,18},{18,... | collective-permute-start | bytes 1671176 | tf_op jit(solution)/shard_map/ppermute | solution.py:50
  54.8 1.5 %collective-permute-start.18 = (bf16[16,1024]{1,0:T(8,128)(2,1)S(1)}, bf16[16,1024]{1,0:T(8,128)(2,1)S(1)}, u32[]{:S(2)}, u32[]{:S(2)}) collective-permute-start(bf16[16,1024]{1,0:T(8,128)(2,1)S(1)} %get-tuple-element.57), channel_id=1, source_target_pairs={{0,6},{2,4},{4,2},{6,0},{8,14},{10,12},{12,10},{14,8},{16,22},{18,... | collective-permute-start | bytes 98312 | tf_op jit(solution)/shard_map/ppermute | solution.py:50
  56.3 2.1 %collective-permute-start.20 = (bf16[64,1024]{1,0:T(8,128)(2,1)S(1)}, bf16[64,1024]{1,0:T(8,128)(2,1)S(1)}, u32[]{:S(2)}, u32[]{:S(2)}) collective-permute-start(bf16[64,1024]{1,0:T(8,128)(2,1)S(1)} %get-tuple-element.66), channel_id=1, source_target_pairs={{0,24},{2,26},{4,28},{6,30},{8,16},{10,18},{12,20},{14,22},{16,8},... | collective-permute-start | bytes 393224 | tf_op jit(solution)/shard_map/ppermute | solution.py:50
  59.0 8.4 %collective-permute-done.18.refs_4_ = bf16[16,1024]{1,0:T(8,128)(2,1)S(1)} collective-permute-done((bf16[16,1024]{1,0:T(8,128)(2,1)S(1)}, bf16[16,1024]{1,0:T(8,128)(2,1)S(1)}, u32[]{:S(2)}, u32[]{:S(2)}) %collective-permute-start.18) | collective-permute-done | bytes 32800 | tf_op jit(solution)/shard_map/ppermute | solution.py:50
  68.7 2.9 %collective-permute-start.24 = (bf16[64,1024]{1,0:T(8,128)(2,1)S(1)}, bf16[64,1024]{1,0:T(8,128)(2,1)S(1)}, u32[]{:S(2)}, u32[]{:S(2)}) collective-permute-start(bf16[64,1024]{1,0:T(8,128)(2,1)S(1)} %get-tuple-element.69), channel_id=1, source_target_pairs={{0,24},{2,26},{4,28},{6,30},{8,16},{10,18},{12,20},{14,22},{16,8},... | collective-permute-start | bytes 393224 | tf_op jit(solution)/shard_map/ppermute | solution.py:50
  72.3 5.4 %vocab_logits.1 = (f32[16,4748]{1,0:T(8,128)S(1)}, f32[32,1,128]{2,1,0:T(1,128)S(1)}) custom-call(f32[16,1024]{1,0:T(8,128)S(1)} %get-tuple-element.58.refs_0_, f32[16,1024]{1,0:T(8,128)S(1)} %collective-permute-done.19.refs_1_, f32[1,2048]{1,0:T(1,128)S(1)} %bitcast.12, bf16[4748,2048]{1,0:T(8,128)(2,1)S(1)} %bitcast.10), custom_call_target="tpu_custom_call" | custom-call | flops 311164928 | bytes 1000000 | tf_op jit(solution)/shard_map/vocab_logits/pallas_call | solution.py:100
  77.8 1.2 %collective-permute-start.26 = (bf16[64,1024]{1,0:T(8,128)(2,1)S(1)}, bf16[64,1024]{1,0:T(8,128)(2,1)S(1)}, u32[]{:S(2)}, u32[]{:S(2)}) collective-permute-start(bf16[64,1024]{1,0:T(8,128)(2,1)S(1)} %get-tuple-element.71), channel_id=1, source_target_pairs={{0,8},{2,10},{4,12},{6,14},{8,0},{10,2},{12,4},{14,6},{16,24},{18,... | collective-permute-start | bytes 393224 | tf_op jit(solution)/shard_map/ppermute | solution.py:50
  79.0 1.6 %collective-permute-start.23 = (bf16[64,1024]{1,0:T(8,128)(2,1)S(1)}, bf16[64,1024]{1,0:T(8,128)(2,1)S(1)}, u32[]{:S(2)}, u32[]{:S(2)}) collective-permute-start(bf16[64,1024]{1,0:T(8,128)(2,1)S(1)} %corner_sum.1), channel_id=1, source_target_pairs={{0,6},{2,4},{4,2},{6,0},{8,14},{10,12},{12,10},{14,8},{16,22},{18,... | collective-permute-start | bytes 393224 | tf_op jit(solution)/shard_map/ppermute | solution.py:50
  80.7 10.8 %all_to_all.5 = f32[32,1,128]{2,1,0:T(1,128)S(1)} all-to-all(f32[32,1,128]{2,1,0:T(1,128)S(1)} %get-tuple-element.60.refs_4_), channel_id=1, replica_groups=mesh['req'=16,'head'=2] {'req','head'}, dimensions={0} | all-to-all | bytes 32768 | tf_op jit(solution)/shard_map/all_to_all | solution.py:564
  (69 shorter events, 11.5 us)
Async XLA Ops:
  9.8 8.3 %collective-permute-start.4 = (bf16[64,1024]{1,0:T(8,128)(2,1)S(1)}, bf16[64,1024]{1,0:T(8,128)(2,1)S(1)}, u32[]{:S(2)}, u32[]{:S(2)}) collective-permute-start(bf16[64,1024]{1,0:T(8,128)(2,1)S(1)} %get-tuple-element.39.refs_0_), channel_id=1, source_target_pairs={{0,6},{2,4},{4,2},{6,0},{8,14},{10,12},{12,10},{14,8},{16,22},{18,... | collective-permute-start | bytes 393224 | tf_op jit(solution)/shard_map/ppermute | solution.py:50
  13.6 8.2 %collective-permute-start.1 = (bf16[64,1024]{1,0:T(8,128)(2,1)S(1)}, bf16[64,1024]{1,0:T(8,128)(2,1)S(1)}, u32[]{:S(2)}, u32[]{:S(2)}) collective-permute-start(bf16[64,1024]{1,0:T(8,128)(2,1)S(1)} %get-tuple-element.39.refs_0_), channel_id=1, source_target_pairs={{0,24},{2,26},{4,28},{6,30},{8,16},{10,18},{12,20},{14,22},{16,8},... | collective-permute-start | bytes 393224 | tf_op jit(solution)/shard_map/ppermute | solution.py:50
  17.2 13.1 %collective-permute-start.2 = (bf16[64,1024]{1,0:T(8,128)(2,1)S(1)}, bf16[64,1024]{1,0:T(8,128)(2,1)S(1)}, u32[]{:S(2)}, u32[]{:S(2)}) collective-permute-start(bf16[64,1024]{1,0:T(8,128)(2,1)S(1)} %get-tuple-element.39.refs_0_), channel_id=1, source_target_pairs={{0,16},{2,18},{4,20},{6,22},{8,24},{10,26},{12,28},{14,30},{16,0},... | collective-permute-start | bytes 393224 | tf_op jit(solution)/shard_map/ppermute | solution.py:50
  17.3 13.1 %collective-permute-start.3 = (bf16[64,1024]{1,0:T(8,128)(2,1)S(1)}, bf16[64,1024]{1,0:T(8,128)(2,1)S(1)}, u32[]{:S(2)}, u32[]{:S(2)}) collective-permute-start(bf16[64,1024]{1,0:T(8,128)(2,1)S(1)} %get-tuple-element.39.refs_0_), channel_id=1, source_target_pairs={{0,8},{2,10},{4,12},{6,14},{8,0},{10,2},{12,4},{14,6},{16,24},{18,... | collective-permute-start | bytes 393224 | tf_op jit(solution)/shard_map/ppermute | solution.py:50
  18.0 14.2 %collective-permute-start.10 = (bf16[64,1024]{1,0:T(8,128)(2,1)S(1)}, bf16[64,1024]{1,0:T(8,128)(2,1)S(1)}, u32[]{:S(2)}, u32[]{:S(2)}) collective-permute-start(bf16[64,1024]{1,0:T(8,128)(2,1)S(1)} %collective-permute-done.4.refs_4_.refs_1_), channel_id=1, source_target_pairs={{0,8},{2,10},{4,12},{6,14},{8,0},{10,2},{12,4},{14,6},{16,24},{18,... | collective-permute-start | bytes 393224 | tf_op jit(solution)/shard_map/ppermute | solution.py:50
  19.3 13.9 %collective-permute-start.8 = (bf16[64,1024]{1,0:T(8,128)(2,1)S(1)}, bf16[64,1024]{1,0:T(8,128)(2,1)S(1)}, u32[]{:S(2)}, u32[]{:S(2)}) collective-permute-start(bf16[64,1024]{1,0:T(8,128)(2,1)S(1)} %collective-permute-done.4.refs_4_.refs_1_), channel_id=1, source_target_pairs={{0,24},{2,26},{4,28},{6,30},{8,16},{10,18},{12,20},{14,22},{16,8},... | collective-permute-start | bytes 393224 | tf_op jit(solution)/shard_map/ppermute | solution.py:50
  21.9 17.7 %collective-permute-start.9 = (bf16[64,1024]{1,0:T(8,128)(2,1)S(1)}, bf16[64,1024]{1,0:T(8,128)(2,1)S(1)}, u32[]{:S(2)}, u32[]{:S(2)}) collective-permute-start(bf16[64,1024]{1,0:T(8,128)(2,1)S(1)} %collective-permute-done.4.refs_4_.refs_1_), channel_id=1, source_target_pairs={{0,16},{2,18},{4,20},{6,22},{8,24},{10,26},{12,28},{14,30},{16,0},... | collective-permute-start | bytes 393224 | tf_op jit(solution)/shard_map/ppermute | solution.py:50
  30.4 11.1 %collective-permute-start.6 = (bf16[256,1024]{1,0:T(8,128)(2,1)S(1)}, bf16[256,1024]{1,0:T(8,128)(2,1)S(1)}, u32[]{:S(2)}, u32[]{:S(2)}) collective-permute-start(bf16[256,1024]{1,0:T(8,128)(2,1)S(1)} %column.1.refs_0_), channel_id=1, source_target_pairs={{0,2},{2,0},{4,6},{6,4},{8,10},{10,8},{12,14},{14,12},{16,18},{18,... | collective-permute-start | bytes 1572872 | tf_op jit(solution)/shard_map/ppermute | solution.py:50
  31.0 10.8 %collective-permute-start.7 = (bf16[256,1024]{1,0:T(8,128)(2,1)S(1)}, bf16[256,1024]{1,0:T(8,128)(2,1)S(1)}, u32[]{:S(2)}, u32[]{:S(2)}) collective-permute-start(bf16[256,1024]{1,0:T(8,128)(2,1)S(1)} %column.1.refs_0_), channel_id=1, source_target_pairs={{0,4},{2,6},{4,0},{6,2},{8,12},{10,14},{12,8},{14,10},{16,20},{18,... | collective-permute-start | bytes 1572872 | tf_op jit(solution)/shard_map/ppermute | solution.py:50
  32.2 10.0 %collective-permute-start.5 = (bf16[2,320,384]{2,1,0:T(8,128)(2,1)S(1)}, bf16[2,320,384]{2,1,0:T(8,128)(2,1)S(1)}, u32[]{:S(2)}, u32[]{:S(2)}) collective-permute-start(bf16[2,320,384]{2,1,0:T(8,128)(2,1)S(1)} %get-tuple-element.41), channel_id=1, source_target_pairs={{0,1},{1,0},{2,3},{3,2},{4,5},{5,4},{6,7},{7,6},{8,9},{9,8},{10,11... | collective-permute-start | bytes 1474568 | tf_op jit(solution)/shard_map/ppermute | solution.py:88
  45.3 4.6 %collective-permute-start.15 = (bf16[2,704,384]{2,1,0:T(8,128)(2,1)S(1)}, bf16[2,704,384]{2,1,0:T(8,128)(2,1)S(1)}, u32[]{:S(2)}, u32[]{:S(2)}) collective-permute-start(bf16[2,704,384]{2,1,0:T(8,128)(2,1)S(1)} %get-tuple-element.51), channel_id=1, source_target_pairs={{0,1},{1,0},{2,3},{3,2},{4,5},{5,4},{6,7},{7,6},{8,9},{9,8},{10,11... | collective-permute-start | bytes 3244040 | tf_op jit(solution)/shard_map/ppermute | solution.py:88
  45.5 5.8 %collective-permute-start.12 = (bf16[16,1024]{1,0:T(8,128)(2,1)S(1)}, bf16[16,1024]{1,0:T(8,128)(2,1)S(1)}, u32[]{:S(2)}, u32[]{:S(2)}) collective-permute-start(bf16[16,1024]{1,0:T(8,128)(2,1)S(1)} %get-tuple-element.49), channel_id=1, source_target_pairs={{0,24},{2,26},{4,28},{6,30},{8,16},{10,18},{12,20},{14,22},{16,8},... | collective-permute-start | bytes 98312 | tf_op jit(solution)/shard_map/ppermute | solution.py:50
  47.9 4.8 %collective-permute-start.13 = (bf16[16,1024]{1,0:T(8,128)(2,1)S(1)}, bf16[16,1024]{1,0:T(8,128)(2,1)S(1)}, u32[]{:S(2)}, u32[]{:S(2)}) collective-permute-start(bf16[16,1024]{1,0:T(8,128)(2,1)S(1)} %get-tuple-element.49), channel_id=1, source_target_pairs={{0,16},{2,18},{4,20},{6,22},{8,24},{10,26},{12,28},{14,30},{16,0},... | collective-permute-start | bytes 98312 | tf_op jit(solution)/shard_map/ppermute | solution.py:50
  47.9 4.8 %collective-permute-start.14 = (bf16[16,1024]{1,0:T(8,128)(2,1)S(1)}, bf16[16,1024]{1,0:T(8,128)(2,1)S(1)}, u32[]{:S(2)}, u32[]{:S(2)}) collective-permute-start(bf16[16,1024]{1,0:T(8,128)(2,1)S(1)} %get-tuple-element.49), channel_id=1, source_target_pairs={{0,8},{2,10},{4,12},{6,14},{8,0},{10,2},{12,4},{14,6},{16,24},{18,... | collective-permute-start | bytes 98312 | tf_op jit(solution)/shard_map/ppermute | solution.py:50
  52.8 15.1 %collective-permute-start.16 = (bf16[272,1024]{1,0:T(8,128)(2,1)S(1)}, bf16[272,1024]{1,0:T(8,128)(2,1)S(1)}, u32[]{:S(2)}, u32[]{:S(2)}) collective-permute-start(bf16[272,1024]{1,0:T(8,128)(2,1)S(1)} %get-tuple-element.55), channel_id=1, source_target_pairs={{0,2},{2,0},{4,6},{6,4},{8,10},{10,8},{12,14},{14,12},{16,18},{18,... | collective-permute-start | bytes 1671176 | tf_op jit(solution)/shard_map/ppermute | solution.py:50
  54.3 14.2 %collective-permute-start.17 = (bf16[272,1024]{1,0:T(8,128)(2,1)S(1)}, bf16[272,1024]{1,0:T(8,128)(2,1)S(1)}, u32[]{:S(2)}, u32[]{:S(2)}) collective-permute-start(bf16[272,1024]{1,0:T(8,128)(2,1)S(1)} %get-tuple-element.56), channel_id=1, source_target_pairs={{0,4},{2,6},{4,0},{6,2},{8,12},{10,14},{12,8},{14,10},{16,20},{18,... | collective-permute-start | bytes 1671176 | tf_op jit(solution)/shard_map/ppermute | solution.py:50
  54.8 12.5 %collective-permute-start.18 = (bf16[16,1024]{1,0:T(8,128)(2,1)S(1)}, bf16[16,1024]{1,0:T(8,128)(2,1)S(1)}, u32[]{:S(2)}, u32[]{:S(2)}) collective-permute-start(bf16[16,1024]{1,0:T(8,128)(2,1)S(1)} %get-tuple-element.57), channel_id=1, source_target_pairs={{0,6},{2,4},{4,2},{6,0},{8,14},{10,12},{12,10},{14,8},{16,22},{18,... | collective-permute-start | bytes 98312 | tf_op jit(solution)/shard_map/ppermute | solution.py:50
  56.3 21.4 %collective-permute-start.20 = (bf16[64,1024]{1,0:T(8,128)(2,1)S(1)}, bf16[64,1024]{1,0:T(8,128)(2,1)S(1)}, u32[]{:S(2)}, u32[]{:S(2)}) collective-permute-start(bf16[64,1024]{1,0:T(8,128)(2,1)S(1)} %get-tuple-element.66), channel_id=1, source_target_pairs={{0,24},{2,26},{4,28},{6,30},{8,16},{10,18},{12,20},{14,22},{16,8},... | collective-permute-start | bytes 393224 | tf_op jit(solution)/shard_map/ppermute | solution.py:50
  58.4 20.6 %collective-permute-start.21 = (bf16[64,1024]{1,0:T(8,128)(2,1)S(1)}, bf16[64,1024]{1,0:T(8,128)(2,1)S(1)}, u32[]{:S(2)}, u32[]{:S(2)}) collective-permute-start(bf16[64,1024]{1,0:T(8,128)(2,1)S(1)} %get-tuple-element.67), channel_id=1, source_target_pairs={{0,16},{2,18},{4,20},{6,22},{8,24},{10,26},{12,28},{14,30},{16,0},... | collective-permute-start | bytes 393224 | tf_op jit(solution)/shard_map/ppermute | solution.py:50
  67.3 11.7 %collective-permute-start.22 = (bf16[64,1024]{1,0:T(8,128)(2,1)S(1)}, bf16[64,1024]{1,0:T(8,128)(2,1)S(1)}, u32[]{:S(2)}, u32[]{:S(2)}) collective-permute-start(bf16[64,1024]{1,0:T(8,128)(2,1)S(1)} %get-tuple-element.68), channel_id=1, source_target_pairs={{0,8},{2,10},{4,12},{6,14},{8,0},{10,2},{12,4},{14,6},{16,24},{18,... | collective-permute-start | bytes 393224 | tf_op jit(solution)/shard_map/ppermute | solution.py:50
  68.7 22.7 %collective-permute-start.24 = (bf16[64,1024]{1,0:T(8,128)(2,1)S(1)}, bf16[64,1024]{1,0:T(8,128)(2,1)S(1)}, u32[]{:S(2)}, u32[]{:S(2)}) collective-permute-start(bf16[64,1024]{1,0:T(8,128)(2,1)S(1)} %get-tuple-element.69), channel_id=1, source_target_pairs={{0,24},{2,26},{4,28},{6,30},{8,16},{10,18},{12,20},{14,22},{16,8},... | collective-permute-start | bytes 393224 | tf_op jit(solution)/shard_map/ppermute | solution.py:50
  71.7 19.8 %collective-permute-start.25 = (bf16[64,1024]{1,0:T(8,128)(2,1)S(1)}, bf16[64,1024]{1,0:T(8,128)(2,1)S(1)}, u32[]{:S(2)}, u32[]{:S(2)}) collective-permute-start(bf16[64,1024]{1,0:T(8,128)(2,1)S(1)} %get-tuple-element.70), channel_id=1, source_target_pairs={{0,16},{2,18},{4,20},{6,22},{8,24},{10,26},{12,28},{14,30},{16,0},... | collective-permute-start | bytes 393224 | tf_op jit(solution)/shard_map/ppermute | solution.py:50
  77.8 13.7 %collective-permute-start.26 = (bf16[64,1024]{1,0:T(8,128)(2,1)S(1)}, bf16[64,1024]{1,0:T(8,128)(2,1)S(1)}, u32[]{:S(2)}, u32[]{:S(2)}) collective-permute-start(bf16[64,1024]{1,0:T(8,128)(2,1)S(1)} %get-tuple-element.71), channel_id=1, source_target_pairs={{0,8},{2,10},{4,12},{6,14},{8,0},{10,2},{12,4},{14,6},{16,24},{18,... | collective-permute-start | bytes 393224 | tf_op jit(solution)/shard_map/ppermute | solution.py:50
  79.0 12.4 %collective-permute-start.23 = (bf16[64,1024]{1,0:T(8,128)(2,1)S(1)}, bf16[64,1024]{1,0:T(8,128)(2,1)S(1)}, u32[]{:S(2)}, u32[]{:S(2)}) collective-permute-start(bf16[64,1024]{1,0:T(8,128)(2,1)S(1)} %corner_sum.1), channel_id=1, source_target_pairs={{0,6},{2,4},{4,2},{6,0},{8,14},{10,12},{12,10},{14,8},{16,22},{18,... | collective-permute-start | bytes 393224 | tf_op jit(solution)/shard_map/ppermute | solution.py:50
  (14 other events, 248.9 us)

commit v6 on v5

--- a/solution.py
+++ b/solution.py
@@ -471,7 +471,7 @@
         last_down, last_outs, 100000000, "last_down",
         last_own, other_core(last_sent), w_down, residual, slot_request[None, :],
     )
-    far_own, far_sent = gate_up(far + far_corner, w_gate, w_up, "far_gate_up", gates=(near[0], last_kept))
+    far_own, far_sent = gate_up(far + far_corner, w_gate, w_up, "far_gate_up", gates=(near[0], last_sent))
     last_lines = [send(last_sent, count, steps) for steps in outer]
     last_outs = [(0, last_shape, jnp.float32), (0, last_shape, jnp.bfloat16)]
     far_outs = [(column.shape, jnp.bfloat16) for _ in far] + [(corner.shape, jnp.bfloat16) for _ in far_corners]
@@ -499,7 +499,7 @@
 
     returned = [send(part, count, back(steps)) for part, steps in zip(packed, inner + middle)]
     last_corners = [send(last_sent, count, steps) for steps in diagonal]
-    far_parts = lax.optimization_barrier((parts[len(far) :], last_kept))[0]
+    far_parts = parts[len(far) :]
     returned_corners = [send(part, count, back(steps)) for part, steps in zip(far_parts, outer)]
 
     def join_columns(*refs):
@@ -573,13 +573,15 @@
         tiles = everyone[...]
         top = jnp.max(tiles, axis=0, keepdims=True)
         scaled = jnp.exp(jnp.minimum(tiles - top, 0.0))[:, :64] * tiles[:, 64:]
-        shift = top[:, :64] + jnp.log(jnp.sum(scaled, axis=0, keepdims=True))
+        spread = jnp.log(jnp.sum(scaled, axis=0, keepdims=True))
         row = lax.broadcasted_iota(jnp.int32, (count, 64), 0)
         lane = lax.broadcasted_iota(jnp.int32, (count, 64), 1)
-        log_out[...] = logits[...] - jnp.sum(jnp.where(lane == row, shift, 0.0), axis=1, keepdims=True)
+        largest = jnp.sum(jnp.where(lane == row, top[:, :64], 0.0), axis=1, keepdims=True)
+        spread = jnp.sum(jnp.where(lane == row, spread, 0.0), axis=1, keepdims=True)
+        log_out[...] = (logits[...] - largest) - spread
 
     outs = [(shape, jnp.bfloat16), ((count, vocab), jnp.float32)]
-    return kernel_call(finish, outs, WEIGHT, "finish", logits, everyone[:, 0], *final, pinned=False)
+    return kernel_call(finish, outs, 1000000, "finish", logits, everyone[:, 0], *final, pinned=False)
 
 
 def solution(mesh):

time: 92.6 us -> 92.6 us (level)
  no operation moved by 1% of the time
where the time goes in v6:
time: 92.6 us; the launch traced here: 92.4 us
  starting transfers between devices  37.7 us (41%)
  waiting for transfers between devices  23.9 us (26%)
  Pallas kernels  19.2 us (21%)
  blocking collectives  10.8 us (12%)
    ppermute x22, starting transfers between devices, send(): return lax.ppermute(rows, 'req', pairs)  36.7 us
    ppermute x22, waiting for transfers between devices, send(): return lax.ppermute(rows, 'req', pairs)  22.2 us
    pallas_call x14, Pallas kernels, kernel_call(): pl.pallas_call(run, out_shape=tuple(((pltpu.VMEM if pinned else jax.Shape...  12.1 us
    all_to_all x1, blocking collectives, on_device(): everyone = lax.all_to_all(stats, ('req', 'head'), 0, 0, tiled=True)  10.8 us
    pallas_call x1, Pallas kernels, attention_rows(): pl.pallas_call(attention_kernel, out_shape=(pltpu.VMEM((rows, width), jnp...  7.03 us
  transfers between devices with their start and end apart: 27, of which 12 were waited for; matrix products, arithmetic and copies ran while one was open for 0% of the time, Pallas kernels for 10%

profile of v6, /device:TPU:0, one launch (start us, length us, event | category | flops | bytes accessed | tf_op | source)
XLA Modules:
  0.0 92.4 jit_solution(3858415308427316798)
XLA Ops:
  0.6 7.0 %attention_rows.1 = (f32[64,2048]{1,0:T(8,128)S(1)}, bf16[64,2048]{1,0:T(8,128)(2,1)S(1)}) custom-call(s32[16]{0:T(128)} %lengths_any.1, s32[16]{0:T(128)} %requests_any.1, bf16[64,2048]{1,0:T(8,128)(2,1)} %hidden_any.1, f32[1,2048]{1,0:T(1,128)} %bitcast.16, f32[1,128]{1,0:T(1,128)} %bitcast.17, f32[1,128]{1,0:T(1,128)} %bitcast.18, ...), custom_call_target="tpu_custom_call" | custom-call | flops 1400000000 | bytes 17500000 | tf_op jit(solution)/shard_map/attention_rows/pallas_call | solution.py:266
  8.2 1.2 %collective-permute-done.refs_1_ = bf16[64,2048]{1,0:T(8,128)(2,1)S(1)} collective-permute-done((bf16[64,2048]{1,0:T(8,128)(2,1)S(1)}, bf16[64,2048]{1,0:T(8,128)(2,1)S(1)}, u32[]{:S(2)}, u32[]{:S(2)}) %collective-permute-start) | collective-permute-done | bytes 262176 | tf_op jit(solution)/shard_map/ppermute | solution.py:88
  9.8 3.9 %collective-permute-start.4 = (bf16[64,1024]{1,0:T(8,128)(2,1)S(1)}, bf16[64,1024]{1,0:T(8,128)(2,1)S(1)}, u32[]{:S(2)}, u32[]{:S(2)}) collective-permute-start(bf16[64,1024]{1,0:T(8,128)(2,1)S(1)} %get-tuple-element.36.refs_0_), channel_id=1, source_target_pairs={{0,6},{2,4},{4,2},{6,0},{8,14},{10,12},{12,10},{14,8},{16,22},{18,... | collective-permute-start | bytes 393224 | tf_op jit(solution)/shard_map/ppermute | solution.py:50
  13.6 3.6 %collective-permute-start.1 = (bf16[64,1024]{1,0:T(8,128)(2,1)S(1)}, bf16[64,1024]{1,0:T(8,128)(2,1)S(1)}, u32[]{:S(2)}, u32[]{:S(2)}) collective-permute-start(bf16[64,1024]{1,0:T(8,128)(2,1)S(1)} %get-tuple-element.36.refs_0_), channel_id=1, source_target_pairs={{0,24},{2,26},{4,28},{6,30},{8,16},{10,18},{12,20},{14,22},{16,8},... | collective-permute-start | bytes 393224 | tf_op jit(solution)/shard_map/ppermute | solution.py:50
  18.0 1.2 %collective-permute-start.10 = (bf16[64,1024]{1,0:T(8,128)(2,1)S(1)}, bf16[64,1024]{1,0:T(8,128)(2,1)S(1)}, u32[]{:S(2)}, u32[]{:S(2)}) collective-permute-start(bf16[64,1024]{1,0:T(8,128)(2,1)S(1)} %collective-permute-done.4.refs_4_.refs_1_), channel_id=1, source_target_pairs={{0,8},{2,10},{4,12},{6,14},{8,0},{10,2},{12,4},{14,6},{16,24},{18,... | collective-permute-start | bytes 393224 | tf_op jit(solution)/shard_map/ppermute | solution.py:50
  19.3 2.4 %collective-permute-start.8 = (bf16[64,1024]{1,0:T(8,128)(2,1)S(1)}, bf16[64,1024]{1,0:T(8,128)(2,1)S(1)}, u32[]{:S(2)}, u32[]{:S(2)}) collective-permute-start(bf16[64,1024]{1,0:T(8,128)(2,1)S(1)} %collective-permute-done.4.refs_4_.refs_1_), channel_id=1, source_target_pairs={{0,24},{2,26},{4,28},{6,30},{8,16},{10,18},{12,20},{14,22},{16,8},... | collective-permute-start | bytes 393224 | tf_op jit(solution)/shard_map/ppermute | solution.py:50
  21.9 6.4 %collective-permute-start.9 = (bf16[64,1024]{1,0:T(8,128)(2,1)S(1)}, bf16[64,1024]{1,0:T(8,128)(2,1)S(1)}, u32[]{:S(2)}, u32[]{:S(2)}) collective-permute-start(bf16[64,1024]{1,0:T(8,128)(2,1)S(1)} %collective-permute-done.4.refs_4_.refs_1_), channel_id=1, source_target_pairs={{0,16},{2,18},{4,20},{6,22},{8,24},{10,26},{12,28},{14,30},{16,0},... | collective-permute-start | bytes 393224 | tf_op jit(solution)/shard_map/ppermute | solution.py:50
  28.2 2.1 %collective-permute-done.2.refs_2_ = bf16[64,1024]{1,0:T(8,128)(2,1)S(1)} collective-permute-done((bf16[64,1024]{1,0:T(8,128)(2,1)S(1)}, bf16[64,1024]{1,0:T(8,128)(2,1)S(1)}, u32[]{:S(2)}, u32[]{:S(2)}) %collective-permute-start.2) | collective-permute-done | bytes 131104 | tf_op jit(solution)/shard_map/ppermute | solution.py:50
  33.2 6.4 %collective-permute-done.9.refs_1_ = bf16[64,1024]{1,0:T(8,128)(2,1)S(1)} collective-permute-done((bf16[64,1024]{1,0:T(8,128)(2,1)S(1)}, bf16[64,1024]{1,0:T(8,128)(2,1)S(1)}, u32[]{:S(2)}, u32[]{:S(2)}) %collective-permute-start.9) | collective-permute-done | bytes 131104 | tf_op jit(solution)/shard_map/ppermute | solution.py:50
  39.7 1.8 %collective-permute-done.6.refs_2_.refs_0_ = bf16[256,1024]{1,0:T(8,128)(2,1)S(1)} collective-permute-done((bf16[256,1024]{1,0:T(8,128)(2,1)S(1)}, bf16[256,1024]{1,0:T(8,128)(2,1)S(1)}, u32[]{:S(2)}, u32[]{:S(2)}) %collective-permute-start.6) | collective-permute-done | bytes 524320 | tf_op jit(solution)/shard_map/ppermute | solution.py:50
  43.6 1.7 %far_gate_up.1 = (f32[2,704,384]{2,1,0:T(8,128)S(1)}, bf16[2,704,384]{2,1,0:T(8,128)(2,1)S(1)}) custom-call(bf16[256,1024]{1,0:T(8,128)(2,1)S(1)} %collective-permute-done.6.refs_2_.refs_0_, bf16[256,1024]{1,0:T(8,128)(2,1)S(1)} %collective-permute-done.7.refs_3_.refs_1_, bf16[192,1024]{1,0:T(8,128)(2,1)S(1)} %far_corner.1.refs_4_.refs_2_, ...), custom_call_target="tpu_custom_call" | custom-call | flops 1107296256 | bytes 1000000 | tf_op jit(solution)/shard_map/far_gate_up/pallas_call | solution.py:100
  45.5 2.3 %collective-permute-start.12 = (bf16[16,1024]{1,0:T(8,128)(2,1)S(1)}, bf16[16,1024]{1,0:T(8,128)(2,1)S(1)}, u32[]{:S(2)}, u32[]{:S(2)}) collective-permute-start(bf16[16,1024]{1,0:T(8,128)(2,1)S(1)} %get-tuple-element.46.refs_6_), channel_id=1, source_target_pairs={{0,24},{2,26},{4,28},{6,30},{8,16},{10,18},{12,20},{14,22},{16,8},... | collective-permute-start | bytes 98312 | tf_op jit(solution)/shard_map/ppermute | solution.py:50
  47.9 2.1 %collective-permute-start.14 = (bf16[16,1024]{1,0:T(8,128)(2,1)S(1)}, bf16[16,1024]{1,0:T(8,128)(2,1)S(1)}, u32[]{:S(2)}, u32[]{:S(2)}) collective-permute-start(bf16[16,1024]{1,0:T(8,128)(2,1)S(1)} %get-tuple-element.46.refs_6_), channel_id=1, source_target_pairs={{0,8},{2,10},{4,12},{6,14},{8,0},{10,2},{12,4},{14,6},{16,24},{18,... | collective-permute-start | bytes 98312 | tf_op jit(solution)/shard_map/ppermute | solution.py:50
  49.9 1.1 %far_down.1 = (bf16[256,1024]{1,0:T(8,128)(2,1)S(1)}, bf16[256,1024]{1,0:T(8,128)(2,1)S(1)}, bf16[64,1024]{1,0:T(8,128)(2,1)S(1)}, bf16[64,1024]{1,0:T(8,128)(2,1)S(1)}, bf16[64,1024]{1,0:T(8,128)(2,1)S(1)}) custom-call(f32[2,704,384]{2,1,0:T(8,128)S(1)} %get-tuple-element.47.refs_0_, bf16[2,704,384]{2,1,0:T(8,128)(2,1)S(1)} %collective-permute-done.15.refs_1_, ...), custom_call_target="tpu_custom_call" | custom-call | flops 553648128 | bytes 1000000 | tf_op jit(solution)/shard_map/far_down/pallas_call | solution.py:100
  51.3 1.3 %collective-permute-done.13.refs_2_ = bf16[16,1024]{1,0:T(8,128)(2,1)S(1)} collective-permute-done((bf16[16,1024]{1,0:T(8,128)(2,1)S(1)}, bf16[16,1024]{1,0:T(8,128)(2,1)S(1)}, u32[]{:S(2)}, u32[]{:S(2)}) %collective-permute-start.13) | collective-permute-done | bytes 32800 | tf_op jit(solution)/shard_map/ppermute | solution.py:50
  52.8 1.6 %collective-permute-start.16 = (bf16[272,1024]{1,0:T(8,128)(2,1)S(1)}, bf16[272,1024]{1,0:T(8,128)(2,1)S(1)}, u32[]{:S(2)}, u32[]{:S(2)}) collective-permute-start(bf16[272,1024]{1,0:T(8,128)(2,1)S(1)} %get-tuple-element.52), channel_id=1, source_target_pairs={{0,2},{2,0},{4,6},{6,4},{8,10},{10,8},{12,14},{14,12},{16,18},{18,... | collective-permute-start | bytes 1671176 | tf_op jit(solution)/shard_map/ppermute | solution.py:50
  54.8 1.5 %collective-permute-start.18 = (bf16[16,1024]{1,0:T(8,128)(2,1)S(1)}, bf16[16,1024]{1,0:T(8,128)(2,1)S(1)}, u32[]{:S(2)}, u32[]{:S(2)}) collective-permute-start(bf16[16,1024]{1,0:T(8,128)(2,1)S(1)} %get-tuple-element.54), channel_id=1, source_target_pairs={{0,6},{2,4},{4,2},{6,0},{8,14},{10,12},{12,10},{14,8},{16,22},{18,... | collective-permute-start | bytes 98312 | tf_op jit(solution)/shard_map/ppermute | solution.py:50
  56.3 2.1 %collective-permute-start.20 = (bf16[64,1024]{1,0:T(8,128)(2,1)S(1)}, bf16[64,1024]{1,0:T(8,128)(2,1)S(1)}, u32[]{:S(2)}, u32[]{:S(2)}) collective-permute-start(bf16[64,1024]{1,0:T(8,128)(2,1)S(1)} %get-tuple-element.60), channel_id=1, source_target_pairs={{0,24},{2,26},{4,28},{6,30},{8,16},{10,18},{12,20},{14,22},{16,8},... | collective-permute-start | bytes 393224 | tf_op jit(solution)/shard_map/ppermute | solution.py:50
  58.9 8.4 %collective-permute-done.18.refs_4_ = bf16[16,1024]{1,0:T(8,128)(2,1)S(1)} collective-permute-done((bf16[16,1024]{1,0:T(8,128)(2,1)S(1)}, bf16[16,1024]{1,0:T(8,128)(2,1)S(1)}, u32[]{:S(2)}, u32[]{:S(2)}) %collective-permute-start.18) | collective-permute-done | bytes 32800 | tf_op jit(solution)/shard_map/ppermute | solution.py:50
  68.7 2.9 %collective-permute-start.24 = (bf16[64,1024]{1,0:T(8,128)(2,1)S(1)}, bf16[64,1024]{1,0:T(8,128)(2,1)S(1)}, u32[]{:S(2)}, u32[]{:S(2)}) collective-permute-start(bf16[64,1024]{1,0:T(8,128)(2,1)S(1)} %get-tuple-element.63), channel_id=1, source_target_pairs={{0,24},{2,26},{4,28},{6,30},{8,16},{10,18},{12,20},{14,22},{16,8},... | collective-permute-start | bytes 393224 | tf_op jit(solution)/shard_map/ppermute | solution.py:50
  72.3 5.4 %vocab_logits.1 = (f32[16,4748]{1,0:T(8,128)S(1)}, f32[32,1,128]{2,1,0:T(1,128)S(1)}) custom-call(f32[16,1024]{1,0:T(8,128)S(1)} %get-tuple-element.55.refs_0_, f32[16,1024]{1,0:T(8,128)S(1)} %collective-permute-done.19.refs_1_, f32[1,2048]{1,0:T(1,128)S(1)} %bitcast.12, bf16[4748,2048]{1,0:T(8,128)(2,1)S(1)} %bitcast.10), custom_call_target="tpu_custom_call" | custom-call | flops 311164928 | bytes 1000000 | tf_op jit(solution)/shard_map/vocab_logits/pallas_call | solution.py:100
  77.8 1.2 %collective-permute-start.26 = (bf16[64,1024]{1,0:T(8,128)(2,1)S(1)}, bf16[64,1024]{1,0:T(8,128)(2,1)S(1)}, u32[]{:S(2)}, u32[]{:S(2)}) collective-permute-start(bf16[64,1024]{1,0:T(8,128)(2,1)S(1)} %get-tuple-element.65), channel_id=1, source_target_pairs={{0,8},{2,10},{4,12},{6,14},{8,0},{10,2},{12,4},{14,6},{16,24},{18,... | collective-permute-start | bytes 393224 | tf_op jit(solution)/shard_map/ppermute | solution.py:50
  79.1 1.6 %collective-permute-start.23 = (bf16[64,1024]{1,0:T(8,128)(2,1)S(1)}, bf16[64,1024]{1,0:T(8,128)(2,1)S(1)}, u32[]{:S(2)}, u32[]{:S(2)}) collective-permute-start(bf16[64,1024]{1,0:T(8,128)(2,1)S(1)} %corner_sum.1), channel_id=1, source_target_pairs={{0,6},{2,4},{4,2},{6,0},{8,14},{10,12},{12,10},{14,8},{16,22},{18,... | collective-permute-start | bytes 393224 | tf_op jit(solution)/shard_map/ppermute | solution.py:50
  80.7 10.8 %all_to_all.5 = f32[32,1,128]{2,1,0:T(1,128)S(1)} all-to-all(f32[32,1,128]{2,1,0:T(1,128)S(1)} %get-tuple-element.57.refs_4_), channel_id=1, replica_groups=mesh['req'=16,'head'=2] {'req','head'}, dimensions={0} | all-to-all | bytes 32768 | tf_op jit(solution)/shard_map/all_to_all | solution.py:564
  (69 shorter events, 11.5 us)
Async XLA Ops:
  9.8 8.3 %collective-permute-start.4 = (bf16[64,1024]{1,0:T(8,128)(2,1)S(1)}, bf16[64,1024]{1,0:T(8,128)(2,1)S(1)}, u32[]{:S(2)}, u32[]{:S(2)}) collective-permute-start(bf16[64,1024]{1,0:T(8,128)(2,1)S(1)} %get-tuple-element.36.refs_0_), channel_id=1, source_target_pairs={{0,6},{2,4},{4,2},{6,0},{8,14},{10,12},{12,10},{14,8},{16,22},{18,... | collective-permute-start | bytes 393224 | tf_op jit(solution)/shard_map/ppermute | solution.py:50
  13.6 8.2 %collective-permute-start.1 = (bf16[64,1024]{1,0:T(8,128)(2,1)S(1)}, bf16[64,1024]{1,0:T(8,128)(2,1)S(1)}, u32[]{:S(2)}, u32[]{:S(2)}) collective-permute-start(bf16[64,1024]{1,0:T(8,128)(2,1)S(1)} %get-tuple-element.36.refs_0_), channel_id=1, source_target_pairs={{0,24},{2,26},{4,28},{6,30},{8,16},{10,18},{12,20},{14,22},{16,8},... | collective-permute-start | bytes 393224 | tf_op jit(solution)/shard_map/ppermute | solution.py:50
  17.2 13.1 %collective-permute-start.2 = (bf16[64,1024]{1,0:T(8,128)(2,1)S(1)}, bf16[64,1024]{1,0:T(8,128)(2,1)S(1)}, u32[]{:S(2)}, u32[]{:S(2)}) collective-permute-start(bf16[64,1024]{1,0:T(8,128)(2,1)S(1)} %get-tuple-element.36.refs_0_), channel_id=1, source_target_pairs={{0,16},{2,18},{4,20},{6,22},{8,24},{10,26},{12,28},{14,30},{16,0},... | collective-permute-start | bytes 393224 | tf_op jit(solution)/shard_map/ppermute | solution.py:50
  17.3 13.1 %collective-permute-start.3 = (bf16[64,1024]{1,0:T(8,128)(2,1)S(1)}, bf16[64,1024]{1,0:T(8,128)(2,1)S(1)}, u32[]{:S(2)}, u32[]{:S(2)}) collective-permute-start(bf16[64,1024]{1,0:T(8,128)(2,1)S(1)} %get-tuple-element.36.refs_0_), channel_id=1, source_target_pairs={{0,8},{2,10},{4,12},{6,14},{8,0},{10,2},{12,4},{14,6},{16,24},{18,... | collective-permute-start | bytes 393224 | tf_op jit(solution)/shard_map/ppermute | solution.py:50
  18.0 14.2 %collective-permute-start.10 = (bf16[64,1024]{1,0:T(8,128)(2,1)S(1)}, bf16[64,1024]{1,0:T(8,128)(2,1)S(1)}, u32[]{:S(2)}, u32[]{:S(2)}) collective-permute-start(bf16[64,1024]{1,0:T(8,128)(2,1)S(1)} %collective-permute-done.4.refs_4_.refs_1_), channel_id=1, source_target_pairs={{0,8},{2,10},{4,12},{6,14},{8,0},{10,2},{12,4},{14,6},{16,24},{18,... | collective-permute-start | bytes 393224 | tf_op jit(solution)/shard_map/ppermute | solution.py:50
  19.3 13.9 %collective-permute-start.8 = (bf16[64,1024]{1,0:T(8,128)(2,1)S(1)}, bf16[64,1024]{1,0:T(8,128)(2,1)S(1)}, u32[]{:S(2)}, u32[]{:S(2)}) collective-permute-start(bf16[64,1024]{1,0:T(8,128)(2,1)S(1)} %collective-permute-done.4.refs_4_.refs_1_), channel_id=1, source_target_pairs={{0,24},{2,26},{4,28},{6,30},{8,16},{10,18},{12,20},{14,22},{16,8},... | collective-permute-start | bytes 393224 | tf_op jit(solution)/shard_map/ppermute | solution.py:50
  21.9 17.7 %collective-permute-start.9 = (bf16[64,1024]{1,0:T(8,128)(2,1)S(1)}, bf16[64,1024]{1,0:T(8,128)(2,1)S(1)}, u32[]{:S(2)}, u32[]{:S(2)}) collective-permute-start(bf16[64,1024]{1,0:T(8,128)(2,1)S(1)} %collective-permute-done.4.refs_4_.refs_1_), channel_id=1, source_target_pairs={{0,16},{2,18},{4,20},{6,22},{8,24},{10,26},{12,28},{14,30},{16,0},... | collective-permute-start | bytes 393224 | tf_op jit(solution)/shard_map/ppermute | solution.py:50
  30.4 11.1 %collective-permute-start.6 = (bf16[256,1024]{1,0:T(8,128)(2,1)S(1)}, bf16[256,1024]{1,0:T(8,128)(2,1)S(1)}, u32[]{:S(2)}, u32[]{:S(2)}) collective-permute-start(bf16[256,1024]{1,0:T(8,128)(2,1)S(1)} %column.1.refs_0_), channel_id=1, source_target_pairs={{0,2},{2,0},{4,6},{6,4},{8,10},{10,8},{12,14},{14,12},{16,18},{18,... | collective-permute-start | bytes 1572872 | tf_op jit(solution)/shard_map/ppermute | solution.py:50
  31.0 10.8 %collective-permute-start.7 = (bf16[256,1024]{1,0:T(8,128)(2,1)S(1)}, bf16[256,1024]{1,0:T(8,128)(2,1)S(1)}, u32[]{:S(2)}, u32[]{:S(2)}) collective-permute-start(bf16[256,1024]{1,0:T(8,128)(2,1)S(1)} %column.1.refs_0_), channel_id=1, source_target_pairs={{0,4},{2,6},{4,0},{6,2},{8,12},{10,14},{12,8},{14,10},{16,20},{18,... | collective-permute-start | bytes 1572872 | tf_op jit(solution)/shard_map/ppermute | solution.py:50
  32.2 10.0 %collective-permute-start.5 = (bf16[2,320,384]{2,1,0:T(8,128)(2,1)S(1)}, bf16[2,320,384]{2,1,0:T(8,128)(2,1)S(1)}, u32[]{:S(2)}, u32[]{:S(2)}) collective-permute-start(bf16[2,320,384]{2,1,0:T(8,128)(2,1)S(1)} %get-tuple-element.38), channel_id=1, source_target_pairs={{0,1},{1,0},{2,3},{3,2},{4,5},{5,4},{6,7},{7,6},{8,9},{9,8},{10,11... | collective-permute-start | bytes 1474568 | tf_op jit(solution)/shard_map/ppermute | solution.py:88
  45.3 4.6 %collective-permute-start.15 = (bf16[2,704,384]{2,1,0:T(8,128)(2,1)S(1)}, bf16[2,704,384]{2,1,0:T(8,128)(2,1)S(1)}, u32[]{:S(2)}, u32[]{:S(2)}) collective-permute-start(bf16[2,704,384]{2,1,0:T(8,128)(2,1)S(1)} %get-tuple-element.48), channel_id=1, source_target_pairs={{0,1},{1,0},{2,3},{3,2},{4,5},{5,4},{6,7},{7,6},{8,9},{9,8},{10,11... | collective-permute-start | bytes 3244040 | tf_op jit(solution)/shard_map/ppermute | solution.py:88
  45.5 5.8 %collective-permute-start.12 = (bf16[16,1024]{1,0:T(8,128)(2,1)S(1)}, bf16[16,1024]{1,0:T(8,128)(2,1)S(1)}, u32[]{:S(2)}, u32[]{:S(2)}) collective-permute-start(bf16[16,1024]{1,0:T(8,128)(2,1)S(1)} %get-tuple-element.46.refs_6_), channel_id=1, source_target_pairs={{0,24},{2,26},{4,28},{6,30},{8,16},{10,18},{12,20},{14,22},{16,8},... | collective-permute-start | bytes 98312 | tf_op jit(solution)/shard_map/ppermute | solution.py:50
  47.9 4.8 %collective-permute-start.13 = (bf16[16,1024]{1,0:T(8,128)(2,1)S(1)}, bf16[16,1024]{1,0:T(8,128)(2,1)S(1)}, u32[]{:S(2)}, u32[]{:S(2)}) collective-permute-start(bf16[16,1024]{1,0:T(8,128)(2,1)S(1)} %get-tuple-element.46.refs_6_), channel_id=1, source_target_pairs={{0,16},{2,18},{4,20},{6,22},{8,24},{10,26},{12,28},{14,30},{16,0},... | collective-permute-start | bytes 98312 | tf_op jit(solution)/shard_map/ppermute | solution.py:50
  47.9 4.8 %collective-permute-start.14 = (bf16[16,1024]{1,0:T(8,128)(2,1)S(1)}, bf16[16,1024]{1,0:T(8,128)(2,1)S(1)}, u32[]{:S(2)}, u32[]{:S(2)}) collective-permute-start(bf16[16,1024]{1,0:T(8,128)(2,1)S(1)} %get-tuple-element.46.refs_6_), channel_id=1, source_target_pairs={{0,8},{2,10},{4,12},{6,14},{8,0},{10,2},{12,4},{14,6},{16,24},{18,... | collective-permute-start | bytes 98312 | tf_op jit(solution)/shard_map/ppermute | solution.py:50
  52.8 15.1 %collective-permute-start.16 = (bf16[272,1024]{1,0:T(8,128)(2,1)S(1)}, bf16[272,1024]{1,0:T(8,128)(2,1)S(1)}, u32[]{:S(2)}, u32[]{:S(2)}) collective-permute-start(bf16[272,1024]{1,0:T(8,128)(2,1)S(1)} %get-tuple-element.52), channel_id=1, source_target_pairs={{0,2},{2,0},{4,6},{6,4},{8,10},{10,8},{12,14},{14,12},{16,18},{18,... | collective-permute-start | bytes 1671176 | tf_op jit(solution)/shard_map/ppermute | solution.py:50
  54.3 14.1 %collective-permute-start.17 = (bf16[272,1024]{1,0:T(8,128)(2,1)S(1)}, bf16[272,1024]{1,0:T(8,128)(2,1)S(1)}, u32[]{:S(2)}, u32[]{:S(2)}) collective-permute-start(bf16[272,1024]{1,0:T(8,128)(2,1)S(1)} %get-tuple-element.53), channel_id=1, source_target_pairs={{0,4},{2,6},{4,0},{6,2},{8,12},{10,14},{12,8},{14,10},{16,20},{18,... | collective-permute-start | bytes 1671176 | tf_op jit(solution)/shard_map/ppermute | solution.py:50
  54.8 12.5 %collective-permute-start.18 = (bf16[16,1024]{1,0:T(8,128)(2,1)S(1)}, bf16[16,1024]{1,0:T(8,128)(2,1)S(1)}, u32[]{:S(2)}, u32[]{:S(2)}) collective-permute-start(bf16[16,1024]{1,0:T(8,128)(2,1)S(1)} %get-tuple-element.54), channel_id=1, source_target_pairs={{0,6},{2,4},{4,2},{6,0},{8,14},{10,12},{12,10},{14,8},{16,22},{18,... | collective-permute-start | bytes 98312 | tf_op jit(solution)/shard_map/ppermute | solution.py:50
  56.3 21.4 %collective-permute-start.20 = (bf16[64,1024]{1,0:T(8,128)(2,1)S(1)}, bf16[64,1024]{1,0:T(8,128)(2,1)S(1)}, u32[]{:S(2)}, u32[]{:S(2)}) collective-permute-start(bf16[64,1024]{1,0:T(8,128)(2,1)S(1)} %get-tuple-element.60), channel_id=1, source_target_pairs={{0,24},{2,26},{4,28},{6,30},{8,16},{10,18},{12,20},{14,22},{16,8},... | collective-permute-start | bytes 393224 | tf_op jit(solution)/shard_map/ppermute | solution.py:50
  58.4 20.6 %collective-permute-start.21 = (bf16[64,1024]{1,0:T(8,128)(2,1)S(1)}, bf16[64,1024]{1,0:T(8,128)(2,1)S(1)}, u32[]{:S(2)}, u32[]{:S(2)}) collective-permute-start(bf16[64,1024]{1,0:T(8,128)(2,1)S(1)} %get-tuple-element.61), channel_id=1, source_target_pairs={{0,16},{2,18},{4,20},{6,22},{8,24},{10,26},{12,28},{14,30},{16,0},... | collective-permute-start | bytes 393224 | tf_op jit(solution)/shard_map/ppermute | solution.py:50
  67.3 11.7 %collective-permute-start.22 = (bf16[64,1024]{1,0:T(8,128)(2,1)S(1)}, bf16[64,1024]{1,0:T(8,128)(2,1)S(1)}, u32[]{:S(2)}, u32[]{:S(2)}) collective-permute-start(bf16[64,1024]{1,0:T(8,128)(2,1)S(1)} %get-tuple-element.62), channel_id=1, source_target_pairs={{0,8},{2,10},{4,12},{6,14},{8,0},{10,2},{12,4},{14,6},{16,24},{18,... | collective-permute-start | bytes 393224 | tf_op jit(solution)/shard_map/ppermute | solution.py:50
  68.7 22.7 %collective-permute-start.24 = (bf16[64,1024]{1,0:T(8,128)(2,1)S(1)}, bf16[64,1024]{1,0:T(8,128)(2,1)S(1)}, u32[]{:S(2)}, u32[]{:S(2)}) collective-permute-start(bf16[64,1024]{1,0:T(8,128)(2,1)S(1)} %get-tuple-element.63), channel_id=1, source_target_pairs={{0,24},{2,26},{4,28},{6,30},{8,16},{10,18},{12,20},{14,22},{16,8},... | collective-permute-start | bytes 393224 | tf_op jit(solution)/shard_map/ppermute | solution.py:50
  71.7 19.8 %collective-permute-start.25 = (bf16[64,1024]{1,0:T(8,128)(2,1)S(1)}, bf16[64,1024]{1,0:T(8,128)(2,1)S(1)}, u32[]{:S(2)}, u32[]{:S(2)}) collective-permute-start(bf16[64,1024]{1,0:T(8,128)(2,1)S(1)} %get-tuple-element.64), channel_id=1, source_target_pairs={{0,16},{2,18},{4,20},{6,22},{8,24},{10,26},{12,28},{14,30},{16,0},... | collective-permute-start | bytes 393224 | tf_op jit(solution)/shard_map/ppermute | solution.py:50
  77.8 13.7 %collective-permute-start.26 = (bf16[64,1024]{1,0:T(8,128)(2,1)S(1)}, bf16[64,1024]{1,0:T(8,128)(2,1)S(1)}, u32[]{:S(2)}, u32[]{:S(2)}) collective-permute-start(bf16[64,1024]{1,0:T(8,128)(2,1)S(1)} %get-tuple-element.65), channel_id=1, source_target_pairs={{0,8},{2,10},{4,12},{6,14},{8,0},{10,2},{12,4},{14,6},{16,24},{18,... | collective-permute-start | bytes 393224 | tf_op jit(solution)/shard_map/ppermute | solution.py:50
  79.1 12.4 %collective-permute-start.23 = (bf16[64,1024]{1,0:T(8,128)(2,1)S(1)}, bf16[64,1024]{1,0:T(8,128)(2,1)S(1)}, u32[]{:S(2)}, u32[]{:S(2)}) collective-permute-start(bf16[64,1024]{1,0:T(8,128)(2,1)S(1)} %corner_sum.1), channel_id=1, source_target_pairs={{0,6},{2,4},{4,2},{6,0},{8,14},{10,12},{12,10},{14,8},{16,22},{18,... | collective-permute-start | bytes 393224 | tf_op jit(solution)/shard_map/ppermute | solution.py:50
  (14 other events, 248.9 us)

commit v7 on v6

--- a/solution.py
+++ b/solution.py
@@ -178,7 +178,8 @@
     lane = lax.broadcasted_iota(jnp.int32, (row_count, HEAD_DIM), 1)
     angles = (row + cache_len).astype(jnp.float32) * frequency[...]
     cosine = jnp.cos(angles)
-    sine = jnp.where(lane < HEAD_DIM // 2, -jnp.sin(angles), jnp.sin(angles))
+    sine = jnp.sin(angles)
+    sine = jnp.where(lane < HEAD_DIM // 2, -sine, sine)
 
     def turned(heads, gain):
         scale = lax.rsqrt(jnp.mean(heads * heads, axis=-1, keepdims=True) + EPS)
@@ -407,7 +408,7 @@
 
     columns = [send(mixed, count, steps) for steps in outer]
     corners = [send(mixed, count, steps) for steps in diagonal]
-    column = stacked([mixed] + columns, "column", gates=corners)
+    column = stacked([mixed] + columns, "column", gates=corners, flops=WEIGHT)
     corner = stacked(corners, "corner") if len(corners) > 1 else corners[0] if corners else None
     far = [send(column, count, steps) for steps in inner + middle]
     far_corners = [send(corner, count, steps) for steps in outer] if corners else []

time: 92.6 us -> 92.6 us (level)
  no operation moved by 1% of the time
where the time goes in v7:
time: 92.6 us; the launch traced here: 92.4 us
  starting transfers between devices  37.7 us (41%)
  waiting for transfers between devices  23.9 us (26%)
  Pallas kernels  19.2 us (21%)
  blocking collectives  10.8 us (12%)
    ppermute x22, starting transfers between devices, send(): return lax.ppermute(rows, 'req', pairs)  36.7 us
    ppermute x22, waiting for transfers between devices, send(): return lax.ppermute(rows, 'req', pairs)  22.2 us
    pallas_call x14, Pallas kernels, kernel_call(): pl.pallas_call(run, out_shape=tuple(((pltpu.VMEM if pinned else jax.Shape...  12.2 us
    all_to_all x1, blocking collectives, on_device(): everyone = lax.all_to_all(stats, ('req', 'head'), 0, 0, tiled=True)  10.8 us
    pallas_call x1, Pallas kernels, attention_rows(): pl.pallas_call(attention_kernel, out_shape=(pltpu.VMEM((rows, width), jnp...  7.03 us
  transfers between devices with their start and end apart: 27, of which 12 were waited for; matrix products, arithmetic and copies ran while one was open for 0% of the time, Pallas kernels for 10%

profile of v7, /device:TPU:0, one launch (start us, length us, event | category | flops | bytes accessed | tf_op | source)
XLA Modules:
  0.0 92.4 jit_solution(7424231909020315347)
XLA Ops:
  0.6 7.0 %attention_rows.1 = (f32[64,2048]{1,0:T(8,128)S(1)}, bf16[64,2048]{1,0:T(8,128)(2,1)S(1)}) custom-call(s32[16]{0:T(128)} %lengths_any.1, s32[16]{0:T(128)} %requests_any.1, bf16[64,2048]{1,0:T(8,128)(2,1)} %hidden_any.1, f32[1,2048]{1,0:T(1,128)} %bitcast.16, f32[1,128]{1,0:T(1,128)} %bitcast.17, f32[1,128]{1,0:T(1,128)} %bitcast.18, ...), custom_call_target="tpu_custom_call" | custom-call | flops 1400000000 | bytes 17500000 | tf_op jit(solution)/shard_map/attention_rows/pallas_call | solution.py:267
  8.2 1.2 %collective-permute-done.refs_1_ = bf16[64,2048]{1,0:T(8,128)(2,1)S(1)} collective-permute-done((bf16[64,2048]{1,0:T(8,128)(2,1)S(1)}, bf16[64,2048]{1,0:T(8,128)(2,1)S(1)}, u32[]{:S(2)}, u32[]{:S(2)}) %collective-permute-start) | collective-permute-done | bytes 262176 | tf_op jit(solution)/shard_map/ppermute | solution.py:88
  9.8 3.9 %collective-permute-start.4 = (bf16[64,1024]{1,0:T(8,128)(2,1)S(1)}, bf16[64,1024]{1,0:T(8,128)(2,1)S(1)}, u32[]{:S(2)}, u32[]{:S(2)}) collective-permute-start(bf16[64,1024]{1,0:T(8,128)(2,1)S(1)} %get-tuple-element.36.refs_0_), channel_id=1, source_target_pairs={{0,6},{2,4},{4,2},{6,0},{8,14},{10,12},{12,10},{14,8},{16,22},{18,... | collective-permute-start | bytes 393224 | tf_op jit(solution)/shard_map/ppermute | solution.py:50
  13.6 3.6 %collective-permute-start.1 = (bf16[64,1024]{1,0:T(8,128)(2,1)S(1)}, bf16[64,1024]{1,0:T(8,128)(2,1)S(1)}, u32[]{:S(2)}, u32[]{:S(2)}) collective-permute-start(bf16[64,1024]{1,0:T(8,128)(2,1)S(1)} %get-tuple-element.36.refs_0_), channel_id=1, source_target_pairs={{0,24},{2,26},{4,28},{6,30},{8,16},{10,18},{12,20},{14,22},{16,8},... | collective-permute-start | bytes 393224 | tf_op jit(solution)/shard_map/ppermute | solution.py:50
  18.0 1.2 %collective-permute-start.10 = (bf16[64,1024]{1,0:T(8,128)(2,1)S(1)}, bf16[64,1024]{1,0:T(8,128)(2,1)S(1)}, u32[]{:S(2)}, u32[]{:S(2)}) collective-permute-start(bf16[64,1024]{1,0:T(8,128)(2,1)S(1)} %collective-permute-done.4.refs_4_.refs_1_), channel_id=1, source_target_pairs={{0,8},{2,10},{4,12},{6,14},{8,0},{10,2},{12,4},{14,6},{16,24},{18,... | collective-permute-start | bytes 393224 | tf_op jit(solution)/shard_map/ppermute | solution.py:50
  19.3 2.4 %collective-permute-start.8 = (bf16[64,1024]{1,0:T(8,128)(2,1)S(1)}, bf16[64,1024]{1,0:T(8,128)(2,1)S(1)}, u32[]{:S(2)}, u32[]{:S(2)}) collective-permute-start(bf16[64,1024]{1,0:T(8,128)(2,1)S(1)} %collective-permute-done.4.refs_4_.refs_1_), channel_id=1, source_target_pairs={{0,24},{2,26},{4,28},{6,30},{8,16},{10,18},{12,20},{14,22},{16,8},... | collective-permute-start | bytes 393224 | tf_op jit(solution)/shard_map/ppermute | solution.py:50
  21.9 6.4 %collective-permute-start.9 = (bf16[64,1024]{1,0:T(8,128)(2,1)S(1)}, bf16[64,1024]{1,0:T(8,128)(2,1)S(1)}, u32[]{:S(2)}, u32[]{:S(2)}) collective-permute-start(bf16[64,1024]{1,0:T(8,128)(2,1)S(1)} %collective-permute-done.4.refs_4_.refs_1_), channel_id=1, source_target_pairs={{0,16},{2,18},{4,20},{6,22},{8,24},{10,26},{12,28},{14,30},{16,0},... | collective-permute-start | bytes 393224 | tf_op jit(solution)/shard_map/ppermute | solution.py:50
  28.2 2.1 %collective-permute-done.2.refs_2_ = bf16[64,1024]{1,0:T(8,128)(2,1)S(1)} collective-permute-done((bf16[64,1024]{1,0:T(8,128)(2,1)S(1)}, bf16[64,1024]{1,0:T(8,128)(2,1)S(1)}, u32[]{:S(2)}, u32[]{:S(2)}) %collective-permute-start.2) | collective-permute-done | bytes 131104 | tf_op jit(solution)/shard_map/ppermute | solution.py:50
  33.2 6.4 %collective-permute-done.9.refs_1_ = bf16[64,1024]{1,0:T(8,128)(2,1)S(1)} collective-permute-done((bf16[64,1024]{1,0:T(8,128)(2,1)S(1)}, bf16[64,1024]{1,0:T(8,128)(2,1)S(1)}, u32[]{:S(2)}, u32[]{:S(2)}) %collective-permute-start.9) | collective-permute-done | bytes 131104 | tf_op jit(solution)/shard_map/ppermute | solution.py:50
  39.7 1.8 %collective-permute-done.6.refs_2_.refs_0_ = bf16[256,1024]{1,0:T(8,128)(2,1)S(1)} collective-permute-done((bf16[256,1024]{1,0:T(8,128)(2,1)S(1)}, bf16[256,1024]{1,0:T(8,128)(2,1)S(1)}, u32[]{:S(2)}, u32[]{:S(2)}) %collective-permute-start.6) | collective-permute-done | bytes 524320 | tf_op jit(solution)/shard_map/ppermute | solution.py:50
  43.6 1.7 %far_gate_up.1 = (f32[2,704,384]{2,1,0:T(8,128)S(1)}, bf16[2,704,384]{2,1,0:T(8,128)(2,1)S(1)}) custom-call(bf16[256,1024]{1,0:T(8,128)(2,1)S(1)} %collective-permute-done.6.refs_2_.refs_0_, bf16[256,1024]{1,0:T(8,128)(2,1)S(1)} %collective-permute-done.7.refs_3_.refs_1_, bf16[192,1024]{1,0:T(8,128)(2,1)S(1)} %far_corner.1.refs_4_.refs_2_, ...), custom_call_target="tpu_custom_call" | custom-call | flops 1107296256 | bytes 1000000 | tf_op jit(solution)/shard_map/far_gate_up/pallas_call | solution.py:100
  45.5 2.3 %collective-permute-start.12 = (bf16[16,1024]{1,0:T(8,128)(2,1)S(1)}, bf16[16,1024]{1,0:T(8,128)(2,1)S(1)}, u32[]{:S(2)}, u32[]{:S(2)}) collective-permute-start(bf16[16,1024]{1,0:T(8,128)(2,1)S(1)} %get-tuple-element.46.refs_6_), channel_id=1, source_target_pairs={{0,24},{2,26},{4,28},{6,30},{8,16},{10,18},{12,20},{14,22},{16,8},... | collective-permute-start | bytes 98312 | tf_op jit(solution)/shard_map/ppermute | solution.py:50
  47.9 2.1 %collective-permute-start.14 = (bf16[16,1024]{1,0:T(8,128)(2,1)S(1)}, bf16[16,1024]{1,0:T(8,128)(2,1)S(1)}, u32[]{:S(2)}, u32[]{:S(2)}) collective-permute-start(bf16[16,1024]{1,0:T(8,128)(2,1)S(1)} %get-tuple-element.46.refs_6_), channel_id=1, source_target_pairs={{0,8},{2,10},{4,12},{6,14},{8,0},{10,2},{12,4},{14,6},{16,24},{18,... | collective-permute-start | bytes 98312 | tf_op jit(solution)/shard_map/ppermute | solution.py:50
  49.9 1.1 %far_down.1 = (bf16[256,1024]{1,0:T(8,128)(2,1)S(1)}, bf16[256,1024]{1,0:T(8,128)(2,1)S(1)}, bf16[64,1024]{1,0:T(8,128)(2,1)S(1)}, bf16[64,1024]{1,0:T(8,128)(2,1)S(1)}, bf16[64,1024]{1,0:T(8,128)(2,1)S(1)}) custom-call(f32[2,704,384]{2,1,0:T(8,128)S(1)} %get-tuple-element.47.refs_0_, bf16[2,704,384]{2,1,0:T(8,128)(2,1)S(1)} %collective-permute-done.15.refs_1_, ...), custom_call_target="tpu_custom_call" | custom-call | flops 553648128 | bytes 1000000 | tf_op jit(solution)/shard_map/far_down/pallas_call | solution.py:100
  51.3 1.3 %collective-permute-done.13.refs_2_ = bf16[16,1024]{1,0:T(8,128)(2,1)S(1)} collective-permute-done((bf16[16,1024]{1,0:T(8,128)(2,1)S(1)}, bf16[16,1024]{1,0:T(8,128)(2,1)S(1)}, u32[]{:S(2)}, u32[]{:S(2)}) %collective-permute-start.13) | collective-permute-done | bytes 32800 | tf_op jit(solution)/shard_map/ppermute | solution.py:50
  52.8 1.6 %collective-permute-start.16 = (bf16[272,1024]{1,0:T(8,128)(2,1)S(1)}, bf16[272,1024]{1,0:T(8,128)(2,1)S(1)}, u32[]{:S(2)}, u32[]{:S(2)}) collective-permute-start(bf16[272,1024]{1,0:T(8,128)(2,1)S(1)} %get-tuple-element.52), channel_id=1, source_target_pairs={{0,2},{2,0},{4,6},{6,4},{8,10},{10,8},{12,14},{14,12},{16,18},{18,... | collective-permute-start | bytes 1671176 | tf_op jit(solution)/shard_map/ppermute | solution.py:50
  54.8 1.5 %collective-permute-start.18 = (bf16[16,1024]{1,0:T(8,128)(2,1)S(1)}, bf16[16,1024]{1,0:T(8,128)(2,1)S(1)}, u32[]{:S(2)}, u32[]{:S(2)}) collective-permute-start(bf16[16,1024]{1,0:T(8,128)(2,1)S(1)} %get-tuple-element.54), channel_id=1, source_target_pairs={{0,6},{2,4},{4,2},{6,0},{8,14},{10,12},{12,10},{14,8},{16,22},{18,... | collective-permute-start | bytes 98312 | tf_op jit(solution)/shard_map/ppermute | solution.py:50
  56.3 2.1 %collective-permute-start.20 = (bf16[64,1024]{1,0:T(8,128)(2,1)S(1)}, bf16[64,1024]{1,0:T(8,128)(2,1)S(1)}, u32[]{:S(2)}, u32[]{:S(2)}) collective-permute-start(bf16[64,1024]{1,0:T(8,128)(2,1)S(1)} %get-tuple-element.60), channel_id=1, source_target_pairs={{0,24},{2,26},{4,28},{6,30},{8,16},{10,18},{12,20},{14,22},{16,8},... | collective-permute-start | bytes 393224 | tf_op jit(solution)/shard_map/ppermute | solution.py:50
  59.0 8.4 %collective-permute-done.18.refs_4_ = bf16[16,1024]{1,0:T(8,128)(2,1)S(1)} collective-permute-done((bf16[16,1024]{1,0:T(8,128)(2,1)S(1)}, bf16[16,1024]{1,0:T(8,128)(2,1)S(1)}, u32[]{:S(2)}, u32[]{:S(2)}) %collective-permute-start.18) | collective-permute-done | bytes 32800 | tf_op jit(solution)/shard_map/ppermute | solution.py:50
  68.7 2.9 %collective-permute-start.24 = (bf16[64,1024]{1,0:T(8,128)(2,1)S(1)}, bf16[64,1024]{1,0:T(8,128)(2,1)S(1)}, u32[]{:S(2)}, u32[]{:S(2)}) collective-permute-start(bf16[64,1024]{1,0:T(8,128)(2,1)S(1)} %get-tuple-element.63), channel_id=1, source_target_pairs={{0,24},{2,26},{4,28},{6,30},{8,16},{10,18},{12,20},{14,22},{16,8},... | collective-permute-start | bytes 393224 | tf_op jit(solution)/shard_map/ppermute | solution.py:50
  72.3 5.4 %vocab_logits.1 = (f32[16,4748]{1,0:T(8,128)S(1)}, f32[32,1,128]{2,1,0:T(1,128)S(1)}) custom-call(f32[16,1024]{1,0:T(8,128)S(1)} %get-tuple-element.55.refs_0_, f32[16,1024]{1,0:T(8,128)S(1)} %collective-permute-done.19.refs_1_, f32[1,2048]{1,0:T(1,128)S(1)} %bitcast.12, bf16[4748,2048]{1,0:T(8,128)(2,1)S(1)} %bitcast.10), custom_call_target="tpu_custom_call" | custom-call | flops 311164928 | bytes 1000000 | tf_op jit(solution)/shard_map/vocab_logits/pallas_call | solution.py:100
  77.8 1.2 %collective-permute-start.26 = (bf16[64,1024]{1,0:T(8,128)(2,1)S(1)}, bf16[64,1024]{1,0:T(8,128)(2,1)S(1)}, u32[]{:S(2)}, u32[]{:S(2)}) collective-permute-start(bf16[64,1024]{1,0:T(8,128)(2,1)S(1)} %get-tuple-element.65), channel_id=1, source_target_pairs={{0,8},{2,10},{4,12},{6,14},{8,0},{10,2},{12,4},{14,6},{16,24},{18,... | collective-permute-start | bytes 393224 | tf_op jit(solution)/shard_map/ppermute | solution.py:50
  79.1 1.6 %collective-permute-start.23 = (bf16[64,1024]{1,0:T(8,128)(2,1)S(1)}, bf16[64,1024]{1,0:T(8,128)(2,1)S(1)}, u32[]{:S(2)}, u32[]{:S(2)}) collective-permute-start(bf16[64,1024]{1,0:T(8,128)(2,1)S(1)} %corner_sum.1), channel_id=1, source_target_pairs={{0,6},{2,4},{4,2},{6,0},{8,14},{10,12},{12,10},{14,8},{16,22},{18,... | collective-permute-start | bytes 393224 | tf_op jit(solution)/shard_map/ppermute | solution.py:50
  80.7 10.8 %all_to_all.5 = f32[32,1,128]{2,1,0:T(1,128)S(1)} all-to-all(f32[32,1,128]{2,1,0:T(1,128)S(1)} %get-tuple-element.57.refs_4_), channel_id=1, replica_groups=mesh['req'=16,'head'=2] {'req','head'}, dimensions={0} | all-to-all | bytes 32768 | tf_op jit(solution)/shard_map/all_to_all | solution.py:565
  (69 shorter events, 11.5 us)
Async XLA Ops:
  9.8 8.3 %collective-permute-start.4 = (bf16[64,1024]{1,0:T(8,128)(2,1)S(1)}, bf16[64,1024]{1,0:T(8,128)(2,1)S(1)}, u32[]{:S(2)}, u32[]{:S(2)}) collective-permute-start(bf16[64,1024]{1,0:T(8,128)(2,1)S(1)} %get-tuple-element.36.refs_0_), channel_id=1, source_target_pairs={{0,6},{2,4},{4,2},{6,0},{8,14},{10,12},{12,10},{14,8},{16,22},{18,... | collective-permute-start | bytes 393224 | tf_op jit(solution)/shard_map/ppermute | solution.py:50
  13.6 8.2 %collective-permute-start.1 = (bf16[64,1024]{1,0:T(8,128)(2,1)S(1)}, bf16[64,1024]{1,0:T(8,128)(2,1)S(1)}, u32[]{:S(2)}, u32[]{:S(2)}) collective-permute-start(bf16[64,1024]{1,0:T(8,128)(2,1)S(1)} %get-tuple-element.36.refs_0_), channel_id=1, source_target_pairs={{0,24},{2,26},{4,28},{6,30},{8,16},{10,18},{12,20},{14,22},{16,8},... | collective-permute-start | bytes 393224 | tf_op jit(solution)/shard_map/ppermute | solution.py:50
  17.2 13.1 %collective-permute-start.2 = (bf16[64,1024]{1,0:T(8,128)(2,1)S(1)}, bf16[64,1024]{1,0:T(8,128)(2,1)S(1)}, u32[]{:S(2)}, u32[]{:S(2)}) collective-permute-start(bf16[64,1024]{1,0:T(8,128)(2,1)S(1)} %get-tuple-element.36.refs_0_), channel_id=1, source_target_pairs={{0,16},{2,18},{4,20},{6,22},{8,24},{10,26},{12,28},{14,30},{16,0},... | collective-permute-start | bytes 393224 | tf_op jit(solution)/shard_map/ppermute | solution.py:50
  17.3 13.1 %collective-permute-start.3 = (bf16[64,1024]{1,0:T(8,128)(2,1)S(1)}, bf16[64,1024]{1,0:T(8,128)(2,1)S(1)}, u32[]{:S(2)}, u32[]{:S(2)}) collective-permute-start(bf16[64,1024]{1,0:T(8,128)(2,1)S(1)} %get-tuple-element.36.refs_0_), channel_id=1, source_target_pairs={{0,8},{2,10},{4,12},{6,14},{8,0},{10,2},{12,4},{14,6},{16,24},{18,... | collective-permute-start | bytes 393224 | tf_op jit(solution)/shard_map/ppermute | solution.py:50
  18.0 14.2 %collective-permute-start.10 = (bf16[64,1024]{1,0:T(8,128)(2,1)S(1)}, bf16[64,1024]{1,0:T(8,128)(2,1)S(1)}, u32[]{:S(2)}, u32[]{:S(2)}) collective-permute-start(bf16[64,1024]{1,0:T(8,128)(2,1)S(1)} %collective-permute-done.4.refs_4_.refs_1_), channel_id=1, source_target_pairs={{0,8},{2,10},{4,12},{6,14},{8,0},{10,2},{12,4},{14,6},{16,24},{18,... | collective-permute-start | bytes 393224 | tf_op jit(solution)/shard_map/ppermute | solution.py:50
  19.3 13.9 %collective-permute-start.8 = (bf16[64,1024]{1,0:T(8,128)(2,1)S(1)}, bf16[64,1024]{1,0:T(8,128)(2,1)S(1)}, u32[]{:S(2)}, u32[]{:S(2)}) collective-permute-start(bf16[64,1024]{1,0:T(8,128)(2,1)S(1)} %collective-permute-done.4.refs_4_.refs_1_), channel_id=1, source_target_pairs={{0,24},{2,26},{4,28},{6,30},{8,16},{10,18},{12,20},{14,22},{16,8},... | collective-permute-start | bytes 393224 | tf_op jit(solution)/shard_map/ppermute | solution.py:50
  21.9 17.7 %collective-permute-start.9 = (bf16[64,1024]{1,0:T(8,128)(2,1)S(1)}, bf16[64,1024]{1,0:T(8,128)(2,1)S(1)}, u32[]{:S(2)}, u32[]{:S(2)}) collective-permute-start(bf16[64,1024]{1,0:T(8,128)(2,1)S(1)} %collective-permute-done.4.refs_4_.refs_1_), channel_id=1, source_target_pairs={{0,16},{2,18},{4,20},{6,22},{8,24},{10,26},{12,28},{14,30},{16,0},... | collective-permute-start | bytes 393224 | tf_op jit(solution)/shard_map/ppermute | solution.py:50
  30.4 11.1 %collective-permute-start.6 = (bf16[256,1024]{1,0:T(8,128)(2,1)S(1)}, bf16[256,1024]{1,0:T(8,128)(2,1)S(1)}, u32[]{:S(2)}, u32[]{:S(2)}) collective-permute-start(bf16[256,1024]{1,0:T(8,128)(2,1)S(1)} %column.1.refs_0_), channel_id=1, source_target_pairs={{0,2},{2,0},{4,6},{6,4},{8,10},{10,8},{12,14},{14,12},{16,18},{18,... | collective-permute-start | bytes 1572872 | tf_op jit(solution)/shard_map/ppermute | solution.py:50
  31.0 10.8 %collective-permute-start.7 = (bf16[256,1024]{1,0:T(8,128)(2,1)S(1)}, bf16[256,1024]{1,0:T(8,128)(2,1)S(1)}, u32[]{:S(2)}, u32[]{:S(2)}) collective-permute-start(bf16[256,1024]{1,0:T(8,128)(2,1)S(1)} %column.1.refs_0_), channel_id=1, source_target_pairs={{0,4},{2,6},{4,0},{6,2},{8,12},{10,14},{12,8},{14,10},{16,20},{18,... | collective-permute-start | bytes 1572872 | tf_op jit(solution)/shard_map/ppermute | solution.py:50
  32.2 10.0 %collective-permute-start.5 = (bf16[2,320,384]{2,1,0:T(8,128)(2,1)S(1)}, bf16[2,320,384]{2,1,0:T(8,128)(2,1)S(1)}, u32[]{:S(2)}, u32[]{:S(2)}) collective-permute-start(bf16[2,320,384]{2,1,0:T(8,128)(2,1)S(1)} %get-tuple-element.38), channel_id=1, source_target_pairs={{0,1},{1,0},{2,3},{3,2},{4,5},{5,4},{6,7},{7,6},{8,9},{9,8},{10,11... | collective-permute-start | bytes 1474568 | tf_op jit(solution)/shard_map/ppermute | solution.py:88
  45.3 4.6 %collective-permute-start.15 = (bf16[2,704,384]{2,1,0:T(8,128)(2,1)S(1)}, bf16[2,704,384]{2,1,0:T(8,128)(2,1)S(1)}, u32[]{:S(2)}, u32[]{:S(2)}) collective-permute-start(bf16[2,704,384]{2,1,0:T(8,128)(2,1)S(1)} %get-tuple-element.48), channel_id=1, source_target_pairs={{0,1},{1,0},{2,3},{3,2},{4,5},{5,4},{6,7},{7,6},{8,9},{9,8},{10,11... | collective-permute-start | bytes 3244040 | tf_op jit(solution)/shard_map/ppermute | solution.py:88
  45.5 5.8 %collective-permute-start.12 = (bf16[16,1024]{1,0:T(8,128)(2,1)S(1)}, bf16[16,1024]{1,0:T(8,128)(2,1)S(1)}, u32[]{:S(2)}, u32[]{:S(2)}) collective-permute-start(bf16[16,1024]{1,0:T(8,128)(2,1)S(1)} %get-tuple-element.46.refs_6_), channel_id=1, source_target_pairs={{0,24},{2,26},{4,28},{6,30},{8,16},{10,18},{12,20},{14,22},{16,8},... | collective-permute-start | bytes 98312 | tf_op jit(solution)/shard_map/ppermute | solution.py:50
  47.9 4.8 %collective-permute-start.13 = (bf16[16,1024]{1,0:T(8,128)(2,1)S(1)}, bf16[16,1024]{1,0:T(8,128)(2,1)S(1)}, u32[]{:S(2)}, u32[]{:S(2)}) collective-permute-start(bf16[16,1024]{1,0:T(8,128)(2,1)S(1)} %get-tuple-element.46.refs_6_), channel_id=1, source_target_pairs={{0,16},{2,18},{4,20},{6,22},{8,24},{10,26},{12,28},{14,30},{16,0},... | collective-permute-start | bytes 98312 | tf_op jit(solution)/shard_map/ppermute | solution.py:50
  47.9 4.8 %collective-permute-start.14 = (bf16[16,1024]{1,0:T(8,128)(2,1)S(1)}, bf16[16,1024]{1,0:T(8,128)(2,1)S(1)}, u32[]{:S(2)}, u32[]{:S(2)}) collective-permute-start(bf16[16,1024]{1,0:T(8,128)(2,1)S(1)} %get-tuple-element.46.refs_6_), channel_id=1, source_target_pairs={{0,8},{2,10},{4,12},{6,14},{8,0},{10,2},{12,4},{14,6},{16,24},{18,... | collective-permute-start | bytes 98312 | tf_op jit(solution)/shard_map/ppermute | solution.py:50
  52.8 15.1 %collective-permute-start.16 = (bf16[272,1024]{1,0:T(8,128)(2,1)S(1)}, bf16[272,1024]{1,0:T(8,128)(2,1)S(1)}, u32[]{:S(2)}, u32[]{:S(2)}) collective-permute-start(bf16[272,1024]{1,0:T(8,128)(2,1)S(1)} %get-tuple-element.52), channel_id=1, source_target_pairs={{0,2},{2,0},{4,6},{6,4},{8,10},{10,8},{12,14},{14,12},{16,18},{18,... | collective-permute-start | bytes 1671176 | tf_op jit(solution)/shard_map/ppermute | solution.py:50
  54.3 14.2 %collective-permute-start.17 = (bf16[272,1024]{1,0:T(8,128)(2,1)S(1)}, bf16[272,1024]{1,0:T(8,128)(2,1)S(1)}, u32[]{:S(2)}, u32[]{:S(2)}) collective-permute-start(bf16[272,1024]{1,0:T(8,128)(2,1)S(1)} %get-tuple-element.53), channel_id=1, source_target_pairs={{0,4},{2,6},{4,0},{6,2},{8,12},{10,14},{12,8},{14,10},{16,20},{18,... | collective-permute-start | bytes 1671176 | tf_op jit(solution)/shard_map/ppermute | solution.py:50
  54.8 12.5 %collective-permute-start.18 = (bf16[16,1024]{1,0:T(8,128)(2,1)S(1)}, bf16[16,1024]{1,0:T(8,128)(2,1)S(1)}, u32[]{:S(2)}, u32[]{:S(2)}) collective-permute-start(bf16[16,1024]{1,0:T(8,128)(2,1)S(1)} %get-tuple-element.54), channel_id=1, source_target_pairs={{0,6},{2,4},{4,2},{6,0},{8,14},{10,12},{12,10},{14,8},{16,22},{18,... | collective-permute-start | bytes 98312 | tf_op jit(solution)/shard_map/ppermute | solution.py:50
  56.3 21.4 %collective-permute-start.20 = (bf16[64,1024]{1,0:T(8,128)(2,1)S(1)}, bf16[64,1024]{1,0:T(8,128)(2,1)S(1)}, u32[]{:S(2)}, u32[]{:S(2)}) collective-permute-start(bf16[64,1024]{1,0:T(8,128)(2,1)S(1)} %get-tuple-element.60), channel_id=1, source_target_pairs={{0,24},{2,26},{4,28},{6,30},{8,16},{10,18},{12,20},{14,22},{16,8},... | collective-permute-start | bytes 393224 | tf_op jit(solution)/shard_map/ppermute | solution.py:50
  58.4 20.6 %collective-permute-start.21 = (bf16[64,1024]{1,0:T(8,128)(2,1)S(1)}, bf16[64,1024]{1,0:T(8,128)(2,1)S(1)}, u32[]{:S(2)}, u32[]{:S(2)}) collective-permute-start(bf16[64,1024]{1,0:T(8,128)(2,1)S(1)} %get-tuple-element.61), channel_id=1, source_target_pairs={{0,16},{2,18},{4,20},{6,22},{8,24},{10,26},{12,28},{14,30},{16,0},... | collective-permute-start | bytes 393224 | tf_op jit(solution)/shard_map/ppermute | solution.py:50
  67.3 11.7 %collective-permute-start.22 = (bf16[64,1024]{1,0:T(8,128)(2,1)S(1)}, bf16[64,1024]{1,0:T(8,128)(2,1)S(1)}, u32[]{:S(2)}, u32[]{:S(2)}) collective-permute-start(bf16[64,1024]{1,0:T(8,128)(2,1)S(1)} %get-tuple-element.62), channel_id=1, source_target_pairs={{0,8},{2,10},{4,12},{6,14},{8,0},{10,2},{12,4},{14,6},{16,24},{18,... | collective-permute-start | bytes 393224 | tf_op jit(solution)/shard_map/ppermute | solution.py:50
  68.7 22.7 %collective-permute-start.24 = (bf16[64,1024]{1,0:T(8,128)(2,1)S(1)}, bf16[64,1024]{1,0:T(8,128)(2,1)S(1)}, u32[]{:S(2)}, u32[]{:S(2)}) collective-permute-start(bf16[64,1024]{1,0:T(8,128)(2,1)S(1)} %get-tuple-element.63), channel_id=1, source_target_pairs={{0,24},{2,26},{4,28},{6,30},{8,16},{10,18},{12,20},{14,22},{16,8},... | collective-permute-start | bytes 393224 | tf_op jit(solution)/shard_map/ppermute | solution.py:50
  71.7 19.8 %collective-permute-start.25 = (bf16[64,1024]{1,0:T(8,128)(2,1)S(1)}, bf16[64,1024]{1,0:T(8,128)(2,1)S(1)}, u32[]{:S(2)}, u32[]{:S(2)}) collective-permute-start(bf16[64,1024]{1,0:T(8,128)(2,1)S(1)} %get-tuple-element.64), channel_id=1, source_target_pairs={{0,16},{2,18},{4,20},{6,22},{8,24},{10,26},{12,28},{14,30},{16,0},... | collective-permute-start | bytes 393224 | tf_op jit(solution)/shard_map/ppermute | solution.py:50
  77.8 13.7 %collective-permute-start.26 = (bf16[64,1024]{1,0:T(8,128)(2,1)S(1)}, bf16[64,1024]{1,0:T(8,128)(2,1)S(1)}, u32[]{:S(2)}, u32[]{:S(2)}) collective-permute-start(bf16[64,1024]{1,0:T(8,128)(2,1)S(1)} %get-tuple-element.65), channel_id=1, source_target_pairs={{0,8},{2,10},{4,12},{6,14},{8,0},{10,2},{12,4},{14,6},{16,24},{18,... | collective-permute-start | bytes 393224 | tf_op jit(solution)/shard_map/ppermute | solution.py:50
  79.1 12.4 %collective-permute-start.23 = (bf16[64,1024]{1,0:T(8,128)(2,1)S(1)}, bf16[64,1024]{1,0:T(8,128)(2,1)S(1)}, u32[]{:S(2)}, u32[]{:S(2)}) collective-permute-start(bf16[64,1024]{1,0:T(8,128)(2,1)S(1)} %corner_sum.1), channel_id=1, source_target_pairs={{0,6},{2,4},{4,2},{6,0},{8,14},{10,12},{12,10},{14,8},{16,22},{18,... | collective-permute-start | bytes 393224 | tf_op jit(solution)/shard_map/ppermute | solution.py:50
  (14 other events, 244.9 us)
